TPU v7x, 32 devices: a whole 2x2x4 slice. The times are simulated.
32 devices in a mesh: orb: 4 (over y, x), aux: 8 (over z, core).
Axes of the slice: x: 2, y: 2, z: 4, core: 2. Of those that a mesh axis runs over, the one named last changes fastest.
Arguments:
- b_rows: bfloat16 [2048, 32, 2, 128], P('aux', 'orb'), may hold values from -6 to 6
- col_blocks: int32 [4, 2], P('orb'), may hold values from 0 to 3, all different within a row
- g_occ: bfloat16 [2, 32, 32], P(None, 'orb'), may hold values from -1 to 1
- occ_live: int32 [2, 4, 4], replicated, may hold values 0 or 1
- g_virt: bfloat16 [2, 4, 128, 128], P(None, 'orb', 'aux'), may hold values from -0.5 to 0.5
- tau_weight: float32 [2], replicated, may hold values from 0.5 to 2
Outputs:
- chi: float32 [256, 2048], P('orb', 'aux')
Inputs may be any that keep to these rules, and one draw needn't show every extreme that they name: `col_blocks`: each row group lists 2 different column blocks, and every column block is listed by some row group.
All inputs are finite; a program needn't handle non-finite values.
Results may differ from a plain program's by a relative error of at most 0.0041.
Values may be sent and summed in bfloat16 or wider, within the bound.
No kernel may reach another device: no remote copies, remote signals or barrier semaphores. Data moves between devices by JAX's collectives and lax.ppermute only.
A program may use at most 128 MiB of HBM per device.

v0:
```python
import math

import jax
import jax.numpy as jnp
from jax import lax
from jax.sharding import PartitionSpec as P


def on_device(b_rows, col_blocks, g_occ, occ_live, g_virt, tau_weight):
    orb_count = lax.axis_size("orb")
    aux_dev, rows_dev, slot_count, tile_width = b_rows.shape
    tau_count = g_occ.shape[0]
    picked = (col_blocks[0][:, None] == jnp.arange(orb_count, dtype=jnp.int32)[None, :]).astype(
        jnp.bfloat16
    )
    outgoing = jnp.einsum("prkc,kd->prdc", b_rows, picked)
    occ_full = lax.all_gather(g_occ, "orb", axis=1, tiled=True)
    total_rows = occ_full.shape[1]
    live_mask = jnp.repeat(jnp.repeat(occ_live, rows_dev, axis=1), rows_dev, axis=2).astype(
        jnp.bfloat16
    )
    occ_masked = occ_full * live_mask
    virt_block = lax.all_gather(g_virt, "aux", axis=2, tiled=True)
    col_dense = lax.all_to_all(outgoing, "orb", split_axis=2, concat_axis=1, tiled=True).reshape(
        aux_dev, total_rows, tile_width
    )
    virt_list = []
    for moment in range(tau_count):
        product = jnp.dot(
            col_dense.reshape(aux_dev * total_rows, tile_width),
            virt_block[moment, 0],
            preferred_element_type=jnp.float32,
        )
        virt_list.append(product.astype(jnp.bfloat16).reshape(aux_dev, total_rows, tile_width))
    partial_value = jnp.zeros((aux_dev, aux_dev), jnp.float32)
    for moment in range(tau_count):
        occ_prod = jnp.einsum(
            "mn,qnc->qmc", occ_masked[moment], col_dense, preferred_element_type=jnp.float32
        ).astype(jnp.bfloat16)
        term = jnp.einsum(
            "pmc,qmc->qp", virt_list[moment], occ_prod, preferred_element_type=jnp.float32
        )
        partial_value = partial_value + tau_weight[moment] * term
    partial_value = partial_value * (1.0 / math.sqrt(total_rows * tile_width * orb_count))
    whole_sum = lax.psum(partial_value, "orb")
    share_rows = aux_dev // orb_count
    share = lax.dynamic_slice_in_dim(whole_sum, lax.axis_index("orb") * share_rows, share_rows, 0)
    return share


def solution(mesh):
    in_specs = (
        P("aux", "orb", None, None),
        P("orb", None),
        P(None, "orb", None),
        P(),
        P(None, "orb", "aux", None),
        P(),
    )
    out_specs = P("orb", "aux")
    return jax.shard_map(
        on_device, mesh=mesh, in_specs=in_specs, out_specs=out_specs, check_vma=False
    )
```

profile of v0, /device:TPU:0, one launch (start us, length us, event | category | flops | bytes accessed | tf_op | source)
XLA Modules:
  0.0 119.3 jit_solution(16933550858440141328)
XLA Ops:
  6.5 0.0 copy-start
  6.5 1.2 %copy-done = bf16[256,8,2,128]{3,2,1,0:T(2,128)(2,1)S(1)} copy-done((bf16[256,8,2,128]{3,2,1,0:T(2,128)(2,1)S(1)}, bf16[256,8,2,128]{3,2,1,0:T(2,128)(2,1)}, u32[]{:S(2)}) %copy-start) | copy-done | bytes 1048600
  7.8 2.5 %convolution_bitcast_fusion = bf16[256,8,4,128]{3,2,1,0:T(4,128)(2,1)S(1)} fusion(bf16[256,8,2,128]{3,2,1,0:T(2,128)(2,1)S(1)} %copy-done, s32[2]{0:T(128)} %bitcast.68), kind=kOutput, calls=%fused_computation.14 | convolution fusion | flops 4194312 | bytes 3145736 | tf_op jit(solution)/shard_map/prkc,kd->prdc/dot_general | solution.py:16
  10.3 1.6 %copy.15 = bf16[256,8,4,128]{3,1,0,2:T(8,128)(2,1)} copy(bf16[256,8,4,128]{3,2,1,0:T(4,128)(2,1)S(1)} %convolution_bitcast_fusion) | data formatting | bytes 4194304 | tf_op jit(solution)/shard_map/prkc,kd->prdc/transpose | solution.py:16
  11.9 0.0 copy-start.2
  11.9 0.0 copy-start.3
  11.9 0.0 copy-start.1
  11.9 0.0 copy-start.4
  11.9 5.3 %all-to-all-start = ((bf16[256,8,4,128]{3,1,0,2:T(8,128)(2,1)}), bf16[256,8,4,128]{3,1,0,2:T(8,128)(2,1)S(1)}, u32[]{:S(2)}, u32[]{:S(2)}) async-start(bf16[256,8,4,128]{3,1,0,2:T(8,128)(2,1)} %copy.15), calls=%async_computation | async-start | bytes 4194304 | tf_op jit(solution)/shard_map/all_to_all | solution.py:24
  17.2 0.0 all-reduce.2.cloned.1.call-start
  17.2 0.0 copy-done.2
  17.2 0.1 copy.18
  17.3 0.1 broadcast_in_dim.7
  17.4 0.1 convert_element_type.31
  17.5 0.1 copy.20
  17.6 0.0 copy-done.3
  17.6 26.1 %all_gather.6 = bf16[2,32,32]{2,0,1:T(2,128)(2,1)S(1)} all-gather(bf16[2,8,32]{2,0,1:T(2,128)(2,1)S(1)} %copy.17), channel_id=1, replica_groups=mesh['orb'=4,'aux'=8] {'orb'}, dimensions={1}, use_global_device_ids=true | all-gather | bytes 5120 | tf_op jit(solution)/shard_map/all_gather | solution.py:17
  43.7 0.0 copy-done.1
  43.8 14.3 %all_gather.7 = bf16[2,1,128,128]{3,2,1,0:T(8,128)(2,1)S(1)} all-gather(bf16[2,1,16,128]{3,2,1,0:T(8,128)(2,1)S(1)} %copy-done.1), channel_id=1, replica_groups=mesh['orb'=4,'aux'=8] {'aux'}, dimensions={2}, use_global_device_ids=true | all-gather | bytes 73728 | tf_op jit(solution)/shard_map/all_gather | solution.py:23
  58.1 0.0 copy-done.4
  58.1 0.6 fusion.48
  58.7 0.0 all-to-all-done
  58.7 0.4 copy.16
  59.0 0.7 convolution_convert_fusion.1
  59.7 0.7 convolution_convert_fusion
  60.4 0.7 convert_bitcast_fusion.1
  61.1 1.9 %fusion.39 = f32[256,256]{1,0:T(8,128)S(1)} fusion(bf16[256,32,128]{2,1,0:T(8,128)(2,1)S(1)} %bitcast.67, bf16[256,32,128]{2,1,0:T(8,128)(2,1)S(1)} %convert_bitcast_fusion.1, f32[]{:T(128)} %bitcast), kind=kOutput, calls=%fused_computation.20 | convolution fusion | flops 536936448 | bytes 4456452 | tf_op jit(solution)/shard_map/pmc,qmc->qp/dot_general | solution.py:40
  63.0 0.7 convert_bitcast_fusion
  63.7 2.6 %fusion.34 = f32[256,256]{1,0:T(8,128)} fusion(f32[256,256]{1,0:T(8,128)S(1)} %fusion.39, bf16[256,32,128]{2,1,0:T(8,128)(2,1)S(1)} %bitcast.66, bf16[256,32,128]{2,1,0:T(8,128)(2,1)S(1)} %convert_bitcast_fusion, f32[]{:T(128)} %bitcast.17), kind=kOutput, calls=%fused_computation.19 | convolution fusion | flops 537067520 | bytes 4718596 | tf_op jit(solution)/shard_map/pmc,qmc->qp/dot_general | solution.py:40
  66.2 0.0 all-reduce.2.cloned.1.call-update
  66.3 44.7 %all-reduce.2.cloned.1.call-done = f32[256,256]{1,0:T(8,128)} async-done(((f32[256,256]{1,0:T(8,128)}), f32[256,256]{1,0:T(8,128)}) %all-reduce.2.cloned.1.call-update) | async-done | bytes 262160 | tf_op jit(solution)/shard_map/psum | solution.py:45
  111.0 1.5 %constant_dynamic-slice_fusion = f32[64,256]{1,0:T(8,128)} fusion(f32[256,256]{1,0:T(8,128)} %all-reduce.2.cloned.1.call-done, s32[]{:T(128)S(6)} %select_n.3), kind=kLoop, calls=%fused_computation.30 | loop fusion | bytes 131076 | tf_op jit(solution)/shard_map/dynamic_slice | solution.py:47
  (4 shorter events, 0.0 us)
Async XLA Ops:
  6.5 1.2 %copy-start = (bf16[256,8,2,128]{3,2,1,0:T(2,128)(2,1)S(1)}, bf16[256,8,2,128]{3,2,1,0:T(2,128)(2,1)}, u32[]{:S(2)}) copy-start(bf16[256,8,2,128]{3,2,1,0:T(2,128)(2,1)} %param.6) | copy-start | bytes 3145732
  11.9 5.3 %copy-start.2 = (s32[2,4,4]{2,1,0:T(4,128)S(1)}, s32[2,4,4]{2,1,0:T(4,128)}, u32[]{:S(2)}) copy-start(s32[2,4,4]{2,1,0:T(4,128)} %param.9) | copy-start | bytes 388
  11.9 5.7 %copy-start.3 = (bf16[2,8,32]{2,1,0:T(8,128)(2,1)S(1)}, bf16[2,8,32]{2,1,0:T(8,128)(2,1)}, u32[]{:S(2)}) copy-start(bf16[2,8,32]{2,1,0:T(8,128)(2,1)} %param.8) | copy-start | bytes 3076
  11.9 31.9 %copy-start.1 = (bf16[2,1,16,128]{3,2,1,0:T(8,128)(2,1)S(1)}, bf16[2,1,16,128]{3,2,1,0:T(8,128)(2,1)}, u32[]{:S(2)}) copy-start(bf16[2,1,16,128]{3,2,1,0:T(8,128)(2,1)} %param.10) | copy-start | bytes 24580
  11.9 46.2 %copy-start.4 = (f32[2]{0:T(128)S(1)}, f32[2]{0:T(128)}, u32[]{:S(2)}) copy-start(f32[2]{0:T(128)} %param.11) | copy-start | bytes 28
  11.9 46.8 %all-to-all-start = ((bf16[256,8,4,128]{3,1,0,2:T(8,128)(2,1)}), bf16[256,8,4,128]{3,1,0,2:T(8,128)(2,1)S(1)}, u32[]{:S(2)}, u32[]{:S(2)}) async-start(bf16[256,8,4,128]{3,1,0,2:T(8,128)(2,1)} %copy.15), calls=%async_computation | async-start | bytes 4194304 | tf_op jit(solution)/shard_map/all_to_all | solution.py:24
  17.2 93.8 %all-reduce.2.cloned.1.call-start = ((), (), s32[]{:S(2)}) async-start(), calls=%async_computation.1 | async-start | bytes 524288 | tf_op jit(solution)/shard_map/psum | solution.py:45
Sparse Core Ops, SparseCore 0:
  66.4 44.5 all-reduce.1
where the time goes:
time: 120 us; the launch traced here: 119 us
  waiting for transfers between devices  44.7 us (37%)
  blocking collectives  40.4 us (34%)
  between operations  13.5 us (11%)
  matrix products  9.68 us (8%)
  local copies, waits for them, and re-layouts  5.65 us (5%)
  starting transfers between devices  5.31 us (4%)
    psum x1, waiting for transfers between devices, on_device(): whole_sum = lax.psum(partial_value, 'orb')  44.7 us
    all_gather x1, blocking collectives, on_device(): occ_full = lax.all_gather(g_occ, 'orb', axis=1, tiled=True)  26.1 us
    all_gather x1, blocking collectives, on_device(): virt_block = lax.all_gather(g_virt, 'aux', axis=2, tiled=True)  14.3 us
    all_to_all x1, starting transfers between devices, on_device(): lax.all_to_all(outgoing, 'orb', split_axis=2, concat_axis=1, tiled=True)  5.31 us
    dot_general x2, matrix products, on_device(): jnp.einsum('pmc,qmc->qp', virt_list[moment], occ_prod, preferred_element_...  4.44 us
    dot_general x1, matrix products, on_device(): outgoing = jnp.einsum('prkc,kd->prdc', b_rows, picked)  2.51 us
  transfers between devices with their start and end apart: 2, of which 1 were waited for; matrix products, arithmetic and copies ran while one was open for 1% of the time, Pallas kernels for 0%

commit v1 on v0

v1 whole, which is shorter than its diff:
```python
import functools
import math

import jax
import jax.numpy as jnp
from jax import lax
from jax.experimental import pallas as pl
from jax.experimental.pallas import tpu as pltpu
from jax.sharding import PartitionSpec as P

SUB = 8
PAIR = 16
F32 = jnp.float32
BF16 = jnp.bfloat16


def iota(shape, dim):
    return lax.broadcasted_iota(jnp.int32, shape, dim)


def dot(a, b):
    return jnp.dot(a, b, preferred_element_type=F32)


def pack_kernel(orb_count, rows_dev, slot_count, steps, me_ref, col_ref, b_ref, occ_ref, *outs):
    me = me_ref[0]
    half_rows = rows_dev * SUB
    out_rows = 2 * half_rows
    in_rows = PAIR * rows_dev * slot_count
    line = iota((out_rows, in_rows), 0)
    place = iota((out_rows, in_rows), 1)
    half = line // half_rows
    row = (line % half_rows) // SUB
    func = half * SUB + line % SUB
    first = (func * rows_dev + row) * slot_count
    pick = jnp.concatenate(
        [jnp.where(place == first + slot, 1.0, 0.0).astype(BF16) for slot in range(slot_count)], 0
    )
    total = steps * out_rows
    for out in outs:
        out[total:, :] = jnp.zeros((out.shape[0] - total, out.shape[1]), BF16)
        out[total:, : occ_ref.shape[1]] = occ_ref[...]

    def step(index, carry):
        source = b_ref[pl.ds(pl.multiple_of(index * in_rows, in_rows), in_rows), :]
        moved = dot(pick, source).astype(BF16)
        slots = [moved[slot * out_rows : (slot + 1) * out_rows] for slot in range(slot_count)]
        zero = jnp.zeros_like(slots[0])
        for distance, out in enumerate(outs):
            value = zero
            for slot in range(slot_count):
                value = jnp.where(col_ref[0, slot] == me ^ distance, slots[slot], value)
            out[pl.ds(pl.multiple_of(index * out_rows, out_rows), out_rows), :] = value
        return carry

    lax.fori_loop(0, steps, step, 0, unroll=min(steps, 4))


def work_kernel(
    orb_count, aux_count, rows_dev, tau_count, steps, share_rows,
    me_ref, live_ref, tau_ref, virt_ref, *refs,
):
    blocks, outs = refs[:orb_count], refs[orb_count : 2 * orb_count]
    mix_ref, occ_ref, virt_out = refs[2 * orb_count :]
    me, aux_me = me_ref[0], me_ref[1]
    rows = orb_count * rows_dev
    half_rows = rows_dev * SUB
    tile = blocks[0].shape[1]
    total = steps * 2 * half_rows
    part = tile // aux_count
    parts = []
    line = iota((tile, virt_ref.shape[0]), 0)
    place = iota((tile, virt_ref.shape[0]), 1)
    for moment in range(tau_count):
        wanted = (((line // part) ^ aux_me) * tau_count + moment) * part + line % part
        parts.append(dot(jnp.where(place == wanted, 1.0, 0.0).astype(BF16), virt_ref[...]).astype(BF16))
    virt = jnp.concatenate(parts, 1)
    occ_all = jnp.concatenate([block[total : total + tau_count * rows_dev, :] for block in blocks], 0)
    left_shape = (tau_count * rows * SUB, occ_all.shape[0])
    line = iota(left_shape, 0)
    moment_of = line // (rows * SUB)
    row_of = (line % (rows * SUB)) // SUB
    wanted = ((row_of // rows_dev) * tau_count + moment_of) * rows_dev + row_of % rows_dev
    left = jnp.where(iota(left_shape, 1) == wanted, 1.0, 0.0).astype(BF16)
    right_shape = (tile, rows * SUB)
    col_of = iota(right_shape, 1) // SUB
    wanted = ((col_of // rows_dev) ^ me) * rows_dev + col_of % rows_dev
    right = jnp.where(iota(right_shape, 0) == wanted, 1.0, 0.0).astype(BF16)
    spread = dot(dot(left, occ_all).astype(BF16), right)
    same = iota((half_rows, rows * SUB), 0) % SUB == iota((half_rows, rows * SUB), 1) % SUB
    group_of = iota((1, rows * SUB), 1) // half_rows
    for moment in range(tau_count):
        for row_group in range(orb_count):
            live = jnp.zeros((1, rows * SUB), jnp.int32)
            for col_group in range(orb_count):
                value = live_ref[(moment * orb_count + (me ^ row_group)) * orb_count + (me ^ col_group)]
                live = jnp.where(group_of == col_group, value, live)
            at = (moment * orb_count + row_group) * half_rows
            keep = jnp.logical_and(same, live != 0)
            mix_ref[at : at + half_rows, :] = jnp.where(keep, spread[at : at + half_rows], 0.0).astype(BF16)

    def step(index, carry):
        occ_halves, virt_halves = [], []
        for half in range(2):
            at = pl.multiple_of((index * 2 + half) * half_rows, half_rows)
            dense = jnp.concatenate([block[pl.ds(at, half_rows), :] for block in blocks], 0)
            occ_halves.append(dot(mix_ref[...], dense).reshape(tau_count * rows, SUB, tile))
            virt_halves.append(dot(dense, virt).reshape(rows, SUB, tau_count * tile))
        occ = jnp.concatenate(occ_halves, 1).astype(BF16)
        vir = jnp.concatenate(virt_halves, 1).astype(BF16)
        here = pl.ds(pl.multiple_of(index * PAIR, PAIR), PAIR)
        for moment in range(tau_count):
            for row in range(rows):
                at = (moment * rows + row) * tile
                occ_ref[here, at : at + tile] = occ[moment * rows + row]
                virt_out[here, at : at + tile] = vir[row, :, moment * tile : (moment + 1) * tile]
        return carry

    lax.fori_loop(0, steps, step, 0)
    chi = None
    depth = rows * tile
    part = min(depth, 4096)
    for moment in range(tau_count):
        for piece in range(depth // part):
            at = moment * depth + piece * part
            term = lax.dot_general(
                occ_ref[:, at : at + part], virt_out[:, at : at + part],
                (((1,), (1,)), ((), ())), preferred_element_type=F32,
            ) * tau_ref[moment]
            chi = term if chi is None else chi + term
    occ_rows = chi * (1.0 / math.sqrt(rows * tile * orb_count))
    hold = outs[0]
    funcs = occ_rows.shape[0]
    for distance, out in enumerate(outs):
        picked = occ_rows[0:share_rows]
        for owner in range(1, orb_count):
            picked = jnp.where(me ^ distance == owner, occ_rows[owner * share_rows : (owner + 1) * share_rows], picked)
        out[...] = picked


def on_device(b_rows, col_blocks, g_occ, occ_live, g_virt, tau_weight):
    orb_count = lax.axis_size("orb")
    aux_count = lax.axis_size("aux")
    aux_dev, rows_dev, slot_count, tile = b_rows.shape
    tau_count = g_occ.shape[0]
    rows = orb_count * rows_dev
    steps = aux_dev // PAIR
    share_rows = aux_dev // orb_count
    me = jnp.stack([lax.axis_index("orb"), lax.axis_index("aux")]).astype(jnp.int32)
    smem = pl.BlockSpec(memory_space=pltpu.SMEM)
    vmem = pl.BlockSpec(memory_space=pltpu.VMEM)
    occ_rows = tau_count * rows_dev
    block = jax.ShapeDtypeStruct((aux_dev * rows_dev + occ_rows, tile), BF16)
    blocks = pl.pallas_call(
        functools.partial(pack_kernel, orb_count, rows_dev, slot_count, steps),
        out_shape=[block] * orb_count,
        in_specs=[smem, smem, vmem, vmem],
        out_specs=[vmem] * orb_count,
        compiler_params=pltpu.CompilerParams(vmem_limit_bytes=32 << 20),
        name="pack",
    )(me, col_blocks, b_rows.reshape(-1, tile), g_occ.reshape(occ_rows, -1))
    dense = [blocks[0]]
    for distance in range(1, orb_count):
        dense.append(lax.ppermute(blocks[distance], "orb", [(i, i ^ distance) for i in range(orb_count)]))
    virt = g_virt.reshape(1, -1, tile)
    distance = 1
    while distance < aux_count:
        other = lax.ppermute(virt, "aux", [(i, i ^ distance) for i in range(aux_count)])
        virt = jnp.concatenate([virt, other], 0)
        distance *= 2
    shares = pl.pallas_call(
        functools.partial(work_kernel, orb_count, aux_count, rows_dev, tau_count, steps, share_rows),
        out_shape=[jax.ShapeDtypeStruct((share_rows, aux_dev), F32)] * orb_count,
        in_specs=[smem, smem, smem, vmem] + [vmem] * orb_count,
        out_specs=[vmem] * orb_count,
        scratch_shapes=[
            pltpu.VMEM((tau_count * rows * SUB, rows * SUB), BF16),
            pltpu.VMEM((aux_dev, tau_count * rows * tile), BF16),
            pltpu.VMEM((aux_dev, tau_count * rows * tile), BF16),
        ],
        compiler_params=pltpu.CompilerParams(vmem_limit_bytes=60 << 20),
        name="work",
    )(me, occ_live.reshape(-1), tau_weight, virt.reshape(-1, tile), *dense)
    total = shares[0]
    for distance in range(1, orb_count):
        total = total + lax.ppermute(shares[distance], "orb", [(i, i ^ distance) for i in range(orb_count)])
    return total


def solution(mesh):
    in_specs = (
        P("aux", "orb", None, None),
        P("orb", None),
        P(None, "orb", None),
        P(),
        P(None, "orb", "aux", None),
        P(),
    )
    out_specs = P("orb", "aux")
    return jax.shard_map(
        on_device, mesh=mesh, in_specs=in_specs, out_specs=out_specs, check_vma=False
    )
```

time: 120 us -> 52.2 us (0.43)
  blocking collectives: 40.4 us -> 0 us
  waiting for transfers between devices: 44.7 us -> 20.8 us
  between operations: 13.5 us -> 0.05 us
  Pallas kernels: 0 us -> 11.5 us
  matrix products: 9.68 us -> 0 us
  starting transfers between devices: 5.31 us -> 13 us
  other arithmetic: 0.01 us -> 2.21 us
  local copies, waits for them, and re-layouts: 5.65 us -> 4.32 us
    psum x1 -> x0, waiting for transfers between devices: 44.7 us -> none  [on_device(): whole_sum = lax.psum(partial_value, 'orb')]
    all_gather x2 -> x0, blocking collectives: 40.4 us -> none  [the longest x1 26.1 us: on_device(): occ_full = lax.all_gather(g_occ, 'orb', axis=1, tiled=True)]
    ppermute x0 -> x9, waiting for transfers between devices: none -> 20.8 us  [the longest x3 12.7 us: on_device(): lax.ppermute(blocks[distance], 'orb', [(i, i ^ distance) for i in range(o...]
    ppermute x0 -> x9, starting transfers between devices: none -> 13 us  [the longest x3 5.09 us: on_device(): lax.ppermute(virt, 'aux', [(i, i ^ distance) for i in range(aux_count)])]
    pallas_call x0 -> x2, Pallas kernels: none -> 11.5 us  [the longest x1 9.67 us: on_device(): pl.pallas_call(functools.partial(work_kernel, orb_count, aux_count, rows_...]
    dot_general x7 -> x0, matrix products: 9.68 us -> none  [the longest x2 4.44 us: on_device(): jnp.einsum('pmc,qmc->qp', virt_list[moment], occ_prod, preferred_element_...]
    all_to_all x1 -> x0, starting transfers between devices: 5.31 us -> none  [on_device(): lax.all_to_all(outgoing, 'orb', split_axis=2, concat_axis=1, tiled=True)]
    unnamed x11 -> x20, local copies, waits for them, and re-layouts: 1.24 us -> 3.64 us
  transfers between devices with their start and end apart: 2 -> 9, of which waited for: 1 -> 8; matrix products, arithmetic and copies ran while one was open for 1% -> 3% of each run, Pallas kernels for 0% -> 0%
where the time goes in v1:
time: 52.2 us; the launch traced here: 51.9 us
  waiting for transfers between devices  20.8 us (40%)
  starting transfers between devices  13 us (25%)
  Pallas kernels  11.5 us (22%)
  local copies, waits for them, and re-layouts  4.32 us (8%)
  other arithmetic  2.21 us (4%)
    ppermute x3, waiting for transfers between devices, on_device(): lax.ppermute(blocks[distance], 'orb', [(i, i ^ distance) for i in range(o...  12.7 us
    pallas_call x1, Pallas kernels, on_device(): pl.pallas_call(functools.partial(work_kernel, orb_count, aux_count, rows_...  9.67 us
    ppermute x3, starting transfers between devices, on_device(): lax.ppermute(virt, 'aux', [(i, i ^ distance) for i in range(aux_count)])  5.09 us
    ppermute x3, starting transfers between devices, on_device(): lax.ppermute(blocks[distance], 'orb', [(i, i ^ distance) for i in range(o...  4.46 us
    ppermute x3, waiting for transfers between devices, on_device(): lax.ppermute(virt, 'aux', [(i, i ^ distance) for i in range(aux_count)])  4.12 us
    ppermute x3, waiting for transfers between devices, on_device(): lax.ppermute(shares[distance], 'orb', [(i, i ^ distance) for i in range(o...  3.93 us
    unnamed x20, local copies, waits for them, and re-layouts  3.64 us
    ppermute x3, starting transfers between devices, on_device(): lax.ppermute(shares[distance], 'orb', [(i, i ^ distance) for i in range(o...  3.49 us
  transfers between devices with their start and end apart: 9, of which 8 were waited for; matrix products, arithmetic and copies ran while one was open for 3% of the time, Pallas kernels for 0%

profile of v1, /device:TPU:0, one launch (start us, length us, event | category | flops | bytes accessed | tf_op | source)
XLA Modules:
  0.0 51.9 jit_solution(34796802929807390)
XLA Ops:
  0.0 0.0 copy-start.2
  0.0 0.1 pad_add_fusion.me_ref
  0.1 0.0 copy-start.3
  0.1 0.0 copy-start.4
  0.1 0.5 copy-done.3
  0.6 0.1 copy-done.2
  0.7 0.0 copy-done.4
  0.7 0.0 copy-start
  0.7 1.2 %copy-done = bf16[256,8,2,128]{3,2,1,0:T(2,128)(2,1)S(1)} copy-done((bf16[256,8,2,128]{3,2,1,0:T(2,128)(2,1)S(1)}, bf16[256,8,2,128]{3,2,1,0:T(2,128)(2,1)}, u32[]{:S(2)}) %copy-start) | copy-done | bytes 1048600
  2.0 0.0 copy-start.8
  2.0 1.8 %pack.1 = (bf16[2064,128]{1,0:T(8,128)(2,1)S(1)}, bf16[2064,128]{1,0:T(8,128)(2,1)S(1)}, bf16[2064,128]{1,0:T(8,128)(2,1)S(1)}, bf16[2064,128]{1,0:T(8,128)(2,1)S(1)}) custom-call(s32[2]{0:T(128)S(1)} %pad_add_fusion.me_ref, s32[1,2]{1,0:T(1,128)S(1)} %copy-done.4, bf16[4096,128]{1,0:T(8,128)(2,1)S(1)} %bitcast.6, bf16[16,32]{1,0:T(8,128)(2,1)S(1)} %bitcast.7), custom_call_target="tpu_custom_call" | custom-call | tf_op jit(solution)/shard_map/pack/pallas_call | solution.py:154
  3.8 0.0 copy-start.1
  3.8 0.8 %copy-done.1 = bf16[2064,128]{1,0:T(8,128)(2,1)} copy-done((bf16[2064,128]{1,0:T(8,128)(2,1)}, bf16[2064,128]{1,0:T(8,128)(2,1)S(1)}, u32[]{:S(2)}) %copy-start.1) | copy-done | bytes 528408
  4.6 2.9 %collective-permute-start.3 = (bf16[2064,128]{1,0:T(8,128)(2,1)S(1)}, bf16[2064,128]{1,0:T(8,128)(2,1)S(1)}, u32[]{:S(2)}, u32[]{:S(2)}) collective-permute-start(bf16[2064,128]{1,0:T(8,128)(2,1)S(1)} %get-tuple-element.14), channel_id=1, source_target_pairs={{0,8},{8,0},{16,24},{24,16},{1,9},{9,1},{17,25},{25,17},{2,10},{10... | collective-permute-start | bytes 1585160 | tf_op jit(solution)/shard_map/ppermute | solution.py:164
  7.6 1.5 %collective-permute-start.4 = (bf16[2064,128]{1,0:T(8,128)(2,1)S(1)}, bf16[2064,128]{1,0:T(8,128)(2,1)S(1)}, u32[]{:S(2)}, u32[]{:S(2)}) collective-permute-start(bf16[2064,128]{1,0:T(8,128)(2,1)S(1)} %get-tuple-element.15), channel_id=1, source_target_pairs={{0,16},{8,24},{16,0},{24,8},{1,17},{9,25},{17,1},{25,9},{2,18},{10... | collective-permute-start | bytes 1585160 | tf_op jit(solution)/shard_map/ppermute | solution.py:164
  9.1 0.0 collective-permute-start.5
  9.1 0.0 copy-done.8
  9.1 0.0 collective-permute-start
  9.1 1.2 %collective-permute-done = bf16[1,32,128]{2,1,0:T(8,128)(2,1)S(1)} collective-permute-done((bf16[1,32,128]{2,1,0:T(8,128)(2,1)S(1)}, bf16[1,32,128]{2,1,0:T(8,128)(2,1)S(1)}, u32[]{:S(2)}, u32[]{:S(2)}) %collective-permute-start) | collective-permute-done | bytes 8224 | tf_op jit(solution)/shard_map/ppermute | solution.py:168
  10.3 0.0 copy-start.9
  10.3 2.0 %collective-permute-start.1 = (bf16[2,32,128]{2,1,0:T(8,128)(2,1)S(1)}, bf16[2,32,128]{2,1,0:T(8,128)(2,1)S(1)}, u32[]{:S(2)}, u32[]{:S(2)}) collective-permute-start(bf16[2,32,128]{2,1,0:T(8,128)(2,1)S(1)} %pad_maximum_fusion.2), channel_id=1, source_target_pairs={{0,2},{1,3},{2,0},{3,1},{4,6},{5,7},{6,4},{7,5},{8,10},{9,11},{10,... | collective-permute-start | bytes 49160 | tf_op jit(solution)/shard_map/ppermute | solution.py:168
  12.3 1.7 %collective-permute-done.1 = bf16[2,32,128]{2,1,0:T(8,128)(2,1)S(1)} collective-permute-done((bf16[2,32,128]{2,1,0:T(8,128)(2,1)S(1)}, bf16[2,32,128]{2,1,0:T(8,128)(2,1)S(1)}, u32[]{:S(2)}, u32[]{:S(2)}) %collective-permute-start.1) | collective-permute-done | bytes 16416 | tf_op jit(solution)/shard_map/ppermute | solution.py:168
  14.0 3.0 %collective-permute-start.2 = (bf16[4,32,128]{2,1,0:T(8,128)(2,1)S(1)}, bf16[4,32,128]{2,1,0:T(8,128)(2,1)S(1)}, u32[]{:S(2)}, u32[]{:S(2)}) collective-permute-start(bf16[4,32,128]{2,1,0:T(8,128)(2,1)S(1)} %pad_maximum_fusion.1), channel_id=1, source_target_pairs={{0,4},{1,5},{2,6},{3,7},{4,0},{5,1},{6,2},{7,3},{8,12},{9,13},{10,... | collective-permute-start | bytes 98312 | tf_op jit(solution)/shard_map/ppermute | solution.py:168
  17.1 0.0 copy-done.9
  17.1 0.7 %reshape.15.live_ref = s32[32]{0:T(128)} reshape(s32[2,4,4]{2,1,0:T(4,128)S(1)} %copy-done.9) | data formatting | bytes 256 | tf_op jit(solution)/shard_map/reshape | solution.py:183
  17.8 1.2 %collective-permute-done.2 = bf16[4,32,128]{2,1,0:T(8,128)(2,1)S(1)} collective-permute-done((bf16[4,32,128]{2,1,0:T(8,128)(2,1)S(1)}, bf16[4,32,128]{2,1,0:T(8,128)(2,1)S(1)}, u32[]{:S(2)}, u32[]{:S(2)}) %collective-permute-start.2) | collective-permute-done | bytes 32800 | tf_op jit(solution)/shard_map/ppermute | solution.py:168
  19.0 0.6 %pad_maximum_fusion = bf16[8,32,128]{2,1,0:T(8,128)(2,1)} fusion(bf16[4,32,128]{2,1,0:T(8,128)(2,1)S(1)} %collective-permute-done.2, bf16[2,32,128]{2,1,0:T(8,128)(2,1)S(1)} %collective-permute-done.1, bf16[1,32,128]{2,1,0:T(8,128)(2,1)S(1)} %collective-permute-done, bf16[1,32,128]{2,1,0:T(8,128)(2,1)S(1)} %bitcast.12), kind=kLoop, calls=%fused_computation | loop fusion | flops 98304 | bytes 131072 | tf_op jit(solution)/shard_map/concatenate | solution.py:169
  19.6 0.8 %collective-permute-done.3.refs_1_ = bf16[2064,128]{1,0:T(8,128)(2,1)S(1)} collective-permute-done((bf16[2064,128]{1,0:T(8,128)(2,1)S(1)}, bf16[2064,128]{1,0:T(8,128)(2,1)S(1)}, u32[]{:S(2)}, u32[]{:S(2)}) %collective-permute-start.3) | collective-permute-done | bytes 528416 | tf_op jit(solution)/shard_map/ppermute | solution.py:164
  20.4 0.0 copy-start.5
  20.4 12.0 %collective-permute-done.4.refs_2_ = bf16[2064,128]{1,0:T(8,128)(2,1)S(1)} collective-permute-done((bf16[2064,128]{1,0:T(8,128)(2,1)S(1)}, bf16[2064,128]{1,0:T(8,128)(2,1)S(1)}, u32[]{:S(2)}, u32[]{:S(2)}) %collective-permute-start.4) | collective-permute-done | bytes 528416 | tf_op jit(solution)/shard_map/ppermute | solution.py:164
  32.4 0.0 copy-start.6
  32.4 0.0 collective-permute-done.5.refs_3_
  32.4 0.0 copy-start.7
  32.4 0.0 copy-done.5
  32.4 0.8 %copy-done.6 = bf16[2064,128]{1,0:T(8,128)(2,1)} copy-done((bf16[2064,128]{1,0:T(8,128)(2,1)}, bf16[2064,128]{1,0:T(8,128)(2,1)S(1)}, u32[]{:S(2)}) %copy-start.6) | copy-done | bytes 528408
  33.2 0.2 copy-done.7
  33.3 9.7 %work.1 = (f32[64,256]{1,0:T(8,128)}, f32[64,256]{1,0:T(8,128)}, f32[64,256]{1,0:T(8,128)}, f32[64,256]{1,0:T(8,128)}) custom-call(s32[2]{0:T(128)} %copy-done.3, s32[32]{0:T(128)} %reshape.15.live_ref, f32[2]{0:T(128)} %tau_ref.1, bf16[256,128]{1,0:T(8,128)(2,1)} %bitcast.8, bf16[2064,128]{1,0:T(8,128)(2,1)} %copy-done.1, bf16[2064,128]{1,0:T(8,128)(2,1)} %copy-done.5, ...), custom_call_target="tpu_custom_call" | custom-call | tf_op jit(solution)/shard_map/work/pallas_call | solution.py:171
  43.0 1.1 %collective-permute-start.6 = (f32[64,256]{1,0:T(8,128)}, f32[64,256]{1,0:T(8,128)S(1)}, u32[]{:S(2)}, u32[]{:S(2)}) collective-permute-start(f32[64,256]{1,0:T(8,128)} %get-tuple-element.18), channel_id=1, source_target_pairs={{0,8},{8,0},{16,24},{24,16},{1,9},{9,1},{17,25},{25,17},{2,10},{10... | collective-permute-start | bytes 196616 | tf_op jit(solution)/shard_map/ppermute | solution.py:186
  44.1 1.0 %collective-permute-start.7 = (f32[64,256]{1,0:T(8,128)}, f32[64,256]{1,0:T(8,128)S(1)}, u32[]{:S(2)}, u32[]{:S(2)}) collective-permute-start(f32[64,256]{1,0:T(8,128)} %get-tuple-element.19), channel_id=1, source_target_pairs={{0,16},{8,24},{16,0},{24,8},{1,17},{9,25},{17,1},{25,9},{2,18},{10... | collective-permute-start | bytes 196616 | tf_op jit(solution)/shard_map/ppermute | solution.py:186
  45.0 1.4 %collective-permute-start.8 = (f32[64,256]{1,0:T(8,128)}, f32[64,256]{1,0:T(8,128)S(1)}, u32[]{:S(2)}, u32[]{:S(2)}) collective-permute-start(f32[64,256]{1,0:T(8,128)} %get-tuple-element.20), channel_id=1, source_target_pairs={{0,24},{8,16},{16,8},{24,0},{1,25},{9,17},{17,9},{25,1},{2,26},{10... | collective-permute-start | bytes 196616 | tf_op jit(solution)/shard_map/ppermute | solution.py:186
  46.5 1.7 %collective-permute-done.6 = f32[64,256]{1,0:T(8,128)S(1)} collective-permute-done((f32[64,256]{1,0:T(8,128)}, f32[64,256]{1,0:T(8,128)S(1)}, u32[]{:S(2)}, u32[]{:S(2)}) %collective-permute-start.6) | collective-permute-done | bytes 65568 | tf_op jit(solution)/shard_map/ppermute | solution.py:186
  48.1 0.4 collective-permute-done.7
  48.5 1.9 %collective-permute-done.8 = f32[64,256]{1,0:T(8,128)S(1)} collective-permute-done((f32[64,256]{1,0:T(8,128)}, f32[64,256]{1,0:T(8,128)S(1)}, u32[]{:S(2)}, u32[]{:S(2)}) %collective-permute-start.8) | collective-permute-done | bytes 65568 | tf_op jit(solution)/shard_map/ppermute | solution.py:186
  50.4 1.5 %add_add_fusion = f32[64,256]{1,0:T(8,128)} fusion(f32[64,256]{1,0:T(8,128)S(1)} %collective-permute-done.8, f32[64,256]{1,0:T(8,128)S(1)} %collective-permute-done.7, f32[64,256]{1,0:T(8,128)} %get-tuple-element.17, f32[64,256]{1,0:T(8,128)S(1)} %collective-permute-done.6), kind=kLoop, calls=%fused_computation.1 | loop fusion | flops 49152 | bytes 327680 | tf_op jit(solution)/shard_map/add | solution.py:186
  (2 shorter events, 0.0 us)
Async XLA Ops:
  0.0 0.7 %copy-start.2 = (bf16[2,8,32]{2,1,0:T(8,128)(2,1)S(1)}, bf16[2,8,32]{2,1,0:T(8,128)(2,1)}, u32[]{:S(2)}) copy-start(bf16[2,8,32]{2,1,0:T(8,128)(2,1)} %param.8) | copy-start | bytes 3076
  0.1 0.5 copy-start.3
  0.1 0.7 %copy-start.4 = (s32[1,2]{1,0:T(1,128)S(1)}, s32[1,2]{1,0:T(1,128)}, u32[]{:S(2)}) copy-start(s32[1,2]{1,0:T(1,128)} %col_ref.1) | copy-start | bytes 28
  0.7 1.2 %copy-start = (bf16[256,8,2,128]{3,2,1,0:T(2,128)(2,1)S(1)}, bf16[256,8,2,128]{3,2,1,0:T(2,128)(2,1)}, u32[]{:S(2)}) copy-start(bf16[256,8,2,128]{3,2,1,0:T(2,128)(2,1)} %param.6) | copy-start | bytes 3145732
  2.0 7.1 %copy-start.8 = (bf16[2,1,16,128]{3,2,1,0:T(8,128)(2,1)S(1)}, bf16[2,1,16,128]{3,2,1,0:T(8,128)(2,1)}, u32[]{:S(2)}) copy-start(bf16[2,1,16,128]{3,2,1,0:T(8,128)(2,1)} %param.10) | copy-start | bytes 24580
  3.8 0.8 %copy-start.1 = (bf16[2064,128]{1,0:T(8,128)(2,1)}, bf16[2064,128]{1,0:T(8,128)(2,1)S(1)}, u32[]{:S(2)}) copy-start(bf16[2064,128]{1,0:T(8,128)(2,1)S(1)} %get-tuple-element.13.refs_0_) | copy-start | bytes 1585156
  4.6 15.8 %collective-permute-start.3 = (bf16[2064,128]{1,0:T(8,128)(2,1)S(1)}, bf16[2064,128]{1,0:T(8,128)(2,1)S(1)}, u32[]{:S(2)}, u32[]{:S(2)}) collective-permute-start(bf16[2064,128]{1,0:T(8,128)(2,1)S(1)} %get-tuple-element.14), channel_id=1, source_target_pairs={{0,8},{8,0},{16,24},{24,16},{1,9},{9,1},{17,25},{25,17},{2,10},{10... | collective-permute-start | bytes 1585160 | tf_op jit(solution)/shard_map/ppermute | solution.py:164
  7.6 24.8 %collective-permute-start.4 = (bf16[2064,128]{1,0:T(8,128)(2,1)S(1)}, bf16[2064,128]{1,0:T(8,128)(2,1)S(1)}, u32[]{:S(2)}, u32[]{:S(2)}) collective-permute-start(bf16[2064,128]{1,0:T(8,128)(2,1)S(1)} %get-tuple-element.15), channel_id=1, source_target_pairs={{0,16},{8,24},{16,0},{24,8},{1,17},{9,25},{17,1},{25,9},{2,18},{10... | collective-permute-start | bytes 1585160 | tf_op jit(solution)/shard_map/ppermute | solution.py:164
  9.1 23.3 %collective-permute-start.5 = (bf16[2064,128]{1,0:T(8,128)(2,1)S(1)}, bf16[2064,128]{1,0:T(8,128)(2,1)S(1)}, u32[]{:S(2)}, u32[]{:S(2)}) collective-permute-start(bf16[2064,128]{1,0:T(8,128)(2,1)S(1)} %get-tuple-element.16), channel_id=1, source_target_pairs={{0,24},{8,16},{16,8},{24,0},{1,25},{9,17},{17,9},{25,1},{2,26},{10... | collective-permute-start | bytes 1585160 | tf_op jit(solution)/shard_map/ppermute | solution.py:164
  9.1 1.2 %collective-permute-start = (bf16[1,32,128]{2,1,0:T(8,128)(2,1)S(1)}, bf16[1,32,128]{2,1,0:T(8,128)(2,1)S(1)}, u32[]{:S(2)}, u32[]{:S(2)}) collective-permute-start(bf16[1,32,128]{2,1,0:T(8,128)(2,1)S(1)} %bitcast.9), channel_id=1, source_target_pairs={{0,1},{1,0},{2,3},{3,2},{4,5},{5,4},{6,7},{7,6},{8,9},{9,8},{10,11... | collective-permute-start | bytes 24584 | tf_op jit(solution)/shard_map/ppermute | solution.py:168
  10.3 6.8 %copy-start.9 = (s32[2,4,4]{2,1,0:T(4,128)S(1)}, s32[2,4,4]{2,1,0:T(4,128)}, u32[]{:S(2)}) copy-start(s32[2,4,4]{2,1,0:T(4,128)} %param.9) | copy-start | bytes 388
  10.3 3.8 %collective-permute-start.1 = (bf16[2,32,128]{2,1,0:T(8,128)(2,1)S(1)}, bf16[2,32,128]{2,1,0:T(8,128)(2,1)S(1)}, u32[]{:S(2)}, u32[]{:S(2)}) collective-permute-start(bf16[2,32,128]{2,1,0:T(8,128)(2,1)S(1)} %pad_maximum_fusion.2), channel_id=1, source_target_pairs={{0,2},{1,3},{2,0},{3,1},{4,6},{5,7},{6,4},{7,5},{8,10},{9,11},{10,... | collective-permute-start | bytes 49160 | tf_op jit(solution)/shard_map/ppermute | solution.py:168
  14.0 5.0 %collective-permute-start.2 = (bf16[4,32,128]{2,1,0:T(8,128)(2,1)S(1)}, bf16[4,32,128]{2,1,0:T(8,128)(2,1)S(1)}, u32[]{:S(2)}, u32[]{:S(2)}) collective-permute-start(bf16[4,32,128]{2,1,0:T(8,128)(2,1)S(1)} %pad_maximum_fusion.1), channel_id=1, source_target_pairs={{0,4},{1,5},{2,6},{3,7},{4,0},{5,1},{6,2},{7,3},{8,12},{9,13},{10,... | collective-permute-start | bytes 98312 | tf_op jit(solution)/shard_map/ppermute | solution.py:168
  20.4 12.0 %copy-start.5 = (bf16[2064,128]{1,0:T(8,128)(2,1)}, bf16[2064,128]{1,0:T(8,128)(2,1)S(1)}, u32[]{:S(2)}) copy-start(bf16[2064,128]{1,0:T(8,128)(2,1)S(1)} %collective-permute-done.3.refs_1_) | copy-start | bytes 1585156
  32.4 0.8 %copy-start.6 = (bf16[2064,128]{1,0:T(8,128)(2,1)}, bf16[2064,128]{1,0:T(8,128)(2,1)S(1)}, u32[]{:S(2)}) copy-start(bf16[2064,128]{1,0:T(8,128)(2,1)S(1)} %collective-permute-done.4.refs_2_) | copy-start | bytes 1585156
  32.4 1.0 %copy-start.7 = (bf16[2064,128]{1,0:T(8,128)(2,1)}, bf16[2064,128]{1,0:T(8,128)(2,1)S(1)}, u32[]{:S(2)}) copy-start(bf16[2064,128]{1,0:T(8,128)(2,1)S(1)} %collective-permute-done.5.refs_3_) | copy-start | bytes 1585156
  43.0 5.1 %collective-permute-start.6 = (f32[64,256]{1,0:T(8,128)}, f32[64,256]{1,0:T(8,128)S(1)}, u32[]{:S(2)}, u32[]{:S(2)}) collective-permute-start(f32[64,256]{1,0:T(8,128)} %get-tuple-element.18), channel_id=1, source_target_pairs={{0,8},{8,0},{16,24},{24,16},{1,9},{9,1},{17,25},{25,17},{2,10},{10... | collective-permute-start | bytes 196616 | tf_op jit(solution)/shard_map/ppermute | solution.py:186
  44.1 4.5 %collective-permute-start.7 = (f32[64,256]{1,0:T(8,128)}, f32[64,256]{1,0:T(8,128)S(1)}, u32[]{:S(2)}, u32[]{:S(2)}) collective-permute-start(f32[64,256]{1,0:T(8,128)} %get-tuple-element.19), channel_id=1, source_target_pairs={{0,16},{8,24},{16,0},{24,8},{1,17},{9,25},{17,1},{25,9},{2,18},{10... | collective-permute-start | bytes 196616 | tf_op jit(solution)/shard_map/ppermute | solution.py:186
  45.0 5.4 %collective-permute-start.8 = (f32[64,256]{1,0:T(8,128)}, f32[64,256]{1,0:T(8,128)S(1)}, u32[]{:S(2)}, u32[]{:S(2)}) collective-permute-start(f32[64,256]{1,0:T(8,128)} %get-tuple-element.20), channel_id=1, source_target_pairs={{0,24},{8,16},{16,8},{24,0},{1,25},{9,17},{17,9},{25,1},{2,26},{10... | collective-permute-start | bytes 196616 | tf_op jit(solution)/shard_map/ppermute | solution.py:186

commit v2 on v1

v2 whole, which is shorter than its diff:
```python
import functools
import math

import jax
import jax.numpy as jnp
from jax import lax
from jax.experimental import pallas as pl
from jax.experimental.pallas import tpu as pltpu
from jax.sharding import PartitionSpec as P

SUB = 8
PAIR = 16
F32 = jnp.float32
BF16 = jnp.bfloat16


def iota(shape, dim):
    return lax.broadcasted_iota(jnp.int32, shape, dim)


def dot(a, b):
    return jnp.dot(a, b, preferred_element_type=F32)


def pack_kernel(rows_dev, slot_count, chunks, pieces, col_hbm, b_hbm, occ_hbm, *refs):
    orb_count = lax.axis_size("orb")
    count = len(chunks) * orb_count
    outs, helds = refs[:count], refs[count : 2 * count]
    b_ref, occ_ref, col_ref, b_sem, occ_sem, col_sem, out_sem = refs[2 * count :]
    me = lax.axis_index("orb")
    half_rows = rows_dev * SUB
    out_rows = 2 * half_rows
    in_rows = PAIR * rows_dev * slot_count
    steps = sum(chunks)
    piece_steps = steps // pieces
    piece_rows = piece_steps * in_rows

    def fetch(piece):
        here = pl.ds(piece * piece_rows, piece_rows)
        return pltpu.make_async_copy(b_hbm.at[here], b_ref.at[here], b_sem.at[piece])

    occ_copy = pltpu.make_async_copy(occ_hbm, occ_ref, occ_sem)
    col_copy = pltpu.make_async_copy(col_hbm, col_ref, col_sem)
    col_copy.start()
    for piece in range(pieces):
        fetch(piece).start()
    occ_copy.start()
    line = iota((out_rows, in_rows), 0)
    place = iota((out_rows, in_rows), 1)
    half = line // half_rows
    row = (line % half_rows) // SUB
    func = half * SUB + line % SUB
    first = (func * rows_dev + row) * slot_count
    pick = jnp.concatenate(
        [jnp.where(place == first + slot, 1.0, 0.0).astype(BF16) for slot in range(slot_count)], 0
    )
    occ_copy.wait()
    total = chunks[0] * out_rows
    for held in helds[:orb_count]:
        held[total:, :] = jnp.zeros((held.shape[0] - total, held.shape[1]), BF16)
        held[total:, : occ_ref.shape[1]] = occ_ref[...]
    col_copy.wait()

    def step(index, group, start):
        at = pl.multiple_of(index * in_rows, in_rows)
        moved = dot(pick, b_ref[pl.ds(at, in_rows), :]).astype(BF16)
        slots = [moved[slot * out_rows : (slot + 1) * out_rows] for slot in range(slot_count)]
        zero = jnp.zeros_like(slots[0])
        for distance, held in enumerate(group):
            value = zero
            for slot in range(slot_count):
                value = jnp.where(col_ref[0, slot] == me ^ distance, slots[slot], value)
            held[pl.ds(pl.multiple_of((index - start) * out_rows, out_rows), out_rows), :] = value

    sent = []
    start = 0
    for number, chunk in enumerate(chunks):
        group = range(number * orb_count, (number + 1) * orb_count)
        for piece in range(start // piece_steps, (start + chunk) // piece_steps):
            fetch(piece).wait()
            low = piece * piece_steps
            lax.fori_loop(
                low, low + piece_steps,
                lambda index, carry: (step(index, [helds[at] for at in group], start), carry)[1],
                0, unroll=True,
            )
            top = low - start + piece_steps
            low_row = (low - start) * out_rows
            high_row = helds[group[0]].shape[0] if top == chunk else top * out_rows
            for distance, at in enumerate(group):
                here = pl.ds(low_row, high_row - low_row)
                copy = pltpu.make_async_copy(helds[at].at[here], outs[at].at[here], out_sem.at[piece, distance])
                copy.start()
                sent.append(copy)
        start += chunk
    for copy in sent:
        copy.wait()


def join_kernel(one_ref, two_ref, out_ref):
    out_ref[: one_ref.shape[0], :] = one_ref[...]
    out_ref[one_ref.shape[0] :, :] = two_ref[...]


def order_virt(sizes, virt_refs, virt_out):
    orb_count, aux_count, rows_dev, tau_count = sizes
    aux_me = lax.axis_index("aux")
    tile = virt_refs[0].shape[1]
    part = tile // aux_count
    virt_all = jnp.concatenate([ref[...] for ref in virt_refs], 0)
    line = iota((tile, virt_all.shape[0]), 0)
    place = iota((tile, virt_all.shape[0]), 1)
    for moment in range(tau_count):
        wanted = (((line // part) ^ aux_me) * tau_count + moment) * part + line % part
        chosen = dot(jnp.where(place == wanted, 1.0, 0.0).astype(BF16), virt_all)
        virt_out[:, moment * tile : (moment + 1) * tile] = chosen.astype(BF16)


def spread_occ(sizes, live_ref, blocks, total, mix_out):
    orb_count, aux_count, rows_dev, tau_count = sizes
    me = lax.axis_index("orb")
    rows = orb_count * rows_dev
    half_rows = rows_dev * SUB
    tile = blocks[0].shape[1]
    occ_all = jnp.concatenate([block[total : total + tau_count * rows_dev, :] for block in blocks], 0)
    left_shape = (tau_count * rows * SUB, occ_all.shape[0])
    line = iota(left_shape, 0)
    moment_of = line // (rows * SUB)
    row_of = (line % (rows * SUB)) // SUB
    wanted = ((row_of // rows_dev) * tau_count + moment_of) * rows_dev + row_of % rows_dev
    left = jnp.where(iota(left_shape, 1) == wanted, 1.0, 0.0).astype(BF16)
    right_shape = (tile, rows * SUB)
    col_of = iota(right_shape, 1) // SUB
    wanted = ((col_of // rows_dev) ^ me) * rows_dev + col_of % rows_dev
    right = jnp.where(iota(right_shape, 0) == wanted, 1.0, 0.0).astype(BF16)
    spread = dot(dot(left, occ_all).astype(BF16), right)
    same = iota((half_rows, rows * SUB), 0) % SUB == iota((half_rows, rows * SUB), 1) % SUB
    group_of = iota((1, rows * SUB), 1) // half_rows
    for moment in range(tau_count):
        for row_group in range(orb_count):
            live = jnp.zeros((1, rows * SUB), jnp.int32)
            for col_group in range(orb_count):
                value = live_ref[moment, me ^ row_group, me ^ col_group]
                live = jnp.where(group_of == col_group, value, live)
            at = (moment * orb_count + row_group) * half_rows
            keep = jnp.logical_and(same, live != 0)
            mix_out[at : at + half_rows, :] = jnp.where(keep, spread[at : at + half_rows], 0.0).astype(BF16)


def products(sizes, steps, blocks, mix_ref, virt_ref, occ_out, vir_out):
    orb_count, aux_count, rows_dev, tau_count = sizes
    rows = orb_count * rows_dev
    half_rows = rows_dev * SUB
    tile = blocks[0].shape[1]

    def step(index, carry):
        here = pl.ds(pl.multiple_of(index * PAIR, PAIR), PAIR)
        halves = []
        for half in range(2):
            at = pl.multiple_of((index * 2 + half) * half_rows, half_rows)
            halves.append(jnp.concatenate([block[pl.ds(at, half_rows), :] for block in blocks], 0))
        if occ_out is not None:
            occ = dot(mix_ref[...], jnp.concatenate(halves, 1))
            occ = [occ[:, half * tile : (half + 1) * tile].reshape(tau_count * rows, SUB, tile) for half in range(2)]
            occ = jnp.concatenate(occ, 1).astype(BF16)
            for row in range(tau_count * rows):
                occ_out[here, row * tile : (row + 1) * tile] = occ[row]
        if vir_out is not None:
            vir = dot(jnp.concatenate(halves, 0), virt_ref[...]).reshape(2, rows, SUB, tau_count * tile)
            vir = jnp.concatenate([vir[0], vir[1]], 1).astype(BF16)
            for moment in range(tau_count):
                for row in range(rows):
                    at = (moment * rows + row) * tile
                    vir_out[here, at : at + tile] = vir[row, :, moment * tile : (moment + 1) * tile]
        return carry

    lax.fori_loop(0, steps, step, 0, unroll=2)


def occ_kernel(sizes, steps, live_ref, *refs):
    blocks, (mix_out, occ_out) = refs[: sizes[0]], refs[sizes[0] :]
    spread_occ(sizes, live_ref, blocks, steps * 2 * sizes[2] * SUB, mix_out)
    products(sizes, steps, blocks, mix_out, None, occ_out, None)


def vir_kernel(sizes, steps, *refs):
    blocks, virt_refs = refs[: sizes[0]], refs[sizes[0] : -3]
    anchor, virt_out, vir_out = refs[-3:]
    order_virt(sizes, virt_refs, virt_out)
    products(sizes, steps, blocks, None, virt_out, None, vir_out)


def last_kernel(sizes, steps, share_rows, tau_ref, mix_ref, virt_ref, occ_first, vir_first, *refs):
    orb_count, aux_count, rows_dev, tau_count = sizes
    blocks, outs = refs[:orb_count], refs[orb_count : 2 * orb_count]
    occ_last, vir_last = refs[2 * orb_count :]
    products(sizes, steps, blocks, mix_ref, virt_ref, occ_last, vir_last)
    me = lax.axis_index("orb")
    rows = orb_count * rows_dev
    tile = blocks[0].shape[1]
    depth = rows * tile
    part = min(depth, 4096)
    chi = None
    for moment in range(tau_count):
        for piece in range(depth // part):
            here = slice(moment * depth + piece * part, moment * depth + (piece + 1) * part)
            term = lax.dot_general(
                jnp.concatenate([occ_first[:, here], occ_last[:, here]], 0),
                jnp.concatenate([vir_first[:, here], vir_last[:, here]], 0),
                (((1,), (1,)), ((), ())), preferred_element_type=F32,
            ) * tau_ref[moment]
            chi = term if chi is None else chi + term
    chi = chi * (1.0 / math.sqrt(rows * tile * orb_count))
    for distance, out in enumerate(outs):
        picked = chi[0:share_rows]
        for owner in range(1, orb_count):
            picked = jnp.where(me ^ distance == owner, chi[owner * share_rows : (owner + 1) * share_rows], picked)
        out[...] = picked


def on_device(b_rows, col_blocks, g_occ, occ_live, g_virt, tau_weight):
    orb_count = lax.axis_size("orb")
    aux_count = lax.axis_size("aux")
    aux_dev, rows_dev, slot_count, tile = b_rows.shape
    tau_count = g_occ.shape[0]
    rows = orb_count * rows_dev
    share_rows = aux_dev // orb_count
    sizes = (orb_count, aux_count, rows_dev, tau_count)
    smem = pl.BlockSpec(memory_space=pltpu.SMEM)
    vmem = pl.BlockSpec(memory_space=pltpu.VMEM)

    def call(kernel, name, out_shape, in_specs, scratch, spare, out_spec=vmem):
        held = sum(math.prod(shape.shape) * 2 for shape in scratch if shape.dtype == BF16)
        return pl.pallas_call(
            kernel,
            out_shape=out_shape,
            in_specs=in_specs,
            out_specs=[out_spec] * len(out_shape),
            scratch_shapes=scratch,
            compiler_params=pltpu.CompilerParams(vmem_limit_bytes=min(held + (spare << 20), 60 << 20)),
            name=name,
        )

    def xor(value, axis, distance):
        return lax.ppermute(value, axis, [(i, i ^ distance) for i in range(lax.axis_size(axis))])

    def half(value):
        return jax.ShapeDtypeStruct(value, BF16)

    all_steps = aux_dev // PAIR
    chunks = (all_steps // 2, all_steps - all_steps // 2)
    occ_rows = tau_count * rows_dev
    b_flat = b_rows.reshape(-1, tile)
    occ_flat = g_occ.reshape(occ_rows, -1)
    hbm = pl.BlockSpec(memory_space=pl.ANY)
    pieces = math.gcd(4, all_steps)
    shapes = [
        (steps * PAIR * rows_dev + (0 if number else occ_rows), tile)
        for number, steps in enumerate(chunks) for _ in range(orb_count)
    ]
    blocks = call(
        functools.partial(pack_kernel, rows_dev, slot_count, chunks, pieces), "pack",
        [half(shape) for shape in shapes], [hbm] * 3,
        [pltpu.VMEM(shape, BF16) for shape in shapes] + [
            pltpu.VMEM(b_flat.shape, BF16), pltpu.VMEM(occ_flat.shape, BF16), pltpu.SMEM(col_blocks.shape, jnp.int32),
            pltpu.SemaphoreType.DMA((pieces,)), pltpu.SemaphoreType.DMA, pltpu.SemaphoreType.DMA,
            pltpu.SemaphoreType.DMA((pieces, orb_count)),
        ], 54, hbm,
    )(col_blocks, b_flat, occ_flat)
    dense = []
    for number in range(len(chunks)):
        own, *others = blocks[number * orb_count : (number + 1) * orb_count]
        dense.append([own] + [xor(value, "orb", d + 1) for d, value in enumerate(others)])
    virt = g_virt.reshape(-1, tile)
    virt = call(join_kernel, "join", [half((2 * virt.shape[0], tile))], [vmem] * 2, [], 2)(virt, xor(virt, "aux", 1))[0]
    virts = [virt] + [xor(virt, "aux", d) for d in range(2, aux_count, 2)]
    wide = half((chunks[0] * PAIR, tau_count * rows * tile))
    mix, occ_first = call(
        functools.partial(occ_kernel, sizes, chunks[0]), "occ",
        [half((tau_count * rows * SUB, rows * SUB)), wide],
        [smem] + [vmem] * orb_count, [], 8,
    )(occ_live, *dense[0])
    virt, vir_first = call(
        functools.partial(vir_kernel, sizes, chunks[0]), "vir",
        [half((tile, tau_count * tile)), wide],
        [vmem] * (orb_count + len(virts)) + [hbm], [], 8,
    )(*dense[0], *virts, mix)
    shares = call(
        functools.partial(last_kernel, sizes, chunks[1], share_rows), "last",
        [jax.ShapeDtypeStruct((share_rows, aux_dev), F32)] * orb_count,
        [smem] + [vmem] * (4 + orb_count),
        [pltpu.VMEM((chunks[1] * PAIR, tau_count * rows * tile), BF16)] * 2, 12,
    )(tau_weight, mix, virt, occ_first, vir_first, *dense[1])
    total = shares[0]
    for distance in range(1, orb_count):
        total = total + xor(shares[distance], "orb", distance)
    return total


def solution(mesh):
    in_specs = (
        P("aux", "orb", None, None),
        P("orb", None),
        P(None, "orb", None),
        P(),
        P(None, "orb", "aux", None),
        P(),
    )
    out_specs = P("orb", "aux")
    return jax.shard_map(
        on_device, mesh=mesh, in_specs=in_specs, out_specs=out_specs, check_vma=False
    )
```

time: 52.2 us -> 44 us (0.84)
  waiting for transfers between devices: 20.8 us -> 9.22 us
  starting transfers between devices: 13 us -> 21 us
  local copies, waits for them, and re-layouts: 4.32 us -> 2.34 us
  other arithmetic: 2.21 us -> 0.65 us
  Pallas kernels: 11.5 us -> 10.5 us
    ppermute x9 -> x13, waiting for transfers between devices: 20.8 us -> 9.22 us  [xor(): lax.ppermute(value, axis, [(i, i ^ distance) for i in range(lax.axis_size...]
    ppermute x9 -> x13, starting transfers between devices: 13 us -> 21 us  [xor(): lax.ppermute(value, axis, [(i, i ^ distance) for i in range(lax.axis_size...]
    unnamed x20 -> x10, local copies, waits for them, and re-layouts: 3.64 us -> 2.34 us
    pallas_call x2 -> x5, Pallas kernels: 11.5 us -> 10.5 us  [the longest x1 3.51 us: on_device(): call(functools.partial(last_kernel, sizes, chunks[1], share_rows), 'last'...]
    add x1, other arithmetic: 1.49 us -> 0.65 us  [on_device(): total = total + xor(shares[distance], 'orb', distance)]
    reshape x1 -> x0, local copies, waits for them, and re-layouts: 0.68 us -> none  [on_device(): occ_live.reshape(-1)]
    concatenate x3 -> x0, other arithmetic: 0.65 us -> none  [on_device(): virt = jnp.concatenate([virt, other], 0)]
  transfers between devices with their start and end apart: 9 -> 13, of which waited for: 8 -> 5; matrix products, arithmetic and copies ran while one was open for 3% -> 0% of each run, Pallas kernels for 0% -> 8%
where the time goes in v2:
time: 44 us; the launch traced here: 43.7 us
  starting transfers between devices  21 us (48%)
  Pallas kernels  10.5 us (24%)
  waiting for transfers between devices  9.22 us (21%)
  local copies, waits for them, and re-layouts  2.34 us (5%)
  other arithmetic  0.65 us (1%)
    ppermute x13, starting transfers between devices, xor(): lax.ppermute(value, axis, [(i, i ^ distance) for i in range(lax.axis_size...  21 us
    ppermute x13, waiting for transfers between devices, xor(): lax.ppermute(value, axis, [(i, i ^ distance) for i in range(lax.axis_size...  9.22 us
    pallas_call x1, Pallas kernels, on_device(): call(functools.partial(last_kernel, sizes, chunks[1], share_rows), 'last'...  3.51 us
    pallas_call x1, Pallas kernels, on_device(): call(functools.partial(pack_kernel, rows_dev, slot_count, chunks, pieces)...  3.31 us
    unnamed x10, local copies, waits for them, and re-layouts  2.34 us
    pallas_call x1, Pallas kernels, on_device(): call(functools.partial(occ_kernel, sizes, chunks[0]), 'occ', [half((tau_c...  2.27 us
    pallas_call x1, Pallas kernels, on_device(): call(functools.partial(vir_kernel, sizes, chunks[0]), 'vir', [half((tile,...  1.39 us
  transfers between devices with their start and end apart: 13, of which 5 were waited for; matrix products, arithmetic and copies ran while one was open for 0% of the time, Pallas kernels for 8%

profile of v2, /device:TPU:0, one launch (start us, length us, event | category | flops | bytes accessed | tf_op | source)
XLA Modules:
  0.0 43.7 jit_solution(1739490723270706863)
XLA Ops:
  0.0 0.0 copy-start.4
  0.0 3.3 %pack.1 = (bf16[1040,128]{1,0:T(8,128)(2,1)}, bf16[1040,128]{1,0:T(8,128)(2,1)}, bf16[1040,128]{1,0:T(8,128)(2,1)}, bf16[1040,128]{1,0:T(8,128)(2,1)}, bf16[1024...) custom-call(s32[1,2]{1,0:T(1,128)} %col_hbm.1, ...), custom_call_target="tpu_custom_call" | custom-call | tf_op jit(solution)/shard_map/pack/pallas_call | solution.py:261
  3.3 3.0 %collective-permute-start = (bf16[1040,128]{1,0:T(8,128)(2,1)}, bf16[1040,128]{1,0:T(8,128)(2,1)S(1)}, u32[]{:S(2)}, u32[]{:S(2)}) collective-permute-start(bf16[1040,128]{1,0:T(8,128)(2,1)} %get-tuple-element.22), channel_id=1, source_target_pairs={{0,8},{8,0},{16,24},{24,16},{1,9},{9,1},{17,25},{25,17},{2,10},{10... | collective-permute-start | bytes 798728 | tf_op jit(solution)/shard_map/ppermute | solution.py:245
  6.3 0.0 collective-permute-start.3
  6.3 1.5 %collective-permute-start.1 = (bf16[1040,128]{1,0:T(8,128)(2,1)}, bf16[1040,128]{1,0:T(8,128)(2,1)S(1)}, u32[]{:S(2)}, u32[]{:S(2)}) collective-permute-start(bf16[1040,128]{1,0:T(8,128)(2,1)} %get-tuple-element.23), channel_id=1, source_target_pairs={{0,16},{8,24},{16,0},{24,8},{1,17},{9,25},{17,1},{25,9},{2,18},{10... | collective-permute-start | bytes 798728 | tf_op jit(solution)/shard_map/ppermute | solution.py:245
  7.9 0.1 collective-permute-start.2
  8.0 0.0 collective-permute-done.3.two_ref
  8.0 0.0 copy-start.2
  8.0 0.7 %copy-done.2 = bf16[2,1,16,128]{3,2,1,0:T(8,128)(2,1)S(1)} copy-done((bf16[2,1,16,128]{3,2,1,0:T(8,128)(2,1)S(1)}, bf16[2,1,16,128]{3,2,1,0:T(8,128)(2,1)}, u32[]{:S(2)}) %copy-start.2) | copy-done | bytes 8216
  8.7 4.0 %collective-permute-start.6 = (bf16[64,128]{1,0:T(8,128)(2,1)S(1)}, bf16[64,128]{1,0:T(8,128)(2,1)S(1)}, u32[]{:S(2)}, u32[]{:S(2)}) collective-permute-start(bf16[64,128]{1,0:T(8,128)(2,1)S(1)} %join.1.refs_4_), channel_id=1, source_target_pairs={{0,6},{1,7},{2,4},{3,5},{4,2},{5,3},{6,0},{7,1},{8,14},{9,15},{10,... | collective-permute-start | bytes 49160 | tf_op jit(solution)/shard_map/ppermute | solution.py:245
  12.6 1.5 %collective-permute-start.7 = (bf16[1024,128]{1,0:T(8,128)(2,1)}, bf16[1024,128]{1,0:T(8,128)(2,1)S(1)}, u32[]{:S(2)}, u32[]{:S(2)}) collective-permute-start(bf16[1024,128]{1,0:T(8,128)(2,1)} %get-tuple-element.30), channel_id=1, source_target_pairs={{0,8},{8,0},{16,24},{24,16},{1,9},{9,1},{17,25},{25,17},{2,10},{10... | collective-permute-start | bytes 786440 | tf_op jit(solution)/shard_map/ppermute | solution.py:245
  14.1 0.2 collective-permute-done.6.refs_7_
  14.4 1.7 %collective-permute-start.8 = (bf16[1024,128]{1,0:T(8,128)(2,1)}, bf16[1024,128]{1,0:T(8,128)(2,1)S(1)}, u32[]{:S(2)}, u32[]{:S(2)}) collective-permute-start(bf16[1024,128]{1,0:T(8,128)(2,1)} %get-tuple-element.31), channel_id=1, source_target_pairs={{0,16},{8,24},{16,0},{24,8},{1,17},{9,25},{17,1},{25,9},{2,18},{10... | collective-permute-start | bytes 786440 | tf_op jit(solution)/shard_map/ppermute | solution.py:245
  16.1 0.0 collective-permute-done.refs_1_
  16.1 1.4 %collective-permute-start.9 = (bf16[1024,128]{1,0:T(8,128)(2,1)}, bf16[1024,128]{1,0:T(8,128)(2,1)S(1)}, u32[]{:S(2)}, u32[]{:S(2)}) collective-permute-start(bf16[1024,128]{1,0:T(8,128)(2,1)} %get-tuple-element.32), channel_id=1, source_target_pairs={{0,24},{8,16},{16,8},{24,0},{1,25},{9,17},{17,9},{25,1},{2,26},{10... | collective-permute-start | bytes 786440 | tf_op jit(solution)/shard_map/ppermute | solution.py:245
  17.5 3.9 %collective-permute-done.1.refs_2_ = bf16[1040,128]{1,0:T(8,128)(2,1)S(1)} collective-permute-done((bf16[1040,128]{1,0:T(8,128)(2,1)}, bf16[1040,128]{1,0:T(8,128)(2,1)S(1)}, u32[]{:S(2)}, u32[]{:S(2)}) %collective-permute-start.1) | collective-permute-done | bytes 266272 | tf_op jit(solution)/shard_map/ppermute | solution.py:245
  21.4 2.6 %collective-permute-start.5 = (bf16[64,128]{1,0:T(8,128)(2,1)S(1)}, bf16[64,128]{1,0:T(8,128)(2,1)S(1)}, u32[]{:S(2)}, u32[]{:S(2)}) collective-permute-start(bf16[64,128]{1,0:T(8,128)(2,1)S(1)} %join.1.refs_4_), channel_id=1, source_target_pairs={{0,4},{1,5},{2,6},{3,7},{4,0},{5,1},{6,2},{7,3},{8,12},{9,13},{10,... | collective-permute-start | bytes 49160 | tf_op jit(solution)/shard_map/ppermute | solution.py:245
  24.0 0.0 collective-permute-done.2.refs_3_
  24.0 1.6 %collective-permute-start.4 = (bf16[64,128]{1,0:T(8,128)(2,1)S(1)}, bf16[64,128]{1,0:T(8,128)(2,1)S(1)}, u32[]{:S(2)}, u32[]{:S(2)}) collective-permute-start(bf16[64,128]{1,0:T(8,128)(2,1)S(1)} %join.1.refs_4_), channel_id=1, source_target_pairs={{0,2},{1,3},{2,0},{3,1},{4,6},{5,7},{6,4},{7,5},{8,10},{9,11},{10,... | collective-permute-start | bytes 49160 | tf_op jit(solution)/shard_map/ppermute | solution.py:245
  25.6 0.0 copy-start
  25.6 0.9 %copy-done = bf16[1040,128]{1,0:T(8,128)(2,1)S(1)} copy-done((bf16[1040,128]{1,0:T(8,128)(2,1)S(1)}, bf16[1040,128]{1,0:T(8,128)(2,1)}, u32[]{:S(2)}) %copy-start) | copy-done | bytes 266264
  26.6 0.0 copy-start.3
  26.6 0.7 %copy-done.3 = s32[2,4,4]{2,1,0:T(4,128)S(1)} copy-done((s32[2,4,4]{2,1,0:T(4,128)S(1)}, s32[2,4,4]{2,1,0:T(4,128)}, u32[]{:S(2)}) %copy-start.3) | copy-done | bytes 152
  27.3 0.0 copy-start.1
  27.3 2.3 %occ.1 = (bf16[512,256]{1,0:T(8,128)(2,1)S(1)}, bf16[128,8192]{1,0:T(8,128)(2,1)S(1)}) custom-call(s32[2,4,4]{2,1,0:T(4,128)S(1)} %copy-done.3, bf16[1040,128]{1,0:T(8,128)(2,1)S(1)} %copy-done, bf16[1040,128]{1,0:T(8,128)(2,1)S(1)} %collective-permute-done.refs_1_, bf16[1040,128]{1,0:T(8,128)(2,1)S(1)} %collective-permute-done.1.refs_2_, ...), custom_call_target="tpu_custom_call" | custom-call | tf_op jit(solution)/shard_map/occ/pallas_call | solution.py:278
  29.5 0.0 collective-permute-done.5.refs_6_
  29.5 0.0 collective-permute-done.4.refs_5_
  29.5 1.4 %vir.1 = (bf16[128,256]{1,0:T(8,128)(2,1)S(1)}, bf16[128,8192]{1,0:T(8,128)(2,1)S(1)}) custom-call(bf16[1040,128]{1,0:T(8,128)(2,1)S(1)} %copy-done, bf16[1040,128]{1,0:T(8,128)(2,1)S(1)} %collective-permute-done.refs_1_, bf16[1040,128]{1,0:T(8,128)(2,1)S(1)} %collective-permute-done.1.refs_2_, bf16[1040,128]{1,0:T(8,128)(2,1)S(1)} %collective-permute-done.2.refs_3_, ...), custom_call_target="tpu_custom_call" | custom-call | tf_op jit(solution)/shard_map/vir/pallas_call | solution.py:283
  30.9 0.0 collective-permute-done.7.refs_1_
  31.0 1.3 %collective-permute-done.8.refs_2_ = bf16[1024,128]{1,0:T(8,128)(2,1)S(1)} collective-permute-done((bf16[1024,128]{1,0:T(8,128)(2,1)}, bf16[1024,128]{1,0:T(8,128)(2,1)S(1)}, u32[]{:S(2)}, u32[]{:S(2)}) %collective-permute-start.8) | collective-permute-done | bytes 262176 | tf_op jit(solution)/shard_map/ppermute | solution.py:245
  32.3 0.0 collective-permute-done.9.refs_3_
  32.3 0.0 copy-done.4
  32.3 0.0 copy-done.1
  32.3 3.5 %last.1 = (f32[64,256]{1,0:T(8,128)S(1)}, f32[64,256]{1,0:T(8,128)S(1)}, f32[64,256]{1,0:T(8,128)S(1)}, f32[64,256]{1,0:T(8,128)S(1)}) custom-call(f32[2]{0:T(128)S(1)} %copy-done.4, bf16[512,256]{1,0:T(8,128)(2,1)S(1)} %get-tuple-element.25.refs_8_.mix_ref, bf16[128,256]{1,0:T(8,128)(2,1)S(1)} %get-tuple-element.26.virt_ref, ...), custom_call_target="tpu_custom_call" | custom-call | tf_op jit(solution)/shard_map/last/pallas_call | solution.py:288
  35.8 0.4 collective-permute-start.10
  36.2 1.7 %collective-permute-start.11 = (f32[64,256]{1,0:T(8,128)S(1)}, f32[64,256]{1,0:T(8,128)S(1)}, u32[]{:S(2)}, u32[]{:S(2)}) collective-permute-start(f32[64,256]{1,0:T(8,128)S(1)} %get-tuple-element.35), channel_id=1, source_target_pairs={{0,16},{8,24},{16,0},{24,8},{1,17},{9,25},{17,1},{25,9},{2,18},{10... | collective-permute-start | bytes 196616 | tf_op jit(solution)/shard_map/ppermute | solution.py:245
  37.9 1.4 %collective-permute-start.12 = (f32[64,256]{1,0:T(8,128)S(1)}, f32[64,256]{1,0:T(8,128)S(1)}, u32[]{:S(2)}, u32[]{:S(2)}) collective-permute-start(f32[64,256]{1,0:T(8,128)S(1)} %get-tuple-element.36), channel_id=1, source_target_pairs={{0,24},{8,16},{16,8},{24,0},{1,25},{9,17},{17,9},{25,1},{2,26},{10... | collective-permute-start | bytes 196616 | tf_op jit(solution)/shard_map/ppermute | solution.py:245
  39.4 1.5 %collective-permute-done.10 = f32[64,256]{1,0:T(8,128)S(1)} collective-permute-done((f32[64,256]{1,0:T(8,128)S(1)}, f32[64,256]{1,0:T(8,128)S(1)}, u32[]{:S(2)}, u32[]{:S(2)}) %collective-permute-start.10) | collective-permute-done | bytes 65568 | tf_op jit(solution)/shard_map/ppermute | solution.py:245
  40.8 0.0 collective-permute-done.11
  40.8 2.3 %collective-permute-done.12 = f32[64,256]{1,0:T(8,128)S(1)} collective-permute-done((f32[64,256]{1,0:T(8,128)S(1)}, f32[64,256]{1,0:T(8,128)S(1)}, u32[]{:S(2)}, u32[]{:S(2)}) %collective-permute-start.12) | collective-permute-done | bytes 65568 | tf_op jit(solution)/shard_map/ppermute | solution.py:245
  43.1 0.6 %add_add_fusion = f32[64,256]{1,0:T(8,128)} fusion(f32[64,256]{1,0:T(8,128)S(1)} %collective-permute-done.12, f32[64,256]{1,0:T(8,128)S(1)} %collective-permute-done.11, f32[64,256]{1,0:T(8,128)S(1)} %get-tuple-element.33, f32[64,256]{1,0:T(8,128)S(1)} %collective-permute-done.10), kind=kLoop, calls=%fused_computation | loop fusion | flops 49152 | bytes 327680 | tf_op jit(solution)/shard_map/add | solution.py:296
  (1 shorter events, 0.0 us)
Async XLA Ops:
  0.0 32.3 %copy-start.4 = (f32[2]{0:T(128)S(1)}, f32[2]{0:T(128)}, u32[]{:S(2)}) copy-start(f32[2]{0:T(128)} %tau_ref.1) | copy-start | bytes 28
  3.3 12.8 %collective-permute-start = (bf16[1040,128]{1,0:T(8,128)(2,1)}, bf16[1040,128]{1,0:T(8,128)(2,1)S(1)}, u32[]{:S(2)}, u32[]{:S(2)}) collective-permute-start(bf16[1040,128]{1,0:T(8,128)(2,1)} %get-tuple-element.22), channel_id=1, source_target_pairs={{0,8},{8,0},{16,24},{24,16},{1,9},{9,1},{17,25},{25,17},{2,10},{10... | collective-permute-start | bytes 798728 | tf_op jit(solution)/shard_map/ppermute | solution.py:245
  6.3 1.6 %collective-permute-start.3 = (bf16[32,128]{1,0:T(8,128)(2,1)}, bf16[32,128]{1,0:T(8,128)(2,1)S(1)}, u32[]{:S(2)}, u32[]{:S(2)}) collective-permute-start(bf16[32,128]{1,0:T(8,128)(2,1)} %bitcast.3), channel_id=1, source_target_pairs={{0,1},{1,0},{2,3},{3,2},{4,5},{5,4},{6,7},{7,6},{8,9},{9,8},{10,11... | collective-permute-start | bytes 24584 | tf_op jit(solution)/shard_map/ppermute | solution.py:245
  6.3 15.1 %collective-permute-start.1 = (bf16[1040,128]{1,0:T(8,128)(2,1)}, bf16[1040,128]{1,0:T(8,128)(2,1)S(1)}, u32[]{:S(2)}, u32[]{:S(2)}) collective-permute-start(bf16[1040,128]{1,0:T(8,128)(2,1)} %get-tuple-element.23), channel_id=1, source_target_pairs={{0,16},{8,24},{16,0},{24,8},{1,17},{9,25},{17,1},{25,9},{2,18},{10... | collective-permute-start | bytes 798728 | tf_op jit(solution)/shard_map/ppermute | solution.py:245
  7.9 16.2 %collective-permute-start.2 = (bf16[1040,128]{1,0:T(8,128)(2,1)}, bf16[1040,128]{1,0:T(8,128)(2,1)S(1)}, u32[]{:S(2)}, u32[]{:S(2)}) collective-permute-start(bf16[1040,128]{1,0:T(8,128)(2,1)} %get-tuple-element.24), channel_id=1, source_target_pairs={{0,24},{8,16},{16,8},{24,0},{1,25},{9,17},{17,9},{25,1},{2,26},{10... | collective-permute-start | bytes 798728 | tf_op jit(solution)/shard_map/ppermute | solution.py:245
  8.0 0.7 %copy-start.2 = (bf16[2,1,16,128]{3,2,1,0:T(8,128)(2,1)S(1)}, bf16[2,1,16,128]{3,2,1,0:T(8,128)(2,1)}, u32[]{:S(2)}) copy-start(bf16[2,1,16,128]{3,2,1,0:T(8,128)(2,1)} %param.10) | copy-start | bytes 24580
  8.7 5.7 %collective-permute-start.6 = (bf16[64,128]{1,0:T(8,128)(2,1)S(1)}, bf16[64,128]{1,0:T(8,128)(2,1)S(1)}, u32[]{:S(2)}, u32[]{:S(2)}) collective-permute-start(bf16[64,128]{1,0:T(8,128)(2,1)S(1)} %join.1.refs_4_), channel_id=1, source_target_pairs={{0,6},{1,7},{2,4},{3,5},{4,2},{5,3},{6,0},{7,1},{8,14},{9,15},{10,... | collective-permute-start | bytes 49160 | tf_op jit(solution)/shard_map/ppermute | solution.py:245
  12.6 18.3 %collective-permute-start.7 = (bf16[1024,128]{1,0:T(8,128)(2,1)}, bf16[1024,128]{1,0:T(8,128)(2,1)S(1)}, u32[]{:S(2)}, u32[]{:S(2)}) collective-permute-start(bf16[1024,128]{1,0:T(8,128)(2,1)} %get-tuple-element.30), channel_id=1, source_target_pairs={{0,8},{8,0},{16,24},{24,16},{1,9},{9,1},{17,25},{25,17},{2,10},{10... | collective-permute-start | bytes 786440 | tf_op jit(solution)/shard_map/ppermute | solution.py:245
  14.4 17.9 %collective-permute-start.8 = (bf16[1024,128]{1,0:T(8,128)(2,1)}, bf16[1024,128]{1,0:T(8,128)(2,1)S(1)}, u32[]{:S(2)}, u32[]{:S(2)}) collective-permute-start(bf16[1024,128]{1,0:T(8,128)(2,1)} %get-tuple-element.31), channel_id=1, source_target_pairs={{0,16},{8,24},{16,0},{24,8},{1,17},{9,25},{17,1},{25,9},{2,18},{10... | collective-permute-start | bytes 786440 | tf_op jit(solution)/shard_map/ppermute | solution.py:245
  16.1 16.2 %collective-permute-start.9 = (bf16[1024,128]{1,0:T(8,128)(2,1)}, bf16[1024,128]{1,0:T(8,128)(2,1)S(1)}, u32[]{:S(2)}, u32[]{:S(2)}) collective-permute-start(bf16[1024,128]{1,0:T(8,128)(2,1)} %get-tuple-element.32), channel_id=1, source_target_pairs={{0,24},{8,16},{16,8},{24,0},{1,25},{9,17},{17,9},{25,1},{2,26},{10... | collective-permute-start | bytes 786440 | tf_op jit(solution)/shard_map/ppermute | solution.py:245
  21.4 8.1 %collective-permute-start.5 = (bf16[64,128]{1,0:T(8,128)(2,1)S(1)}, bf16[64,128]{1,0:T(8,128)(2,1)S(1)}, u32[]{:S(2)}, u32[]{:S(2)}) collective-permute-start(bf16[64,128]{1,0:T(8,128)(2,1)S(1)} %join.1.refs_4_), channel_id=1, source_target_pairs={{0,4},{1,5},{2,6},{3,7},{4,0},{5,1},{6,2},{7,3},{8,12},{9,13},{10,... | collective-permute-start | bytes 49160 | tf_op jit(solution)/shard_map/ppermute | solution.py:245
  24.0 5.5 %collective-permute-start.4 = (bf16[64,128]{1,0:T(8,128)(2,1)S(1)}, bf16[64,128]{1,0:T(8,128)(2,1)S(1)}, u32[]{:S(2)}, u32[]{:S(2)}) collective-permute-start(bf16[64,128]{1,0:T(8,128)(2,1)S(1)} %join.1.refs_4_), channel_id=1, source_target_pairs={{0,2},{1,3},{2,0},{3,1},{4,6},{5,7},{6,4},{7,5},{8,10},{9,11},{10,... | collective-permute-start | bytes 49160 | tf_op jit(solution)/shard_map/ppermute | solution.py:245
  25.6 1.0 %copy-start = (bf16[1040,128]{1,0:T(8,128)(2,1)S(1)}, bf16[1040,128]{1,0:T(8,128)(2,1)}, u32[]{:S(2)}) copy-start(bf16[1040,128]{1,0:T(8,128)(2,1)} %get-tuple-element.21.refs_0_) | copy-start | bytes 798724
  26.6 0.7 %copy-start.3 = (s32[2,4,4]{2,1,0:T(4,128)S(1)}, s32[2,4,4]{2,1,0:T(4,128)}, u32[]{:S(2)}) copy-start(s32[2,4,4]{2,1,0:T(4,128)} %live_ref.1) | copy-start | bytes 388
  27.3 5.1 %copy-start.1 = (bf16[1024,128]{1,0:T(8,128)(2,1)S(1)}, bf16[1024,128]{1,0:T(8,128)(2,1)}, u32[]{:S(2)}) copy-start(bf16[1024,128]{1,0:T(8,128)(2,1)} %get-tuple-element.29.refs_0_) | copy-start | bytes 786436
  35.8 5.0 %collective-permute-start.10 = (f32[64,256]{1,0:T(8,128)S(1)}, f32[64,256]{1,0:T(8,128)S(1)}, u32[]{:S(2)}, u32[]{:S(2)}) collective-permute-start(f32[64,256]{1,0:T(8,128)S(1)} %get-tuple-element.34), channel_id=1, source_target_pairs={{0,8},{8,0},{16,24},{24,16},{1,9},{9,1},{17,25},{25,17},{2,10},{10... | collective-permute-start | bytes 196616 | tf_op jit(solution)/shard_map/ppermute | solution.py:245
  36.2 4.6 %collective-permute-start.11 = (f32[64,256]{1,0:T(8,128)S(1)}, f32[64,256]{1,0:T(8,128)S(1)}, u32[]{:S(2)}, u32[]{:S(2)}) collective-permute-start(f32[64,256]{1,0:T(8,128)S(1)} %get-tuple-element.35), channel_id=1, source_target_pairs={{0,16},{8,24},{16,0},{24,8},{1,17},{9,25},{17,1},{25,9},{2,18},{10... | collective-permute-start | bytes 196616 | tf_op jit(solution)/shard_map/ppermute | solution.py:245
  37.9 5.2 %collective-permute-start.12 = (f32[64,256]{1,0:T(8,128)S(1)}, f32[64,256]{1,0:T(8,128)S(1)}, u32[]{:S(2)}, u32[]{:S(2)}) collective-permute-start(f32[64,256]{1,0:T(8,128)S(1)} %get-tuple-element.36), channel_id=1, source_target_pairs={{0,24},{8,16},{16,8},{24,0},{1,25},{9,17},{17,9},{25,1},{2,26},{10... | collective-permute-start | bytes 196616 | tf_op jit(solution)/shard_map/ppermute | solution.py:245

commit v3 on v2

--- a/solution.py
+++ b/solution.py
@@ -20,6 +20,17 @@
 
 def dot(a, b):
     return jnp.dot(a, b, preferred_element_type=F32)
+
+
+def partners(count):
+    return [0] + sorted(range(1, count), key=lambda distance: (-distance.bit_count(), distance))
+
+
+def pick_static(index, values):
+    found = jnp.zeros_like(index)
+    for place, value in enumerate(values):
+        found = jnp.where(index == place, value, found)
+    return found
 
 
 def pack_kernel(rows_dev, slot_count, chunks, pieces, col_hbm, b_hbm, occ_hbm, *refs):
@@ -66,7 +77,7 @@
         moved = dot(pick, b_ref[pl.ds(at, in_rows), :]).astype(BF16)
         slots = [moved[slot * out_rows : (slot + 1) * out_rows] for slot in range(slot_count)]
         zero = jnp.zeros_like(slots[0])
-        for distance, held in enumerate(group):
+        for distance, held in zip(partners(orb_count), group):
             value = zero
             for slot in range(slot_count):
                 value = jnp.where(col_ref[0, slot] == me ^ distance, slots[slot], value)
@@ -87,13 +98,41 @@
             top = low - start + piece_steps
             low_row = (low - start) * out_rows
             high_row = helds[group[0]].shape[0] if top == chunk else top * out_rows
-            for distance, at in enumerate(group):
+            for place, at in enumerate(group):
                 here = pl.ds(low_row, high_row - low_row)
-                copy = pltpu.make_async_copy(helds[at].at[here], outs[at].at[here], out_sem.at[piece, distance])
+                copy = pltpu.make_async_copy(helds[at].at[here], outs[at].at[here], out_sem.at[piece, place])
                 copy.start()
                 sent.append(copy)
         start += chunk
     for copy in sent:
+        copy.wait()
+
+
+def stage_kernel(orb_count, own_count, live_hbm, one_ref, two_ref, *refs):
+    owns, outs = refs[:own_count], refs[own_count : 2 * own_count]
+    live_out, join_out, live_ref, live_sem, own_sem = refs[2 * own_count :]
+    live_copy = pltpu.make_async_copy(live_hbm, live_ref, live_sem)
+    live_copy.start()
+    copies = [pltpu.make_async_copy(own, out, own_sem.at[at]) for at, (own, out) in enumerate(zip(owns, outs))]
+    for copy in copies:
+        copy.start()
+    join_out[: one_ref.shape[0], :] = one_ref[...]
+    join_out[one_ref.shape[0] :, :] = two_ref[...]
+    live_copy.wait()
+    me = lax.axis_index("orb")
+    order = partners(orb_count)
+    tau_count = live_ref.shape[0]
+    width = live_out.shape[1]
+    group_of = iota((1, width), 1) // (width // orb_count)
+    for moment in range(tau_count):
+        for row_group in range(orb_count):
+            live = jnp.zeros((1, width), jnp.int32)
+            for col_group in range(orb_count):
+                value = live_ref[moment, me ^ order[row_group], me ^ order[col_group]]
+                live = jnp.where(group_of == col_group, value, live)
+            at = moment * orb_count + row_group
+            live_out[at : at + 1, :] = live
+    for copy in copies:
         copy.wait()
 
 
@@ -131,20 +170,15 @@
     left = jnp.where(iota(left_shape, 1) == wanted, 1.0, 0.0).astype(BF16)
     right_shape = (tile, rows * SUB)
     col_of = iota(right_shape, 1) // SUB
-    wanted = ((col_of // rows_dev) ^ me) * rows_dev + col_of % rows_dev
+    group = pick_static(col_of // rows_dev, partners(orb_count)) ^ me
+    wanted = group * rows_dev + col_of % rows_dev
     right = jnp.where(iota(right_shape, 0) == wanted, 1.0, 0.0).astype(BF16)
     spread = dot(dot(left, occ_all).astype(BF16), right)
     same = iota((half_rows, rows * SUB), 0) % SUB == iota((half_rows, rows * SUB), 1) % SUB
-    group_of = iota((1, rows * SUB), 1) // half_rows
-    for moment in range(tau_count):
-        for row_group in range(orb_count):
-            live = jnp.zeros((1, rows * SUB), jnp.int32)
-            for col_group in range(orb_count):
-                value = live_ref[moment, me ^ row_group, me ^ col_group]
-                live = jnp.where(group_of == col_group, value, live)
-            at = (moment * orb_count + row_group) * half_rows
-            keep = jnp.logical_and(same, live != 0)
-            mix_out[at : at + half_rows, :] = jnp.where(keep, spread[at : at + half_rows], 0.0).astype(BF16)
+    for at in range(tau_count * orb_count):
+        here = slice(at * half_rows, (at + 1) * half_rows)
+        keep = jnp.logical_and(same, live_ref[at : at + 1, :] != 0)
+        mix_out[here, :] = jnp.where(keep, spread[here], 0.0).astype(BF16)
 
 
 def products(sizes, steps, blocks, mix_ref, virt_ref, occ_out, vir_out):
@@ -211,7 +245,7 @@
             ) * tau_ref[moment]
             chi = term if chi is None else chi + term
     chi = chi * (1.0 / math.sqrt(rows * tile * orb_count))
-    for distance, out in enumerate(outs):
+    for distance, out in zip(partners(orb_count), outs):
         picked = chi[0:share_rows]
         for owner in range(1, orb_count):
             picked = jnp.where(me ^ distance == owner, chi[owner * share_rows : (owner + 1) * share_rows], picked)
@@ -248,7 +282,7 @@
         return jax.ShapeDtypeStruct(value, BF16)
 
     all_steps = aux_dev // PAIR
-    chunks = (all_steps // 2, all_steps - all_steps // 2)
+    chunks = (all_steps * 12 // 16, all_steps - all_steps * 12 // 16)
     occ_rows = tau_count * rows_dev
     b_flat = b_rows.reshape(-1, tile)
     occ_flat = g_occ.reshape(occ_rows, -1)
@@ -267,19 +301,34 @@
             pltpu.SemaphoreType.DMA((pieces, orb_count)),
         ], 54, hbm,
     )(col_blocks, b_flat, occ_flat)
+    order = partners(orb_count)
     dense = []
     for number in range(len(chunks)):
         own, *others = blocks[number * orb_count : (number + 1) * orb_count]
-        dense.append([own] + [xor(value, "orb", d + 1) for d, value in enumerate(others)])
+        dense.append([own] + [xor(value, "orb", d) for d, value in zip(order[1:], others)])
     virt = g_virt.reshape(-1, tile)
-    virt = call(join_kernel, "join", [half((2 * virt.shape[0], tile))], [vmem] * 2, [], 2)(virt, xor(virt, "aux", 1))[0]
-    virts = [virt] + [xor(virt, "aux", d) for d in range(2, aux_count, 2)]
+    owns = [blocks[number * orb_count] for number in range(len(chunks))]
+    *owns, live, virt = call(
+        functools.partial(stage_kernel, orb_count, len(chunks)), "stage",
+        [half(own.shape) for own in owns]
+        + [jax.ShapeDtypeStruct((tau_count * orb_count, rows * SUB), jnp.int32), half((2 * virt.shape[0], tile))],
+        [hbm, vmem, vmem] + [hbm] * len(owns),
+        [pltpu.SMEM(occ_live.shape, jnp.int32), pltpu.SemaphoreType.DMA, pltpu.SemaphoreType.DMA((len(owns),))], 4,
+    )(occ_live, virt, xor(virt, "aux", 1), *owns)
+    for own, group in zip(owns, dense):
+        group[0] = own
+    distance = 2
+    while distance < aux_count:
+        pair = half((2 * virt.shape[0], tile))
+        virt = call(join_kernel, "join", [pair], [vmem] * 2, [], 2)(virt, xor(virt, "aux", distance))[0]
+        distance *= 2
+    virts = [virt]
     wide = half((chunks[0] * PAIR, tau_count * rows * tile))
     mix, occ_first = call(
         functools.partial(occ_kernel, sizes, chunks[0]), "occ",
         [half((tau_count * rows * SUB, rows * SUB)), wide],
-        [smem] + [vmem] * orb_count, [], 8,
-    )(occ_live, *dense[0])
+        [vmem] * (1 + orb_count), [], 8,
+    )(live, *dense[0])
     virt, vir_first = call(
         functools.partial(vir_kernel, sizes, chunks[0]), "vir",
         [half((tile, tau_count * tile)), wide],
@@ -292,8 +341,8 @@
         [pltpu.VMEM((chunks[1] * PAIR, tau_count * rows * tile), BF16)] * 2, 12,
     )(tau_weight, mix, virt, occ_first, vir_first, *dense[1])
     total = shares[0]
-    for distance in range(1, orb_count):
-        total = total + xor(shares[distance], "orb", distance)
+    for distance, share in zip(order[1:], shares[1:]):
+        total = total + xor(share, "orb", distance)
     return total
 
 

time: 44 us -> 41.9 us (0.952)
  starting transfers between devices: 21 us -> 18.4 us
  waiting for transfers between devices: 9.22 us -> 8.27 us
  local copies, waits for them, and re-layouts: 2.34 us -> 3.29 us
  Pallas kernels: 10.5 us -> 11 us
    ppermute x13 -> x12, starting transfers between devices: 21 us -> 18.4 us  [xor(): lax.ppermute(value, axis, [(i, i ^ distance) for i in range(lax.axis_size...]
    unnamed x10, local copies, waits for them, and re-layouts: 2.34 us -> 3.29 us
    ppermute x13 -> x12, waiting for transfers between devices: 9.22 us -> 8.27 us  [xor(): lax.ppermute(value, axis, [(i, i ^ distance) for i in range(lax.axis_size...]
    pallas_call x1, Pallas kernels: 3.51 us -> 2.66 us  [on_device(): call(functools.partial(last_kernel, sizes, chunks[1], share_rows), 'last'...]
    pallas_call x1 -> x3, Pallas kernels: 0.01 us -> 0.69 us  [the longest x1 0.68 us: on_device(): call(functools.partial(stage_kernel, orb_count, len(chunks)), 'stage', [h...]
    pallas_call x1, Pallas kernels: 1.39 us -> 1.97 us  [on_device(): call(functools.partial(vir_kernel, sizes, chunks[0]), 'vir', [half((tile,...]
  transfers between devices with their start and end apart: 13 -> 12, of which waited for: 5 -> 7; matrix products, arithmetic and copies ran while one was open for 0% -> 0% of each run, Pallas kernels for 8% -> 12%
where the time goes in v3:
time: 41.9 us; the launch traced here: 41.7 us
  starting transfers between devices  18.4 us (44%)
  Pallas kernels  11 us (26%)
  waiting for transfers between devices  8.27 us (20%)
  local copies, waits for them, and re-layouts  3.29 us (8%)
  other arithmetic  0.65 us (2%)
    ppermute x12, starting transfers between devices, xor(): lax.ppermute(value, axis, [(i, i ^ distance) for i in range(lax.axis_size...  18.4 us
    ppermute x12, waiting for transfers between devices, xor(): lax.ppermute(value, axis, [(i, i ^ distance) for i in range(lax.axis_size...  8.27 us
    pallas_call x1, Pallas kernels, on_device(): call(functools.partial(pack_kernel, rows_dev, slot_count, chunks, pieces)...  3.31 us
    unnamed x10, local copies, waits for them, and re-layouts  3.29 us
    pallas_call x1, Pallas kernels, on_device(): call(functools.partial(last_kernel, sizes, chunks[1], share_rows), 'last'...  2.66 us
    pallas_call x1, Pallas kernels, on_device(): call(functools.partial(occ_kernel, sizes, chunks[0]), 'occ', [half((tau_c...  2.33 us
    pallas_call x1, Pallas kernels, on_device(): call(functools.partial(vir_kernel, sizes, chunks[0]), 'vir', [half((tile,...  1.97 us
  transfers between devices with their start and end apart: 12, of which 7 were waited for; matrix products, arithmetic and copies ran while one was open for 0% of the time, Pallas kernels for 12%

profile of v3, /device:TPU:0, one launch (start us, length us, event | category | flops | bytes accessed | tf_op | source)
XLA Modules:
  0.0 41.7 jit_solution(3638207819054355802)
XLA Ops:
  0.0 0.0 copy-start.4
  0.0 3.3 %pack.1 = (bf16[1552,128]{1,0:T(8,128)(2,1)}, bf16[1552,128]{1,0:T(8,128)(2,1)}, bf16[1552,128]{1,0:T(8,128)(2,1)}, bf16[1552,128]{1,0:T(8,128)(2,1)}, bf16[512,...) custom-call(s32[1,2]{1,0:T(1,128)} %col_hbm.1, ...), custom_call_target="tpu_custom_call" | custom-call | tf_op jit(solution)/shard_map/pack/pallas_call | solution.py:295
  3.3 4.0 %collective-permute-start.1 = (bf16[1552,128]{1,0:T(8,128)(2,1)}, bf16[1552,128]{1,0:T(8,128)(2,1)S(1)}, u32[]{:S(2)}, u32[]{:S(2)}) collective-permute-start(bf16[1552,128]{1,0:T(8,128)(2,1)} %get-tuple-element.29), channel_id=1, source_target_pairs={{0,24},{8,16},{16,8},{24,0},{1,25},{9,17},{17,9},{25,1},{2,26},{10... | collective-permute-start | bytes 1191944 | tf_op jit(solution)/shard_map/ppermute | solution.py:279
  7.3 0.5 %collective-permute-start.2 = (bf16[1552,128]{1,0:T(8,128)(2,1)}, bf16[1552,128]{1,0:T(8,128)(2,1)S(1)}, u32[]{:S(2)}, u32[]{:S(2)}) collective-permute-start(bf16[1552,128]{1,0:T(8,128)(2,1)} %get-tuple-element.30), channel_id=1, source_target_pairs={{0,8},{8,0},{16,24},{24,16},{1,9},{9,1},{17,25},{25,17},{2,10},{10... | collective-permute-start | bytes 1191944 | tf_op jit(solution)/shard_map/ppermute | solution.py:279
  7.8 0.1 collective-permute-start.3
  7.9 0.0 collective-permute-start
  7.9 1.4 %collective-permute-done.two_ref = bf16[32,128]{1,0:T(8,128)(2,1)S(1)} collective-permute-done((bf16[32,128]{1,0:T(8,128)(2,1)}, bf16[32,128]{1,0:T(8,128)(2,1)S(1)}, u32[]{:S(2)}, u32[]{:S(2)}) %collective-permute-start) | collective-permute-done | bytes 8224 | tf_op jit(solution)/shard_map/ppermute | solution.py:279
  9.3 0.0 copy-start
  9.3 1.0 %copy-done = bf16[1552,128]{1,0:T(8,128)(2,1)S(1)} copy-done((bf16[1552,128]{1,0:T(8,128)(2,1)S(1)}, bf16[1552,128]{1,0:T(8,128)(2,1)}, u32[]{:S(2)}) %copy-start) | copy-done | bytes 397336
  10.3 0.0 copy-start.1
  10.3 0.9 %copy-done.1 = bf16[512,128]{1,0:T(8,128)(2,1)S(1)} copy-done((bf16[512,128]{1,0:T(8,128)(2,1)S(1)}, bf16[512,128]{1,0:T(8,128)(2,1)}, u32[]{:S(2)}) %copy-start.1) | copy-done | bytes 131096
  11.2 0.0 copy-start.2
  11.2 0.7 %copy-done.2 = bf16[2,1,16,128]{3,2,1,0:T(8,128)(2,1)S(1)} copy-done((bf16[2,1,16,128]{3,2,1,0:T(8,128)(2,1)S(1)}, bf16[2,1,16,128]{3,2,1,0:T(8,128)(2,1)}, u32[]{:S(2)}) %copy-start.2) | copy-done | bytes 8216
  11.9 0.0 copy-start.3
  11.9 0.7 %copy-done.3 = s32[2,4,4]{2,1,0:T(4,128)S(1)} copy-done((s32[2,4,4]{2,1,0:T(4,128)S(1)}, s32[2,4,4]{2,1,0:T(4,128)}, u32[]{:S(2)}) %copy-start.3) | copy-done | bytes 152
  12.6 0.7 %stage.1 = (bf16[1552,128]{1,0:T(8,128)(2,1)S(1)}, bf16[512,128]{1,0:T(8,128)(2,1)S(1)}, s32[8,256]{1,0:T(8,128)S(1)}, bf16[64,128]{1,0:T(8,128)(2,1)S(1)}) custom-call(s32[2,4,4]{2,1,0:T(4,128)S(1)} %copy-done.3, bf16[32,128]{1,0:T(8,128)(2,1)S(1)} %bitcast.4, bf16[32,128]{1,0:T(8,128)(2,1)S(1)} %collective-permute-done.two_ref, ...), custom_call_target="tpu_custom_call" | custom-call | tf_op jit(solution)/shard_map/stage/pallas_call | solution.py:311
  13.3 2.0 %collective-permute-start.4 = (bf16[64,128]{1,0:T(8,128)(2,1)S(1)}, bf16[64,128]{1,0:T(8,128)(2,1)S(1)}, u32[]{:S(2)}, u32[]{:S(2)}) collective-permute-start(bf16[64,128]{1,0:T(8,128)(2,1)S(1)} %get-tuple-element.33.one_ref), channel_id=1, source_target_pairs={{0,2},{1,3},{2,0},{3,1},{4,6},{5,7},{6,4},{7,5},{8,10},{9,11},{10,... | collective-permute-start | bytes 49160 | tf_op jit(solution)/shard_map/ppermute | solution.py:279
  15.3 1.8 %collective-permute-done.4.two_ref = bf16[64,128]{1,0:T(8,128)(2,1)S(1)} collective-permute-done((bf16[64,128]{1,0:T(8,128)(2,1)S(1)}, bf16[64,128]{1,0:T(8,128)(2,1)S(1)}, u32[]{:S(2)}, u32[]{:S(2)}) %collective-permute-start.4) | collective-permute-done | bytes 16416 | tf_op jit(solution)/shard_map/ppermute | solution.py:279
  17.1 3.0 %collective-permute-start.5 = (bf16[128,128]{1,0:T(8,128)(2,1)S(1)}, bf16[128,128]{1,0:T(8,128)(2,1)S(1)}, u32[]{:S(2)}, u32[]{:S(2)}) collective-permute-start(bf16[128,128]{1,0:T(8,128)(2,1)S(1)} %join.2.one_ref), channel_id=1, source_target_pairs={{0,4},{1,5},{2,6},{3,7},{4,0},{5,1},{6,2},{7,3},{8,12},{9,13},{10,... | collective-permute-start | bytes 98312 | tf_op jit(solution)/shard_map/ppermute | solution.py:279
  20.1 2.4 %collective-permute-start.6 = (bf16[512,128]{1,0:T(8,128)(2,1)}, bf16[512,128]{1,0:T(8,128)(2,1)S(1)}, u32[]{:S(2)}, u32[]{:S(2)}) collective-permute-start(bf16[512,128]{1,0:T(8,128)(2,1)} %get-tuple-element.38), channel_id=1, source_target_pairs={{0,24},{8,16},{16,8},{24,0},{1,25},{9,17},{17,9},{25,1},{2,26},{10... | collective-permute-start | bytes 393224 | tf_op jit(solution)/shard_map/ppermute | solution.py:279
  22.5 0.0 collective-permute-done.5.two_ref
  22.5 1.3 %collective-permute-start.7 = (bf16[512,128]{1,0:T(8,128)(2,1)}, bf16[512,128]{1,0:T(8,128)(2,1)S(1)}, u32[]{:S(2)}, u32[]{:S(2)}) collective-permute-start(bf16[512,128]{1,0:T(8,128)(2,1)} %get-tuple-element.39), channel_id=1, source_target_pairs={{0,8},{8,0},{16,24},{24,16},{1,9},{9,1},{17,25},{25,17},{2,10},{10... | collective-permute-start | bytes 393224 | tf_op jit(solution)/shard_map/ppermute | solution.py:279
  23.8 0.0 collective-permute-done.1.refs_1_
  23.8 1.5 %collective-permute-start.8 = (bf16[512,128]{1,0:T(8,128)(2,1)}, bf16[512,128]{1,0:T(8,128)(2,1)S(1)}, u32[]{:S(2)}, u32[]{:S(2)}) collective-permute-start(bf16[512,128]{1,0:T(8,128)(2,1)} %get-tuple-element.40), channel_id=1, source_target_pairs={{0,16},{8,24},{16,0},{24,8},{1,17},{9,25},{17,1},{25,9},{2,18},{10... | collective-permute-start | bytes 393224 | tf_op jit(solution)/shard_map/ppermute | solution.py:279
  25.3 1.3 %collective-permute-done.2.refs_2_ = bf16[1552,128]{1,0:T(8,128)(2,1)S(1)} collective-permute-done((bf16[1552,128]{1,0:T(8,128)(2,1)}, bf16[1552,128]{1,0:T(8,128)(2,1)S(1)}, u32[]{:S(2)}, u32[]{:S(2)}) %collective-permute-start.2) | collective-permute-done | bytes 397344 | tf_op jit(solution)/shard_map/ppermute | solution.py:279
  26.6 0.0 collective-permute-done.3.refs_3_
  26.7 2.3 %occ.1 = (bf16[512,256]{1,0:T(8,128)(2,1)S(1)}, bf16[192,8192]{1,0:T(8,128)(2,1)S(1)}) custom-call(s32[8,256]{1,0:T(8,128)S(1)} %get-tuple-element.27.live_ref, bf16[1552,128]{1,0:T(8,128)(2,1)S(1)} %get-tuple-element.28.refs_0_, bf16[1552,128]{1,0:T(8,128)(2,1)S(1)} %collective-permute-done.1.refs_1_, bf16[1552,128]{1,0:T(8,128)(2,1)S(1)} %collective-permute-done.2.refs_2_, ...), custom_call_target="tpu_custom_call" | custom-call | tf_op jit(solution)/shard_map/occ/pallas_call | solution.py:327
  29.0 2.0 %vir.1 = (bf16[128,256]{1,0:T(8,128)(2,1)S(1)}, bf16[192,8192]{1,0:T(8,128)(2,1)S(1)}) custom-call(bf16[1552,128]{1,0:T(8,128)(2,1)S(1)} %get-tuple-element.28.refs_0_, bf16[1552,128]{1,0:T(8,128)(2,1)S(1)} %collective-permute-done.1.refs_1_, bf16[1552,128]{1,0:T(8,128)(2,1)S(1)} %collective-permute-done.2.refs_2_, ...), custom_call_target="tpu_custom_call" | custom-call | tf_op jit(solution)/shard_map/vir/pallas_call | solution.py:332
  31.0 0.0 collective-permute-done.6.refs_1_
  31.0 0.1 collective-permute-done.7.refs_2_
  31.1 0.0 collective-permute-done.8.refs_3_
  31.1 0.0 copy-done.4
  31.1 2.7 %last.1 = (f32[64,256]{1,0:T(8,128)S(1)}, f32[64,256]{1,0:T(8,128)S(1)}, f32[64,256]{1,0:T(8,128)S(1)}, f32[64,256]{1,0:T(8,128)S(1)}) custom-call(f32[2]{0:T(128)S(1)} %copy-done.4, bf16[512,256]{1,0:T(8,128)(2,1)S(1)} %get-tuple-element.32.refs_5_.mix_ref, bf16[128,256]{1,0:T(8,128)(2,1)S(1)} %get-tuple-element.34.virt_ref, ...), custom_call_target="tpu_custom_call" | custom-call | tf_op jit(solution)/shard_map/last/pallas_call | solution.py:337
  33.8 2.4 %collective-permute-start.9 = (f32[64,256]{1,0:T(8,128)S(1)}, f32[64,256]{1,0:T(8,128)S(1)}, u32[]{:S(2)}, u32[]{:S(2)}) collective-permute-start(f32[64,256]{1,0:T(8,128)S(1)} %get-tuple-element.42), channel_id=1, source_target_pairs={{0,24},{8,16},{16,8},{24,0},{1,25},{9,17},{17,9},{25,1},{2,26},{10... | collective-permute-start | bytes 196616 | tf_op jit(solution)/shard_map/ppermute | solution.py:279
  36.2 0.5 %collective-permute-start.10 = (f32[64,256]{1,0:T(8,128)S(1)}, f32[64,256]{1,0:T(8,128)S(1)}, u32[]{:S(2)}, u32[]{:S(2)}) collective-permute-start(f32[64,256]{1,0:T(8,128)S(1)} %get-tuple-element.43), channel_id=1, source_target_pairs={{0,8},{8,0},{16,24},{24,16},{1,9},{9,1},{17,25},{25,17},{2,10},{10... | collective-permute-start | bytes 196616 | tf_op jit(solution)/shard_map/ppermute | solution.py:279
  36.7 0.6 %collective-permute-start.11 = (f32[64,256]{1,0:T(8,128)S(1)}, f32[64,256]{1,0:T(8,128)S(1)}, u32[]{:S(2)}, u32[]{:S(2)}) collective-permute-start(f32[64,256]{1,0:T(8,128)S(1)} %get-tuple-element.44), channel_id=1, source_target_pairs={{0,16},{8,24},{16,0},{24,8},{1,17},{9,25},{17,1},{25,9},{2,18},{10... | collective-permute-start | bytes 196616 | tf_op jit(solution)/shard_map/ppermute | solution.py:279
  37.3 2.3 %collective-permute-done.9 = f32[64,256]{1,0:T(8,128)S(1)} collective-permute-done((f32[64,256]{1,0:T(8,128)S(1)}, f32[64,256]{1,0:T(8,128)S(1)}, u32[]{:S(2)}, u32[]{:S(2)}) %collective-permute-start.9) | collective-permute-done | bytes 65568 | tf_op jit(solution)/shard_map/ppermute | solution.py:279
  39.7 0.8 %collective-permute-done.10 = f32[64,256]{1,0:T(8,128)S(1)} collective-permute-done((f32[64,256]{1,0:T(8,128)S(1)}, f32[64,256]{1,0:T(8,128)S(1)}, u32[]{:S(2)}, u32[]{:S(2)}) %collective-permute-start.10) | collective-permute-done | bytes 65568 | tf_op jit(solution)/shard_map/ppermute | solution.py:279
  40.5 0.5 %collective-permute-done.11 = f32[64,256]{1,0:T(8,128)S(1)} collective-permute-done((f32[64,256]{1,0:T(8,128)S(1)}, f32[64,256]{1,0:T(8,128)S(1)}, u32[]{:S(2)}, u32[]{:S(2)}) %collective-permute-start.11) | collective-permute-done | bytes 65568 | tf_op jit(solution)/shard_map/ppermute | solution.py:279
  41.0 0.6 %add_add_fusion = f32[64,256]{1,0:T(8,128)} fusion(f32[64,256]{1,0:T(8,128)S(1)} %collective-permute-done.11, f32[64,256]{1,0:T(8,128)S(1)} %collective-permute-done.10, f32[64,256]{1,0:T(8,128)S(1)} %get-tuple-element.41, f32[64,256]{1,0:T(8,128)S(1)} %collective-permute-done.9), kind=kLoop, calls=%fused_computation | loop fusion | flops 49152 | bytes 327680 | tf_op jit(solution)/shard_map/add | solution.py:345
  (2 shorter events, 0.0 us)
Async XLA Ops:
  0.0 31.1 %copy-start.4 = (f32[2]{0:T(128)S(1)}, f32[2]{0:T(128)}, u32[]{:S(2)}) copy-start(f32[2]{0:T(128)} %tau_ref.1) | copy-start | bytes 28
  3.3 20.5 %collective-permute-start.1 = (bf16[1552,128]{1,0:T(8,128)(2,1)}, bf16[1552,128]{1,0:T(8,128)(2,1)S(1)}, u32[]{:S(2)}, u32[]{:S(2)}) collective-permute-start(bf16[1552,128]{1,0:T(8,128)(2,1)} %get-tuple-element.29), channel_id=1, source_target_pairs={{0,24},{8,16},{16,8},{24,0},{1,25},{9,17},{17,9},{25,1},{2,26},{10... | collective-permute-start | bytes 1191944 | tf_op jit(solution)/shard_map/ppermute | solution.py:279
  7.3 19.4 %collective-permute-start.2 = (bf16[1552,128]{1,0:T(8,128)(2,1)}, bf16[1552,128]{1,0:T(8,128)(2,1)S(1)}, u32[]{:S(2)}, u32[]{:S(2)}) collective-permute-start(bf16[1552,128]{1,0:T(8,128)(2,1)} %get-tuple-element.30), channel_id=1, source_target_pairs={{0,8},{8,0},{16,24},{24,16},{1,9},{9,1},{17,25},{25,17},{2,10},{10... | collective-permute-start | bytes 1191944 | tf_op jit(solution)/shard_map/ppermute | solution.py:279
  7.8 18.8 %collective-permute-start.3 = (bf16[1552,128]{1,0:T(8,128)(2,1)}, bf16[1552,128]{1,0:T(8,128)(2,1)S(1)}, u32[]{:S(2)}, u32[]{:S(2)}) collective-permute-start(bf16[1552,128]{1,0:T(8,128)(2,1)} %get-tuple-element.31), channel_id=1, source_target_pairs={{0,16},{8,24},{16,0},{24,8},{1,17},{9,25},{17,1},{25,9},{2,18},{10... | collective-permute-start | bytes 1191944 | tf_op jit(solution)/shard_map/ppermute | solution.py:279
  7.9 1.4 %collective-permute-start = (bf16[32,128]{1,0:T(8,128)(2,1)}, bf16[32,128]{1,0:T(8,128)(2,1)S(1)}, u32[]{:S(2)}, u32[]{:S(2)}) collective-permute-start(bf16[32,128]{1,0:T(8,128)(2,1)} %bitcast.3), channel_id=1, source_target_pairs={{0,1},{1,0},{2,3},{3,2},{4,5},{5,4},{6,7},{7,6},{8,9},{9,8},{10,11... | collective-permute-start | bytes 24584 | tf_op jit(solution)/shard_map/ppermute | solution.py:279
  9.3 1.0 %copy-start = (bf16[1552,128]{1,0:T(8,128)(2,1)S(1)}, bf16[1552,128]{1,0:T(8,128)(2,1)}, u32[]{:S(2)}) copy-start(bf16[1552,128]{1,0:T(8,128)(2,1)} %get-tuple-element.25.refs_0_) | copy-start | bytes 1191940
  10.3 0.9 %copy-start.1 = (bf16[512,128]{1,0:T(8,128)(2,1)S(1)}, bf16[512,128]{1,0:T(8,128)(2,1)}, u32[]{:S(2)}) copy-start(bf16[512,128]{1,0:T(8,128)(2,1)} %get-tuple-element.26.refs_1_) | copy-start | bytes 393220
  11.2 0.7 %copy-start.2 = (bf16[2,1,16,128]{3,2,1,0:T(8,128)(2,1)S(1)}, bf16[2,1,16,128]{3,2,1,0:T(8,128)(2,1)}, u32[]{:S(2)}) copy-start(bf16[2,1,16,128]{3,2,1,0:T(8,128)(2,1)} %param.10) | copy-start | bytes 24580
  11.9 0.7 %copy-start.3 = (s32[2,4,4]{2,1,0:T(4,128)S(1)}, s32[2,4,4]{2,1,0:T(4,128)}, u32[]{:S(2)}) copy-start(s32[2,4,4]{2,1,0:T(4,128)} %live_hbm.1) | copy-start | bytes 388
  13.3 3.8 %collective-permute-start.4 = (bf16[64,128]{1,0:T(8,128)(2,1)S(1)}, bf16[64,128]{1,0:T(8,128)(2,1)S(1)}, u32[]{:S(2)}, u32[]{:S(2)}) collective-permute-start(bf16[64,128]{1,0:T(8,128)(2,1)S(1)} %get-tuple-element.33.one_ref), channel_id=1, source_target_pairs={{0,2},{1,3},{2,0},{3,1},{4,6},{5,7},{6,4},{7,5},{8,10},{9,11},{10,... | collective-permute-start | bytes 49160 | tf_op jit(solution)/shard_map/ppermute | solution.py:279
  17.1 5.4 %collective-permute-start.5 = (bf16[128,128]{1,0:T(8,128)(2,1)S(1)}, bf16[128,128]{1,0:T(8,128)(2,1)S(1)}, u32[]{:S(2)}, u32[]{:S(2)}) collective-permute-start(bf16[128,128]{1,0:T(8,128)(2,1)S(1)} %join.2.one_ref), channel_id=1, source_target_pairs={{0,4},{1,5},{2,6},{3,7},{4,0},{5,1},{6,2},{7,3},{8,12},{9,13},{10,... | collective-permute-start | bytes 98312 | tf_op jit(solution)/shard_map/ppermute | solution.py:279
  20.1 10.9 %collective-permute-start.6 = (bf16[512,128]{1,0:T(8,128)(2,1)}, bf16[512,128]{1,0:T(8,128)(2,1)S(1)}, u32[]{:S(2)}, u32[]{:S(2)}) collective-permute-start(bf16[512,128]{1,0:T(8,128)(2,1)} %get-tuple-element.38), channel_id=1, source_target_pairs={{0,24},{8,16},{16,8},{24,0},{1,25},{9,17},{17,9},{25,1},{2,26},{10... | collective-permute-start | bytes 393224 | tf_op jit(solution)/shard_map/ppermute | solution.py:279
  22.5 8.6 %collective-permute-start.7 = (bf16[512,128]{1,0:T(8,128)(2,1)}, bf16[512,128]{1,0:T(8,128)(2,1)S(1)}, u32[]{:S(2)}, u32[]{:S(2)}) collective-permute-start(bf16[512,128]{1,0:T(8,128)(2,1)} %get-tuple-element.39), channel_id=1, source_target_pairs={{0,8},{8,0},{16,24},{24,16},{1,9},{9,1},{17,25},{25,17},{2,10},{10... | collective-permute-start | bytes 393224 | tf_op jit(solution)/shard_map/ppermute | solution.py:279
  23.8 7.3 %collective-permute-start.8 = (bf16[512,128]{1,0:T(8,128)(2,1)}, bf16[512,128]{1,0:T(8,128)(2,1)S(1)}, u32[]{:S(2)}, u32[]{:S(2)}) collective-permute-start(bf16[512,128]{1,0:T(8,128)(2,1)} %get-tuple-element.40), channel_id=1, source_target_pairs={{0,16},{8,24},{16,0},{24,8},{1,17},{9,25},{17,1},{25,9},{2,18},{10... | collective-permute-start | bytes 393224 | tf_op jit(solution)/shard_map/ppermute | solution.py:279
  33.8 5.9 %collective-permute-start.9 = (f32[64,256]{1,0:T(8,128)S(1)}, f32[64,256]{1,0:T(8,128)S(1)}, u32[]{:S(2)}, u32[]{:S(2)}) collective-permute-start(f32[64,256]{1,0:T(8,128)S(1)} %get-tuple-element.42), channel_id=1, source_target_pairs={{0,24},{8,16},{16,8},{24,0},{1,25},{9,17},{17,9},{25,1},{2,26},{10... | collective-permute-start | bytes 196616 | tf_op jit(solution)/shard_map/ppermute | solution.py:279
  36.2 4.3 %collective-permute-start.10 = (f32[64,256]{1,0:T(8,128)S(1)}, f32[64,256]{1,0:T(8,128)S(1)}, u32[]{:S(2)}, u32[]{:S(2)}) collective-permute-start(f32[64,256]{1,0:T(8,128)S(1)} %get-tuple-element.43), channel_id=1, source_target_pairs={{0,8},{8,0},{16,24},{24,16},{1,9},{9,1},{17,25},{25,17},{2,10},{10... | collective-permute-start | bytes 196616 | tf_op jit(solution)/shard_map/ppermute | solution.py:279
  36.7 4.3 %collective-permute-start.11 = (f32[64,256]{1,0:T(8,128)S(1)}, f32[64,256]{1,0:T(8,128)S(1)}, u32[]{:S(2)}, u32[]{:S(2)}) collective-permute-start(f32[64,256]{1,0:T(8,128)S(1)} %get-tuple-element.44), channel_id=1, source_target_pairs={{0,16},{8,24},{16,0},{24,8},{1,17},{9,25},{17,1},{25,9},{2,18},{10... | collective-permute-start | bytes 196616 | tf_op jit(solution)/shard_map/ppermute | solution.py:279

commit v4 on v3

--- a/solution.py
+++ b/solution.py
@@ -10,6 +10,7 @@
 
 SUB = 8
 PAIR = 16
+UNROLL = 16
 F32 = jnp.float32
 BF16 = jnp.bfloat16
 
@@ -208,7 +209,7 @@
                     vir_out[here, at : at + tile] = vir[row, :, moment * tile : (moment + 1) * tile]
         return carry
 
-    lax.fori_loop(0, steps, step, 0, unroll=2)
+    lax.fori_loop(0, steps, step, 0, unroll=min(steps, UNROLL))
 
 
 def occ_kernel(sizes, steps, live_ref, *refs):
@@ -252,7 +253,7 @@
         out[...] = picked
 
 
-def on_device(b_rows, col_blocks, g_occ, occ_live, g_virt, tau_weight):
+def on_device_dense(b_rows, col_blocks, g_occ, occ_live, g_virt, tau_weight):
     orb_count = lax.axis_size("orb")
     aux_count = lax.axis_size("aux")
     aux_dev, rows_dev, slot_count, tile = b_rows.shape
@@ -346,6 +347,336 @@
     return total
 
 
+class Message:
+    def __init__(self, virt_rows, occ_rows):
+        self.virt = slice(0, virt_rows)
+        self.occ = slice(virt_rows, virt_rows + occ_rows)
+        self.list = slice(virt_rows + occ_rows, virt_rows + occ_rows + 16)
+        self.rows = virt_rows + occ_rows + 16
+
+
+def equal(one, two):
+    return jnp.where(one == two, 1.0, 0.0)
+
+
+def at_group(group, values):
+    found = values[0]
+    for place in range(1, len(values)):
+        found = jnp.where(group == place, values[place], found)
+    return found
+
+
+class Choice:
+    def __init__(self, message, refs):
+        me = lax.axis_index("orb")
+        near = []
+        for ref in refs:
+            row = ref[message.list, :].astype(F32)[0:1, :]
+            near.append([row[:, slot : slot + 1] for slot in range(2)])
+        lists = [[at_group(me ^ group, [near[d][slot] for d in range(4)]) for slot in range(2)] for group in range(4)]
+        shape = (8, 128)
+        index = iota(shape, 0) * shape[1] + iota(shape, 1)
+        bits = [((index >> place) & 1).astype(F32) for place in range(8)]
+        sent_x = [lists[g][0] + bits[g] * (lists[g][1] - lists[g][0]) for g in range(4)]
+        sent_y = [lists[g][0] + bits[4 + g] * (lists[g][1] - lists[g][0]) for g in range(4)]
+        good = jnp.where(index < 256, 1.0, 0.0)
+        for one, two in ((0, 1), (2, 3), (0, 2), (1, 3), (0, 3), (1, 2)):
+            for slot in range(2):
+                column = lists[one][slot]
+                shared = jnp.maximum(equal(column, lists[two][0]), equal(column, lists[two][1]))
+                if two == one ^ 1:
+                    met = jnp.maximum(equal(sent_x[one], column), equal(sent_x[two], column))
+                elif two == one ^ 2:
+                    met = jnp.maximum(equal(sent_y[one], column), equal(sent_y[two], column))
+                else:
+                    met = jnp.maximum(
+                        equal(sent_x[one], column) * equal(sent_y[two], column),
+                        equal(sent_y[one], column) * equal(sent_x[two], column),
+                    )
+                good = good * jnp.maximum(met, 1.0 - shared)
+        number = jnp.where(good > 0.5, index.astype(F32), 1024.0)
+        number = jnp.min(jnp.min(number, axis=1, keepdims=True), axis=0, keepdims=True)
+        chosen = []
+        for place in range(8):
+            rest = jnp.floor(number * (1.0 / (1 << place)))
+            chosen.append(rest - 2.0 * jnp.floor(rest * 0.5))
+        all_x = [lists[g][0] + chosen[g] * (lists[g][1] - lists[g][0]) for g in range(4)]
+        all_y = [lists[g][0] + chosen[4 + g] * (lists[g][1] - lists[g][0]) for g in range(4)]
+        self.own = at_group(me, [lists[g][0] for g in range(4)]), at_group(me, [lists[g][1] for g in range(4)])
+        self.slot_x = at_group(me, chosen[:4])
+        self.slot_y = at_group(me, chosen[4:])
+        got_x, got_y = at_group(me ^ 1, all_x), at_group(me ^ 2, all_y)
+        self.got = got_x, got_y
+        one = jnp.ones_like(got_x)
+        foreign = one - jnp.maximum(equal(got_x, self.own[0]), equal(got_x, self.own[1]))
+        self.third = foreign * got_x + (one - foreign) * got_y
+        first_x = jnp.where(me < (me ^ 1), one, one - equal(at_group(me, all_x), got_x))
+        first_y = jnp.where(me < (me ^ 2), one, one - equal(at_group(me, all_y), got_y))
+        also = equal(at_group(me ^ 2, all_x), got_x) * equal(at_group(me ^ 1, all_y), got_x)
+        first_far = jnp.where(me < (me ^ 3), one, one - also)
+        zero = jnp.zeros_like(one)
+        with_x = [equal(got_x, column) * first_x for column in self.own]
+        with_y = [equal(got_y, column) * first_y for column in self.own]
+        far = equal(got_x, got_y) * first_far
+        self.pairs = [
+            [one, zero, with_x[0], with_y[0]],
+            [zero, one, with_x[1], with_y[1]],
+            [with_x[0], with_x[1], zero, far],
+            [with_y[0], with_y[1], far, zero],
+        ]
+
+
+def message_kernel(message, virt_hbm, occ_hbm, col_hbm, out_hbm, out_ref, occ_ref, col_ref, sem):
+    copies = [
+        pltpu.make_async_copy(virt_hbm, out_ref.at[message.virt], sem.at[0]),
+        pltpu.make_async_copy(occ_hbm, occ_ref, sem.at[1]),
+        pltpu.make_async_copy(col_hbm, col_ref, sem.at[2]),
+    ]
+    for copy in copies:
+        copy.start()
+    tile = out_ref.shape[1]
+    out_ref[message.occ, :] = jnp.zeros((occ_ref.shape[0], tile), BF16)
+    for copy in copies:
+        copy.wait()
+    out_ref[message.occ, : occ_ref.shape[1]] = occ_ref[...]
+    row, lane = iota((16, tile), 0), iota((16, tile), 1)
+    value = jnp.zeros((16, tile), F32)
+    for slot in range(col_ref.shape[1]):
+        here = jnp.logical_and(row == 0, lane == slot)
+        value = jnp.where(here, col_ref[0, slot].astype(F32), value)
+    out_ref[message.list, :] = value.astype(BF16)
+    copy = pltpu.make_async_copy(out_ref, out_hbm, sem.at[3])
+    copy.start()
+    copy.wait()
+
+
+def own_kernel(rows_dev, steps, b_ref, *outs):
+    half_rows = rows_dev * SUB
+    out_rows = 2 * half_rows
+    in_rows = PAIR * rows_dev * 2
+    line = iota((out_rows, in_rows), 0)
+    place = iota((out_rows, in_rows), 1)
+    func = (line // half_rows) * SUB + line % SUB
+    first = (func * rows_dev + (line % half_rows) // SUB) * 2
+    pick = jnp.concatenate([jnp.where(place == first + slot, 1.0, 0.0).astype(BF16) for slot in range(2)], 0)
+    for index in range(steps):
+        moved = dot(pick, b_ref[index * in_rows : (index + 1) * in_rows, :]).astype(BF16)
+        for slot, out in enumerate(outs):
+            out[index * out_rows : (index + 1) * out_rows, :] = moved[slot * out_rows : (slot + 1) * out_rows]
+
+
+def send_kernel(message, *refs):
+    messages, (own0, own1, to_x, to_y, virt_out) = refs[:4], refs[4:]
+    choice = Choice(message, messages)
+    to_x[...] = jnp.where(choice.slot_x > 0.5, own1[...], own0[...])
+    to_y[...] = jnp.where(choice.slot_y > 0.5, own1[...], own0[...])
+    me = lax.axis_index("orb")
+    rows = message.virt.stop
+    for slot, column in enumerate((choice.own[0], choice.own[1], choice.third)):
+        total = jnp.zeros((rows, virt_out.shape[1]), F32)
+        for distance in range(4):
+            weight = equal(column, (me ^ distance).astype(F32))
+            total = total + weight * messages[distance][message.virt, :].astype(F32)
+        virt_out[slot * rows : (slot + 1) * rows, :] = total.astype(BF16)
+
+
+def aux_steps(aux_count):
+    steps = []
+    distance = aux_count // 2
+    while distance:
+        steps.append(distance)
+        distance //= 2
+    return steps
+
+
+def aux_order(aux_count):
+    order = [0]
+    for distance in aux_steps(aux_count):
+        order = order + [value ^ distance for value in order]
+    return order
+
+
+def virt_kernel(sizes, message, *refs):
+    aux_count, rows_dev, tau_count = sizes
+    messages, (virt_ref, virt_out) = refs[:4], refs[4:]
+    choice = Choice(message, messages)
+    aux_me = lax.axis_index("aux")
+    tile = virt_ref.shape[1]
+    part = tile // aux_count
+    order = aux_order(aux_count)
+    line = iota((tile, virt_ref.shape[0]), 0)
+    place = iota((tile, virt_ref.shape[0]), 1)
+    virts = []
+    for slot in range(3):
+        columns = []
+        for moment in range(tau_count):
+            held = pick_static((line // part) ^ aux_me, [order.index(value) for value in range(aux_count)])
+            wanted = ((held * 3 + slot) * tau_count + moment) * part + line % part
+            columns.append(dot(jnp.where(place == wanted, 1.0, 0.0).astype(BF16), virt_ref[...]))
+        virts.append(jnp.concatenate(columns, 1))
+    virt_out[0] = virts[0].astype(BF16)
+    virt_out[1] = virts[1].astype(BF16)
+    for at, column in enumerate(choice.got):
+        one, two = equal(column, choice.own[0]), equal(column, choice.own[1])
+        virt_out[2 + at] = (one * virts[0] + two * virts[1] + (1.0 - one - two) * virts[2]).astype(BF16)
+
+
+def mix_kernel(sizes, message, live_ref, *refs):
+    aux_count, rows_dev, tau_count = sizes
+    messages, mix_out = refs[:4], refs[4]
+    choice = Choice(message, messages)
+    me = lax.axis_index("orb")
+    tile = messages[0].shape[1]
+    rows = 4 * rows_dev
+    half_rows = rows_dev * SUB
+    groups = [me, me, me ^ 1, me ^ 2]
+    occ_all = jnp.concatenate([messages[at][message.occ, :] for at in (0, 0, 1, 2)], 0)
+    left_shape = (tau_count * rows * SUB, occ_all.shape[0])
+    line = iota(left_shape, 0)
+    row_of = (line % (rows * SUB)) // SUB
+    wanted = ((row_of // rows_dev) * tau_count + line // (rows * SUB)) * rows_dev + row_of % rows_dev
+    left = jnp.where(iota(left_shape, 1) == wanted, 1.0, 0.0).astype(BF16)
+    right_shape = (tile, rows * SUB)
+    col_of = iota(right_shape, 1) // SUB
+    wanted = pick_static(col_of // rows_dev, groups) * rows_dev + col_of % rows_dev
+    right = jnp.where(iota(right_shape, 0) == wanted, 1.0, 0.0).astype(BF16)
+    spread = dot(dot(left, occ_all).astype(BF16), right)
+    same = iota((half_rows, rows * SUB), 0) % SUB == iota((half_rows, rows * SUB), 1) % SUB
+    group_of = iota((1, rows * SUB), 1) // half_rows
+    for moment in range(tau_count):
+        for one in range(4):
+            live = jnp.zeros((1, rows * SUB), F32)
+            for two in range(4):
+                value = live_ref[moment, groups[one], groups[two]].astype(F32) * choice.pairs[one][two]
+                live = jnp.where(group_of == two, value, live)
+            at = (moment * 4 + one) * half_rows
+            keep = jnp.logical_and(same, live != 0.0)
+            mix_out[at : at + half_rows, :] = jnp.where(keep, spread[at : at + half_rows], 0.0).astype(BF16)
+
+
+def work_kernel(rows_dev, tau_count, steps, scale, tau_ref, mix_ref, virt_ref, *refs):
+    blocks, outs, (occ_ref, vir_ref) = refs[:4], refs[4:8], refs[8:]
+    rows = 4 * rows_dev
+    half_rows = rows_dev * SUB
+    tile = blocks[0].shape[1]
+
+    def step(index, carry):
+        here = pl.ds(pl.multiple_of(index * PAIR, PAIR), PAIR)
+        halves = []
+        for half in range(2):
+            at = pl.multiple_of((index * 2 + half) * half_rows, half_rows)
+            halves.append(jnp.concatenate([block[pl.ds(at, half_rows), :] for block in blocks], 0))
+        occ = dot(mix_ref[...], jnp.concatenate(halves, 1))
+        occ = [occ[:, half * tile : (half + 1) * tile].reshape(tau_count * rows, SUB, tile) for half in range(2)]
+        occ = jnp.concatenate(occ, 1).astype(BF16)
+        for row in range(tau_count * rows):
+            occ_ref[here, row * tile : (row + 1) * tile] = occ[row]
+        for group, block in enumerate(blocks):
+            both = block[pl.ds(pl.multiple_of(index * 2 * half_rows, half_rows), 2 * half_rows), :]
+            vir = dot(both, virt_ref[group]).reshape(2, rows_dev, SUB, tau_count * tile)
+            vir = jnp.concatenate([vir[0], vir[1]], 1).astype(BF16)
+            for moment in range(tau_count):
+                for row in range(rows_dev):
+                    at = (moment * rows + group * rows_dev + row) * tile
+                    vir_ref[here, at : at + tile] = vir[row, :, moment * tile : (moment + 1) * tile]
+        return carry
+
+    lax.fori_loop(0, steps, step, 0, unroll=min(steps, UNROLL))
+    depth = rows * tile
+    chi = None
+    for moment in range(tau_count):
+        here = slice(moment * depth, (moment + 1) * depth)
+        term = lax.dot_general(
+            occ_ref[:, here], vir_ref[:, here], (((1,), (1,)), ((), ())), preferred_element_type=F32
+        ) * tau_ref[moment]
+        chi = term if chi is None else chi + term
+    chi = chi * scale
+    me = lax.axis_index("orb")
+    share_rows = outs[0].shape[0]
+    for distance, out in zip(partners(4), outs):
+        picked = chi[0:share_rows]
+        for owner in range(1, 4):
+            picked = jnp.where(me ^ distance == owner, chi[owner * share_rows : (owner + 1) * share_rows], picked)
+        out[...] = picked
+
+
+def on_device_square(b_rows, col_blocks, g_occ, occ_live, g_virt, tau_weight):
+    orb_count = lax.axis_size("orb")
+    aux_count = lax.axis_size("aux")
+    aux_dev, rows_dev, slot_count, tile = b_rows.shape
+    tau_count = g_occ.shape[0]
+    rows = orb_count * rows_dev
+    steps = aux_dev // PAIR
+    share_rows = aux_dev // orb_count
+    sizes = (aux_count, rows_dev, tau_count)
+    scale = 1.0 / math.sqrt(rows * tile * orb_count)
+    smem = pl.BlockSpec(memory_space=pltpu.SMEM)
+    vmem = pl.BlockSpec(memory_space=pltpu.VMEM)
+    hbm = pl.BlockSpec(memory_space=pl.ANY)
+
+    def call(kernel, name, out_shape, in_specs, scratch, limit, out_spec=vmem):
+        return pl.pallas_call(
+            kernel, out_shape=out_shape, in_specs=in_specs, out_specs=[out_spec] * len(out_shape),
+            scratch_shapes=scratch, compiler_params=pltpu.CompilerParams(vmem_limit_bytes=limit << 20), name=name,
+        )
+
+    def xor(value, axis, distance):
+        return lax.ppermute(value, axis, [(i, i ^ distance) for i in range(lax.axis_size(axis))])
+
+    def half(*shape):
+        return jax.ShapeDtypeStruct(shape, BF16)
+
+    flat = b_rows.reshape(-1, tile)
+    virt = g_virt.reshape(-1, tile)
+    occ = g_occ.reshape(tau_count * rows_dev, -1)
+    message = Message(virt.shape[0], occ.shape[0])
+    dma = pltpu.SemaphoreType.DMA
+    (sent,) = call(
+        functools.partial(message_kernel, message), "message", [half(message.rows, tile)], [hbm] * 3,
+        [
+            pltpu.VMEM((message.rows, tile), BF16), pltpu.VMEM(occ.shape, BF16),
+            pltpu.SMEM(col_blocks.shape, jnp.int32), dma((4,)),
+        ], 60, hbm,
+    )(virt, occ, col_blocks)
+    came = {distance: xor(sent, "orb", distance) for distance in partners(orb_count)[1:]}
+    messages = [sent] + [came[distance] for distance in range(1, orb_count)]
+    block = half(aux_dev * rows_dev, tile)
+    owns = call(functools.partial(own_kernel, rows_dev, steps), "own", [block] * 2, [vmem], [], 6)(flat)
+    to_x, to_y, virt = call(
+        functools.partial(send_kernel, message), "send",
+        [block] * 2 + [half(3 * message.virt.stop, tile)], [vmem] * 6, [], 6,
+    )(*messages, *owns)
+    from_x, from_y = xor(to_x, "orb", 1), xor(to_y, "orb", 2)
+    for distance in aux_steps(aux_count):
+        virt = call(join_kernel, "join", [half(2 * virt.shape[0], tile)], [vmem] * 2, [], 4)(
+            virt, xor(virt, "aux", distance)
+        )[0]
+    (mix,) = call(
+        functools.partial(mix_kernel, sizes, message), "mix",
+        [half(tau_count * rows * SUB, rows * SUB)], [smem] + [vmem] * 4, [], 8,
+    )(occ_live, *messages)
+    (virt,) = call(
+        functools.partial(virt_kernel, sizes, message), "virt",
+        [half(4, tile, tau_count * tile)], [vmem] * 5, [], 8,
+    )(*messages, virt)
+    wide = tau_count * rows * tile
+    shares = call(
+        functools.partial(work_kernel, rows_dev, tau_count, steps, scale), "work",
+        [jax.ShapeDtypeStruct((share_rows, aux_dev), F32)] * orb_count, [smem] + [vmem] * 6,
+        [pltpu.VMEM((aux_dev, wide), BF16), pltpu.VMEM((aux_dev, wide), BF16)], 24,
+    )(tau_weight, mix, virt, *owns, from_x, from_y)
+    total = shares[0]
+    for distance, share in zip(partners(orb_count)[1:], shares[1:]):
+        total = total + xor(share, "orb", distance)
+    return total
+
+
+def on_device(b_rows, col_blocks, g_occ, occ_live, g_virt, tau_weight):
+    square = lax.axis_size("orb") == 4 and b_rows.shape[2] == 2
+    plan = on_device_square if square else on_device_dense
+    return plan(b_rows, col_blocks, g_occ, occ_live, g_virt, tau_weight)
+
+
 def solution(mesh):
     in_specs = (
         P("aux", "orb", None, None),

time: 41.9 us -> 36 us (0.86)
  starting transfers between devices: 18.4 us -> 13.8 us
  waiting for transfers between devices: 8.27 us -> 11.4 us
  Pallas kernels: 11 us -> 8.65 us
  local copies, waits for them, and re-layouts: 3.29 us -> 1.24 us
    ppermute x12 -> x11, starting transfers between devices: 18.4 us -> 13.8 us  [xor(): lax.ppermute(value, axis, [(i, i ^ distance) for i in range(lax.axis_size...]
    ppermute x12 -> x11, waiting for transfers between devices: 8.27 us -> 11.4 us  [xor(): lax.ppermute(value, axis, [(i, i ^ distance) for i in range(lax.axis_size...]
    pallas_call x7 -> x9, Pallas kernels: 11 us -> 8.65 us  [the longest x1 4.03 us: on_device_square(): call(functools.partial(work_kernel, rows_dev, tau_count, steps, scale), '...]
    unnamed x10 -> x8, local copies, waits for them, and re-layouts: 3.29 us -> 1.24 us
  transfers between devices with their start and end apart: 12 -> 11, of which waited for: 7 -> 10; matrix products, arithmetic and copies ran while one was open for 0% -> 0% of each run, Pallas kernels for 12% -> 7%
where the time goes in v4:
time: 36 us; the launch traced here: 35.8 us
  starting transfers between devices  13.8 us (38%)
  waiting for transfers between devices  11.4 us (32%)
  Pallas kernels  8.65 us (24%)
  local copies, waits for them, and re-layouts  1.24 us (3%)
  other arithmetic  0.65 us (2%)
    ppermute x11, starting transfers between devices, xor(): lax.ppermute(value, axis, [(i, i ^ distance) for i in range(lax.axis_size...  13.8 us
    ppermute x11, waiting for transfers between devices, xor(): lax.ppermute(value, axis, [(i, i ^ distance) for i in range(lax.axis_size...  11.4 us
    pallas_call x1, Pallas kernels, on_device_square(): call(functools.partial(work_kernel, rows_dev, tau_count, steps, scale), '...  4.03 us
    pallas_call x1, Pallas kernels, on_device_square(): call(functools.partial(message_kernel, message), 'message', [half(message...  1.44 us
    unnamed x8, local copies, waits for them, and re-layouts  1.24 us
    pallas_call x1, Pallas kernels, on_device_square(): call(functools.partial(mix_kernel, sizes, message), 'mix', [half(tau_coun...  1.14 us
  transfers between devices with their start and end apart: 11, of which 10 were waited for; matrix products, arithmetic and copies ran while one was open for 0% of the time, Pallas kernels for 7%

profile of v4, /device:TPU:0, one launch (start us, length us, event | category | flops | bytes accessed | tf_op | source)
XLA Modules:
  0.0 35.8 jit_solution(6608267582713971783)
XLA Ops:
  0.0 1.4 %message.1.refs_0_ = bf16[64,128]{1,0:T(8,128)(2,1)} custom-call(bf16[32,128]{1,0:T(8,128)(2,1)} %bitcast.4, bf16[16,32]{1,0:T(8,128)(2,1)} %bitcast.5, s32[1,2]{1,0:T(1,128)} %col_hbm.1), custom_call_target="tpu_custom_call" | custom-call | tf_op jit(solution)/shard_map/message/pallas_call | solution.py:634
  1.4 3.0 %collective-permute-start = (bf16[64,128]{1,0:T(8,128)(2,1)}, bf16[64,128]{1,0:T(8,128)(2,1)S(1)}, u32[]{:S(2)}, u32[]{:S(2)}) collective-permute-start(bf16[64,128]{1,0:T(8,128)(2,1)} %message.1.refs_0_), channel_id=1, source_target_pairs={{0,8},{8,0},{16,24},{24,16},{1,9},{9,1},{17,25},{25,17},{2,10},{10... | collective-permute-start | bytes 49160 | tf_op jit(solution)/shard_map/ppermute | solution.py:624
  4.5 1.5 %collective-permute-start.1 = (bf16[64,128]{1,0:T(8,128)(2,1)}, bf16[64,128]{1,0:T(8,128)(2,1)S(1)}, u32[]{:S(2)}, u32[]{:S(2)}) collective-permute-start(bf16[64,128]{1,0:T(8,128)(2,1)} %message.1.refs_0_), channel_id=1, source_target_pairs={{0,16},{8,24},{16,0},{24,8},{1,17},{9,25},{17,1},{25,9},{2,18},{10... | collective-permute-start | bytes 49160 | tf_op jit(solution)/shard_map/ppermute | solution.py:624
  6.0 0.0 collective-permute-start.2
  6.0 0.0 copy-start
  6.0 1.2 %copy-done = bf16[256,8,2,128]{3,2,1,0:T(2,128)(2,1)S(1)} copy-done((bf16[256,8,2,128]{3,2,1,0:T(2,128)(2,1)S(1)}, bf16[256,8,2,128]{3,2,1,0:T(2,128)(2,1)}, u32[]{:S(2)}) %copy-start) | copy-done | bytes 1048600
  7.2 0.0 copy-start.1
  7.2 0.7 %own.1 = (bf16[2048,128]{1,0:T(8,128)(2,1)S(1)}, bf16[2048,128]{1,0:T(8,128)(2,1)S(1)}) custom-call(bf16[4096,128]{1,0:T(8,128)(2,1)S(1)} %bitcast.3), custom_call_target="tpu_custom_call" | custom-call | tf_op jit(solution)/shard_map/own/pallas_call | solution.py:644
  7.9 0.0 collective-permute-done.refs_1_
  7.9 0.5 %collective-permute-done.1.refs_2_ = bf16[64,128]{1,0:T(8,128)(2,1)S(1)} collective-permute-done((bf16[64,128]{1,0:T(8,128)(2,1)}, bf16[64,128]{1,0:T(8,128)(2,1)S(1)}, u32[]{:S(2)}, u32[]{:S(2)}) %collective-permute-start.1) | collective-permute-done | bytes 16416 | tf_op jit(solution)/shard_map/ppermute | solution.py:624
  8.4 2.4 %collective-permute-done.2.refs_3_ = bf16[64,128]{1,0:T(8,128)(2,1)S(1)} collective-permute-done((bf16[64,128]{1,0:T(8,128)(2,1)}, bf16[64,128]{1,0:T(8,128)(2,1)S(1)}, u32[]{:S(2)}, u32[]{:S(2)}) %collective-permute-start.2) | collective-permute-done | bytes 16416 | tf_op jit(solution)/shard_map/ppermute | solution.py:624
  10.8 0.0 copy-done.1
  10.8 0.7 %send.1 = (bf16[2048,128]{1,0:T(8,128)(2,1)S(1)}, bf16[2048,128]{1,0:T(8,128)(2,1)S(1)}, bf16[96,128]{1,0:T(8,128)(2,1)S(1)}) custom-call(bf16[64,128]{1,0:T(8,128)(2,1)S(1)} %copy-done.1, bf16[64,128]{1,0:T(8,128)(2,1)S(1)} %collective-permute-done.refs_1_, bf16[64,128]{1,0:T(8,128)(2,1)S(1)} %collective-permute-done.1.refs_2_, ...), custom_call_target="tpu_custom_call" | custom-call | tf_op jit(solution)/shard_map/send/pallas_call | solution.py:645
  11.5 0.6 %collective-permute-start.6 = (bf16[2048,128]{1,0:T(8,128)(2,1)S(1)}, bf16[2048,128]{1,0:T(8,128)(2,1)S(1)}, u32[]{:S(2)}, u32[]{:S(2)}) collective-permute-start(bf16[2048,128]{1,0:T(8,128)(2,1)S(1)} %get-tuple-element.17), channel_id=1, source_target_pairs={{0,8},{8,0},{16,24},{24,16},{1,9},{9,1},{17,25},{25,17},{2,10},{10... | collective-permute-start | bytes 1572872 | tf_op jit(solution)/shard_map/ppermute | solution.py:624
  12.1 0.1 collective-permute-start.7
  12.2 3.0 %collective-permute-start.3 = (bf16[96,128]{1,0:T(8,128)(2,1)S(1)}, bf16[96,128]{1,0:T(8,128)(2,1)S(1)}, u32[]{:S(2)}, u32[]{:S(2)}) collective-permute-start(bf16[96,128]{1,0:T(8,128)(2,1)S(1)} %get-tuple-element.16.one_ref), channel_id=1, source_target_pairs={{0,4},{1,5},{2,6},{3,7},{4,0},{5,1},{6,2},{7,3},{8,12},{9,13},{10,... | collective-permute-start | bytes 73736 | tf_op jit(solution)/shard_map/ppermute | solution.py:624
  15.2 1.8 %collective-permute-done.3.two_ref = bf16[96,128]{1,0:T(8,128)(2,1)S(1)} collective-permute-done((bf16[96,128]{1,0:T(8,128)(2,1)S(1)}, bf16[96,128]{1,0:T(8,128)(2,1)S(1)}, u32[]{:S(2)}, u32[]{:S(2)}) %collective-permute-start.3) | collective-permute-done | bytes 24608 | tf_op jit(solution)/shard_map/ppermute | solution.py:624
  17.0 0.0 copy-start.2
  17.0 1.9 %collective-permute-start.4 = (bf16[192,128]{1,0:T(8,128)(2,1)S(1)}, bf16[192,128]{1,0:T(8,128)(2,1)S(1)}, u32[]{:S(2)}, u32[]{:S(2)}) collective-permute-start(bf16[192,128]{1,0:T(8,128)(2,1)S(1)} %join.3.one_ref), channel_id=1, source_target_pairs={{0,2},{1,3},{2,0},{3,1},{4,6},{5,7},{6,4},{7,5},{8,10},{9,11},{10,... | collective-permute-start | bytes 147464 | tf_op jit(solution)/shard_map/ppermute | solution.py:624
  18.9 2.2 %collective-permute-done.4.two_ref = bf16[192,128]{1,0:T(8,128)(2,1)S(1)} collective-permute-done((bf16[192,128]{1,0:T(8,128)(2,1)S(1)}, bf16[192,128]{1,0:T(8,128)(2,1)S(1)}, u32[]{:S(2)}, u32[]{:S(2)}) %collective-permute-start.4) | collective-permute-done | bytes 49184 | tf_op jit(solution)/shard_map/ppermute | solution.py:624
  21.1 0.1 collective-permute-start.5
  21.2 0.0 copy-done.2
  21.2 1.1 %mix.1.mix_ref = bf16[512,256]{1,0:T(8,128)(2,1)S(1)} custom-call(s32[2,4,4]{2,1,0:T(4,128)S(1)} %copy-done.2, bf16[64,128]{1,0:T(8,128)(2,1)S(1)} %copy-done.1, bf16[64,128]{1,0:T(8,128)(2,1)S(1)} %collective-permute-done.refs_1_, bf16[64,128]{1,0:T(8,128)(2,1)S(1)} %collective-permute-done.1.refs_2_, bf16[64,128]{1,0:T(8,128)(2,1)S(1)} %collective-permute-done.2.refs_3_), custom_call_target="tpu_custom_call" | custom-call | tf_op jit(solution)/shard_map/mix/pallas_call | solution.py:654
  22.4 0.1 collective-permute-done.5.two_ref
  22.5 0.0 copy-start.3
  22.5 0.6 %virt.1.virt_ref = bf16[4,128,256]{2,1,0:T(8,128)(2,1)S(1)} custom-call(bf16[64,128]{1,0:T(8,128)(2,1)S(1)} %copy-done.1, bf16[64,128]{1,0:T(8,128)(2,1)S(1)} %collective-permute-done.refs_1_, bf16[64,128]{1,0:T(8,128)(2,1)S(1)} %collective-permute-done.1.refs_2_, bf16[64,128]{1,0:T(8,128)(2,1)S(1)} %collective-permute-done.2.refs_3_, ...), custom_call_target="tpu_custom_call" | custom-call | tf_op jit(solution)/shard_map/virt/pallas_call | solution.py:658
  23.2 0.4 collective-permute-done.6.refs_2_
  23.5 0.3 collective-permute-done.7.refs_3_
  23.8 0.0 copy-done.3
  23.8 4.0 %work.1 = (f32[64,256]{1,0:T(8,128)S(1)}, f32[64,256]{1,0:T(8,128)S(1)}, f32[64,256]{1,0:T(8,128)S(1)}, f32[64,256]{1,0:T(8,128)S(1)}) custom-call(f32[2]{0:T(128)S(1)} %copy-done.3, bf16[512,256]{1,0:T(8,128)(2,1)S(1)} %mix.1.mix_ref, bf16[4,128,256]{2,1,0:T(8,128)(2,1)S(1)} %virt.1.virt_ref, bf16[2048,128]{1,0:T(8,128)(2,1)S(1)} %get-tuple-element.14.refs_4_.refs_0_, ...), custom_call_target="tpu_custom_call" | custom-call | tf_op jit(solution)/shard_map/work/pallas_call | solution.py:663
  27.8 1.3 %collective-permute-start.10 = (f32[64,256]{1,0:T(8,128)S(1)}, f32[64,256]{1,0:T(8,128)S(1)}, u32[]{:S(2)}, u32[]{:S(2)}) collective-permute-start(f32[64,256]{1,0:T(8,128)S(1)} %get-tuple-element.22), channel_id=1, source_target_pairs={{0,16},{8,24},{16,0},{24,8},{1,17},{9,25},{17,1},{25,9},{2,18},{10... | collective-permute-start | bytes 196616 | tf_op jit(solution)/shard_map/ppermute | solution.py:624
  29.2 1.7 %collective-permute-start.8 = (f32[64,256]{1,0:T(8,128)S(1)}, f32[64,256]{1,0:T(8,128)S(1)}, u32[]{:S(2)}, u32[]{:S(2)}) collective-permute-start(f32[64,256]{1,0:T(8,128)S(1)} %get-tuple-element.20), channel_id=1, source_target_pairs={{0,24},{8,16},{16,8},{24,0},{1,25},{9,17},{17,9},{25,1},{2,26},{10... | collective-permute-start | bytes 196616 | tf_op jit(solution)/shard_map/ppermute | solution.py:624
  30.8 0.5 %collective-permute-start.9 = (f32[64,256]{1,0:T(8,128)S(1)}, f32[64,256]{1,0:T(8,128)S(1)}, u32[]{:S(2)}, u32[]{:S(2)}) collective-permute-start(f32[64,256]{1,0:T(8,128)S(1)} %get-tuple-element.21), channel_id=1, source_target_pairs={{0,8},{8,0},{16,24},{24,16},{1,9},{9,1},{17,25},{25,17},{2,10},{10... | collective-permute-start | bytes 196616 | tf_op jit(solution)/shard_map/ppermute | solution.py:624
  31.4 0.8 %collective-permute-done.10 = f32[64,256]{1,0:T(8,128)S(1)} collective-permute-done((f32[64,256]{1,0:T(8,128)S(1)}, f32[64,256]{1,0:T(8,128)S(1)}, u32[]{:S(2)}, u32[]{:S(2)}) %collective-permute-start.10) | collective-permute-done | bytes 65568 | tf_op jit(solution)/shard_map/ppermute | solution.py:624
  32.2 2.6 %collective-permute-done.8 = f32[64,256]{1,0:T(8,128)S(1)} collective-permute-done((f32[64,256]{1,0:T(8,128)S(1)}, f32[64,256]{1,0:T(8,128)S(1)}, u32[]{:S(2)}, u32[]{:S(2)}) %collective-permute-start.8) | collective-permute-done | bytes 65568 | tf_op jit(solution)/shard_map/ppermute | solution.py:624
  34.7 0.4 %collective-permute-done.9 = f32[64,256]{1,0:T(8,128)S(1)} collective-permute-done((f32[64,256]{1,0:T(8,128)S(1)}, f32[64,256]{1,0:T(8,128)S(1)}, u32[]{:S(2)}, u32[]{:S(2)}) %collective-permute-start.9) | collective-permute-done | bytes 65568 | tf_op jit(solution)/shard_map/ppermute | solution.py:624
  35.1 0.6 %add_add_fusion = f32[64,256]{1,0:T(8,128)} fusion(f32[64,256]{1,0:T(8,128)S(1)} %collective-permute-done.10, f32[64,256]{1,0:T(8,128)S(1)} %collective-permute-done.9, f32[64,256]{1,0:T(8,128)S(1)} %get-tuple-element.19, f32[64,256]{1,0:T(8,128)S(1)} %collective-permute-done.8), kind=kLoop, calls=%fused_computation | loop fusion | flops 49152 | bytes 327680 | tf_op jit(solution)/shard_map/add | solution.py:670
  (3 shorter events, 0.0 us)
Async XLA Ops:
  1.4 6.5 %collective-permute-start = (bf16[64,128]{1,0:T(8,128)(2,1)}, bf16[64,128]{1,0:T(8,128)(2,1)S(1)}, u32[]{:S(2)}, u32[]{:S(2)}) collective-permute-start(bf16[64,128]{1,0:T(8,128)(2,1)} %message.1.refs_0_), channel_id=1, source_target_pairs={{0,8},{8,0},{16,24},{24,16},{1,9},{9,1},{17,25},{25,17},{2,10},{10... | collective-permute-start | bytes 49160 | tf_op jit(solution)/shard_map/ppermute | solution.py:624
  4.5 3.9 %collective-permute-start.1 = (bf16[64,128]{1,0:T(8,128)(2,1)}, bf16[64,128]{1,0:T(8,128)(2,1)S(1)}, u32[]{:S(2)}, u32[]{:S(2)}) collective-permute-start(bf16[64,128]{1,0:T(8,128)(2,1)} %message.1.refs_0_), channel_id=1, source_target_pairs={{0,16},{8,24},{16,0},{24,8},{1,17},{9,25},{17,1},{25,9},{2,18},{10... | collective-permute-start | bytes 49160 | tf_op jit(solution)/shard_map/ppermute | solution.py:624
  6.0 4.8 %collective-permute-start.2 = (bf16[64,128]{1,0:T(8,128)(2,1)}, bf16[64,128]{1,0:T(8,128)(2,1)S(1)}, u32[]{:S(2)}, u32[]{:S(2)}) collective-permute-start(bf16[64,128]{1,0:T(8,128)(2,1)} %message.1.refs_0_), channel_id=1, source_target_pairs={{0,24},{8,16},{16,8},{24,0},{1,25},{9,17},{17,9},{25,1},{2,26},{10... | collective-permute-start | bytes 49160 | tf_op jit(solution)/shard_map/ppermute | solution.py:624
  6.0 1.2 %copy-start = (bf16[256,8,2,128]{3,2,1,0:T(2,128)(2,1)S(1)}, bf16[256,8,2,128]{3,2,1,0:T(2,128)(2,1)}, u32[]{:S(2)}) copy-start(bf16[256,8,2,128]{3,2,1,0:T(2,128)(2,1)} %param.6) | copy-start | bytes 3145732
  7.2 3.6 %copy-start.1 = (bf16[64,128]{1,0:T(8,128)(2,1)S(1)}, bf16[64,128]{1,0:T(8,128)(2,1)}, u32[]{:S(2)}) copy-start(bf16[64,128]{1,0:T(8,128)(2,1)} %message.1.refs_0_) | copy-start | bytes 49156
  11.5 12.0 %collective-permute-start.6 = (bf16[2048,128]{1,0:T(8,128)(2,1)S(1)}, bf16[2048,128]{1,0:T(8,128)(2,1)S(1)}, u32[]{:S(2)}, u32[]{:S(2)}) collective-permute-start(bf16[2048,128]{1,0:T(8,128)(2,1)S(1)} %get-tuple-element.17), channel_id=1, source_target_pairs={{0,8},{8,0},{16,24},{24,16},{1,9},{9,1},{17,25},{25,17},{2,10},{10... | collective-permute-start | bytes 1572872 | tf_op jit(solution)/shard_map/ppermute | solution.py:624
  12.1 11.7 %collective-permute-start.7 = (bf16[2048,128]{1,0:T(8,128)(2,1)S(1)}, bf16[2048,128]{1,0:T(8,128)(2,1)S(1)}, u32[]{:S(2)}, u32[]{:S(2)}) collective-permute-start(bf16[2048,128]{1,0:T(8,128)(2,1)S(1)} %get-tuple-element.18), channel_id=1, source_target_pairs={{0,16},{8,24},{16,0},{24,8},{1,17},{9,25},{17,1},{25,9},{2,18},{10... | collective-permute-start | bytes 1572872 | tf_op jit(solution)/shard_map/ppermute | solution.py:624
  12.2 4.8 %collective-permute-start.3 = (bf16[96,128]{1,0:T(8,128)(2,1)S(1)}, bf16[96,128]{1,0:T(8,128)(2,1)S(1)}, u32[]{:S(2)}, u32[]{:S(2)}) collective-permute-start(bf16[96,128]{1,0:T(8,128)(2,1)S(1)} %get-tuple-element.16.one_ref), channel_id=1, source_target_pairs={{0,4},{1,5},{2,6},{3,7},{4,0},{5,1},{6,2},{7,3},{8,12},{9,13},{10,... | collective-permute-start | bytes 73736 | tf_op jit(solution)/shard_map/ppermute | solution.py:624
  17.0 4.2 %copy-start.2 = (s32[2,4,4]{2,1,0:T(4,128)S(1)}, s32[2,4,4]{2,1,0:T(4,128)}, u32[]{:S(2)}) copy-start(s32[2,4,4]{2,1,0:T(4,128)} %live_ref.1) | copy-start | bytes 388
  17.0 4.1 %collective-permute-start.4 = (bf16[192,128]{1,0:T(8,128)(2,1)S(1)}, bf16[192,128]{1,0:T(8,128)(2,1)S(1)}, u32[]{:S(2)}, u32[]{:S(2)}) collective-permute-start(bf16[192,128]{1,0:T(8,128)(2,1)S(1)} %join.3.one_ref), channel_id=1, source_target_pairs={{0,2},{1,3},{2,0},{3,1},{4,6},{5,7},{6,4},{7,5},{8,10},{9,11},{10,... | collective-permute-start | bytes 147464 | tf_op jit(solution)/shard_map/ppermute | solution.py:624
  21.1 1.4 %collective-permute-start.5 = (bf16[384,128]{1,0:T(8,128)(2,1)S(1)}, bf16[384,128]{1,0:T(8,128)(2,1)S(1)}, u32[]{:S(2)}, u32[]{:S(2)}) collective-permute-start(bf16[384,128]{1,0:T(8,128)(2,1)S(1)} %join.4.one_ref), channel_id=1, source_target_pairs={{0,1},{1,0},{2,3},{3,2},{4,5},{5,4},{6,7},{7,6},{8,9},{9,8},{10,11... | collective-permute-start | bytes 294920 | tf_op jit(solution)/shard_map/ppermute | solution.py:624
  22.5 1.3 %copy-start.3 = (f32[2]{0:T(128)S(1)}, f32[2]{0:T(128)}, u32[]{:S(2)}) copy-start(f32[2]{0:T(128)} %tau_ref.1) | copy-start | bytes 28
  27.8 4.3 %collective-permute-start.10 = (f32[64,256]{1,0:T(8,128)S(1)}, f32[64,256]{1,0:T(8,128)S(1)}, u32[]{:S(2)}, u32[]{:S(2)}) collective-permute-start(f32[64,256]{1,0:T(8,128)S(1)} %get-tuple-element.22), channel_id=1, source_target_pairs={{0,16},{8,24},{16,0},{24,8},{1,17},{9,25},{17,1},{25,9},{2,18},{10... | collective-permute-start | bytes 196616 | tf_op jit(solution)/shard_map/ppermute | solution.py:624
  29.2 5.5 %collective-permute-start.8 = (f32[64,256]{1,0:T(8,128)S(1)}, f32[64,256]{1,0:T(8,128)S(1)}, u32[]{:S(2)}, u32[]{:S(2)}) collective-permute-start(f32[64,256]{1,0:T(8,128)S(1)} %get-tuple-element.20), channel_id=1, source_target_pairs={{0,24},{8,16},{16,8},{24,0},{1,25},{9,17},{17,9},{25,1},{2,26},{10... | collective-permute-start | bytes 196616 | tf_op jit(solution)/shard_map/ppermute | solution.py:624
  30.8 4.3 %collective-permute-start.9 = (f32[64,256]{1,0:T(8,128)S(1)}, f32[64,256]{1,0:T(8,128)S(1)}, u32[]{:S(2)}, u32[]{:S(2)}) collective-permute-start(f32[64,256]{1,0:T(8,128)S(1)} %get-tuple-element.21), channel_id=1, source_target_pairs={{0,8},{8,0},{16,24},{24,16},{1,9},{9,1},{17,25},{25,17},{2,10},{10... | collective-permute-start | bytes 196616 | tf_op jit(solution)/shard_map/ppermute | solution.py:624

commit v5 on v4

--- a/solution.py
+++ b/solution.py
@@ -135,6 +135,10 @@
             live_out[at : at + 1, :] = live
     for copy in copies:
         copy.wait()
+
+
+def join_after_kernel(one_ref, two_ref, anchor, out_ref):
+    join_kernel(one_ref, two_ref, out_ref)
 
 
 def join_kernel(one_ref, two_ref, out_ref):
@@ -359,6 +363,10 @@
     return jnp.where(one == two, 1.0, 0.0)
 
 
+def by_distance(refs):
+    return [refs[partners(4).index(distance)] for distance in range(4)]
+
+
 def at_group(group, values):
     found = values[0]
     for place in range(1, len(values)):
@@ -426,7 +434,24 @@
         ]
 
 
-def message_kernel(message, virt_hbm, occ_hbm, col_hbm, out_hbm, out_ref, occ_ref, col_ref, sem):
+class Chosen:
+    def __init__(self, ref):
+        values = [ref[0:1, place : place + 1] for place in range(20)]
+        self.own, self.got = values[0:2], values[2:4]
+        self.pairs = [values[4 + 4 * block : 8 + 4 * block] for block in range(4)]
+
+    @staticmethod
+    def leave(choice, ref):
+        values = [*choice.own, *choice.got] + [value for row in choice.pairs for value in row]
+        lane = iota(ref.shape, 1)
+        total = jnp.zeros(ref.shape, F32)
+        for place, value in enumerate(values):
+            total = jnp.where(lane == place, value, total)
+        ref[...] = total
+
+
+def message_kernel(message, virt_hbm, occ_hbm, col_hbm, *refs):
+    *outs, out_ref, occ_ref, col_ref, sem = refs
     copies = [
         pltpu.make_async_copy(virt_hbm, out_ref.at[message.virt], sem.at[0]),
         pltpu.make_async_copy(occ_hbm, occ_ref, sem.at[1]),
@@ -445,9 +470,11 @@
         here = jnp.logical_and(row == 0, lane == slot)
         value = jnp.where(here, col_ref[0, slot].astype(F32), value)
     out_ref[message.list, :] = value.astype(BF16)
-    copy = pltpu.make_async_copy(out_ref, out_hbm, sem.at[3])
-    copy.start()
-    copy.wait()
+    copies = [pltpu.make_async_copy(out_ref, out, sem.at[3 + at]) for at, out in enumerate(outs)]
+    for copy in copies:
+        copy.start()
+    for copy in copies:
+        copy.wait()
 
 
 def own_kernel(rows_dev, steps, b_ref, *outs):
@@ -466,10 +493,15 @@
 
 
 def send_kernel(message, *refs):
-    messages, (own0, own1, to_x, to_y, virt_out) = refs[:4], refs[4:]
+    messages, (own0, own1), (virt_out, chosen, *outs) = by_distance(refs[2:6]), refs[:2], refs[6:]
     choice = Choice(message, messages)
-    to_x[...] = jnp.where(choice.slot_x > 0.5, own1[...], own0[...])
-    to_y[...] = jnp.where(choice.slot_y > 0.5, own1[...], own0[...])
+    Chosen.leave(choice, chosen)
+    at = 0
+    for to_x, to_y in zip(outs[0::2], outs[1::2]):
+        here = slice(at, at + to_x.shape[0])
+        to_x[...] = jnp.where(choice.slot_x > 0.5, own1[here, :], own0[here, :])
+        to_y[...] = jnp.where(choice.slot_y > 0.5, own1[here, :], own0[here, :])
+        at += to_x.shape[0]
     me = lax.axis_index("orb")
     rows = message.virt.stop
     for slot, column in enumerate((choice.own[0], choice.own[1], choice.third)):
@@ -496,10 +528,10 @@
     return order
 
 
-def virt_kernel(sizes, message, *refs):
+def virt_kernel(sizes, *refs):
     aux_count, rows_dev, tau_count = sizes
-    messages, (virt_ref, virt_out) = refs[:4], refs[4:]
-    choice = Choice(message, messages)
+    chosen, virt_ref, virt_out = refs
+    choice = Chosen(chosen)
     aux_me = lax.axis_index("aux")
     tile = virt_ref.shape[1]
     part = tile // aux_count
@@ -523,8 +555,8 @@
 
 def mix_kernel(sizes, message, live_ref, *refs):
     aux_count, rows_dev, tau_count = sizes
-    messages, mix_out = refs[:4], refs[4]
-    choice = Choice(message, messages)
+    messages, chosen, mix_out = by_distance(refs[:4]), refs[4], refs[5]
+    choice = Chosen(chosen)
     me = lax.axis_index("orb")
     tile = messages[0].shape[1]
     rows = 4 * rows_dev
@@ -554,40 +586,60 @@
             mix_out[at : at + half_rows, :] = jnp.where(keep, spread[at : at + half_rows], 0.0).astype(BF16)
 
 
-def work_kernel(rows_dev, tau_count, steps, scale, tau_ref, mix_ref, virt_ref, *refs):
-    blocks, outs, (occ_ref, vir_ref) = refs[:4], refs[4:8], refs[8:]
+def four_products(rows_dev, tau_count, first, steps, owns, got, mix_ref, virt_ref, occ_ref, vir_ref):
     rows = 4 * rows_dev
     half_rows = rows_dev * SUB
-    tile = blocks[0].shape[1]
+    tile = owns[0].shape[1]
+    blocks = [(own, first) for own in owns] + [(block, 0) for block in got]
 
     def step(index, carry):
         here = pl.ds(pl.multiple_of(index * PAIR, PAIR), PAIR)
-        halves = []
-        for half in range(2):
-            at = pl.multiple_of((index * 2 + half) * half_rows, half_rows)
-            halves.append(jnp.concatenate([block[pl.ds(at, half_rows), :] for block in blocks], 0))
-        occ = dot(mix_ref[...], jnp.concatenate(halves, 1))
-        occ = [occ[:, half * tile : (half + 1) * tile].reshape(tau_count * rows, SUB, tile) for half in range(2)]
-        occ = jnp.concatenate(occ, 1).astype(BF16)
-        for row in range(tau_count * rows):
-            occ_ref[here, row * tile : (row + 1) * tile] = occ[row]
-        for group, block in enumerate(blocks):
-            both = block[pl.ds(pl.multiple_of(index * 2 * half_rows, half_rows), 2 * half_rows), :]
-            vir = dot(both, virt_ref[group]).reshape(2, rows_dev, SUB, tau_count * tile)
-            vir = jnp.concatenate([vir[0], vir[1]], 1).astype(BF16)
-            for moment in range(tau_count):
-                for row in range(rows_dev):
-                    at = (moment * rows + group * rows_dev + row) * tile
-                    vir_ref[here, at : at + tile] = vir[row, :, moment * tile : (moment + 1) * tile]
+        if occ_ref is not None:
+            halves = []
+            for half in range(2):
+                halves.append(jnp.concatenate([
+                    block[pl.ds(pl.multiple_of(((index + shift) * 2 + half) * half_rows, half_rows), half_rows), :]
+                    for block, shift in blocks
+                ], 0))
+            occ = dot(mix_ref[...], jnp.concatenate(halves, 1))
+            occ = [occ[:, half * tile : (half + 1) * tile].reshape(tau_count * rows, SUB, tile) for half in range(2)]
+            occ = jnp.concatenate(occ, 1).astype(BF16)
+            for row in range(tau_count * rows):
+                occ_ref[here, row * tile : (row + 1) * tile] = occ[row]
+        if vir_ref is not None:
+            for group, (block, shift) in enumerate(blocks):
+                at = pl.multiple_of((index + shift) * 2 * half_rows, half_rows)
+                vir = dot(block[pl.ds(at, 2 * half_rows), :], virt_ref[group])
+                vir = vir.reshape(2, rows_dev, SUB, tau_count * tile)
+                vir = jnp.concatenate([vir[0], vir[1]], 1).astype(BF16)
+                for moment in range(tau_count):
+                    for row in range(rows_dev):
+                        at = (moment * rows + group * rows_dev + row) * tile
+                        vir_ref[here, at : at + tile] = vir[row, :, moment * tile : (moment + 1) * tile]
         return carry
 
     lax.fori_loop(0, steps, step, 0, unroll=min(steps, UNROLL))
-    depth = rows * tile
+
+
+def early_occ_kernel(rows_dev, tau_count, steps, mix_ref, own0, own1, from_x, from_y, occ_out):
+    four_products(rows_dev, tau_count, 0, steps, [own0, own1], [from_x, from_y], mix_ref, None, occ_out, None)
+
+
+def early_vir_kernel(rows_dev, tau_count, steps, virt_ref, own0, own1, from_x, from_y, vir_out):
+    four_products(rows_dev, tau_count, 0, steps, [own0, own1], [from_x, from_y], None, virt_ref, None, vir_out)
+
+
+def late_kernel(rows_dev, tau_count, first, steps, scale, tau_ref, mix_ref, virt_ref, *refs):
+    (own0, own1, from_x, from_y, occ_early, vir_early), outs, (occ_ref, vir_ref) = refs[:6], refs[6:10], refs[10:]
+    four_products(rows_dev, tau_count, first, steps, [own0, own1], [from_x, from_y], mix_ref, virt_ref, occ_ref, vir_ref)
+    depth = 4 * rows_dev * own0.shape[1]
     chi = None
     for moment in range(tau_count):
         here = slice(moment * depth, (moment + 1) * depth)
         term = lax.dot_general(
-            occ_ref[:, here], vir_ref[:, here], (((1,), (1,)), ((), ())), preferred_element_type=F32
+            jnp.concatenate([occ_early[:, here], occ_ref[:, here]], 0),
+            jnp.concatenate([vir_early[:, here], vir_ref[:, here]], 0),
+            (((1,), (1,)), ((), ())), preferred_element_type=F32,
         ) * tau_ref[moment]
         chi = term if chi is None else chi + term
     chi = chi * scale
@@ -614,10 +666,11 @@
     vmem = pl.BlockSpec(memory_space=pltpu.VMEM)
     hbm = pl.BlockSpec(memory_space=pl.ANY)
 
-    def call(kernel, name, out_shape, in_specs, scratch, limit, out_spec=vmem):
+    def call(kernel, name, out_shape, in_specs, scratch, limit, out_spec=vmem, flops=0):
         return pl.pallas_call(
             kernel, out_shape=out_shape, in_specs=in_specs, out_specs=[out_spec] * len(out_shape),
             scratch_shapes=scratch, compiler_params=pltpu.CompilerParams(vmem_limit_bytes=limit << 20), name=name,
+            cost_estimate=pl.CostEstimate(flops=flops, bytes_accessed=0, transcendentals=0) if flops else None,
         )
 
     def xor(value, axis, distance):
@@ -631,40 +684,54 @@
     occ = g_occ.reshape(tau_count * rows_dev, -1)
     message = Message(virt.shape[0], occ.shape[0])
     dma = pltpu.SemaphoreType.DMA
-    (sent,) = call(
-        functools.partial(message_kernel, message), "message", [half(message.rows, tile)], [hbm] * 3,
+    sent = call(
+        functools.partial(message_kernel, message), "message", [half(message.rows, tile)] * orb_count, [hbm] * 3,
         [
             pltpu.VMEM((message.rows, tile), BF16), pltpu.VMEM(occ.shape, BF16),
-            pltpu.SMEM(col_blocks.shape, jnp.int32), dma((4,)),
-        ], 60, hbm,
+            pltpu.SMEM(col_blocks.shape, jnp.int32), dma((3 + orb_count,)),
+        ], 60, hbm, 10**10,
     )(virt, occ, col_blocks)
-    came = {distance: xor(sent, "orb", distance) for distance in partners(orb_count)[1:]}
-    messages = [sent] + [came[distance] for distance in range(1, orb_count)]
+    came = {distance: xor(part, "orb", distance) for distance, part in zip(partners(orb_count)[1:], sent[1:])}
+    messages = [sent[0]] + [came[distance] for distance in partners(orb_count)[1:]]
     block = half(aux_dev * rows_dev, tile)
-    owns = call(functools.partial(own_kernel, rows_dev, steps), "own", [block] * 2, [vmem], [], 6)(flat)
-    to_x, to_y, virt = call(
+    owns = call(functools.partial(own_kernel, rows_dev, steps), "own", [block] * 2, [vmem], [], 6, vmem, 10**10)(flat)
+    early = steps * 12 // 16
+    chunks = (early, steps - early)
+    virt, chosen, *sends = call(
         functools.partial(send_kernel, message), "send",
-        [block] * 2 + [half(3 * message.virt.stop, tile)], [vmem] * 6, [], 6,
-    )(*messages, *owns)
-    from_x, from_y = xor(to_x, "orb", 1), xor(to_y, "orb", 2)
-    for distance in aux_steps(aux_count):
-        virt = call(join_kernel, "join", [half(2 * virt.shape[0], tile)], [vmem] * 2, [], 4)(
-            virt, xor(virt, "aux", distance)
-        )[0]
+        [half(3 * message.virt.stop, tile), jax.ShapeDtypeStruct((8, tile), F32)]
+        + [half(count * PAIR * rows_dev, tile) for count in chunks for _ in range(2)],
+        [vmem] * 6, [], 6, vmem, 10**10,
+    )(*owns, *messages)
+    got = [(xor(to_x, "orb", 1), xor(to_y, "orb", 2)) for to_x, to_y in zip(sends[0::2], sends[1::2])]
     (mix,) = call(
         functools.partial(mix_kernel, sizes, message), "mix",
-        [half(tau_count * rows * SUB, rows * SUB)], [smem] + [vmem] * 4, [], 8,
-    )(occ_live, *messages)
+        [half(tau_count * rows * SUB, rows * SUB)], [smem] + [vmem] * 5, [], 8,
+    )(occ_live, *messages, chosen)
+    wide = tau_count * rows * tile
+    first = half(early * PAIR, wide)
+    (occ_early,) = call(
+        functools.partial(early_occ_kernel, rows_dev, tau_count, early), "occ", [first], [vmem] * 5, [], 6
+    )(mix, *owns, *got[0])
+    distances = aux_steps(aux_count)
+    for number, distance in enumerate(distances):
+        pair, other = half(2 * virt.shape[0], tile), xor(virt, "aux", distance)
+        anchor = {0: mix, len(distances) - 1: occ_early}.get(number)
+        if anchor is None:
+            (virt,) = call(join_kernel, "join", [pair], [vmem] * 2, [], 4)(virt, other)
+        else:
+            (virt,) = call(join_after_kernel, "join", [pair], [vmem] * 2 + [hbm], [], 4)(virt, other, anchor)
     (virt,) = call(
-        functools.partial(virt_kernel, sizes, message), "virt",
-        [half(4, tile, tau_count * tile)], [vmem] * 5, [], 8,
-    )(*messages, virt)
-    wide = tau_count * rows * tile
+        functools.partial(virt_kernel, sizes), "virt", [half(4, tile, tau_count * tile)], [vmem] * 2, [], 8
+    )(chosen, virt)
+    (vir_early,) = call(
+        functools.partial(early_vir_kernel, rows_dev, tau_count, early), "vir", [first], [vmem] * 5, [], 6
+    )(virt, *owns, *got[0])
     shares = call(
-        functools.partial(work_kernel, rows_dev, tau_count, steps, scale), "work",
-        [jax.ShapeDtypeStruct((share_rows, aux_dev), F32)] * orb_count, [smem] + [vmem] * 6,
-        [pltpu.VMEM((aux_dev, wide), BF16), pltpu.VMEM((aux_dev, wide), BF16)], 24,
-    )(tau_weight, mix, virt, *owns, from_x, from_y)
+        functools.partial(late_kernel, rows_dev, tau_count, early, steps - early, scale), "late",
+        [jax.ShapeDtypeStruct((share_rows, aux_dev), F32)] * orb_count, [smem] + [vmem] * 8,
+        [pltpu.VMEM(((steps - early) * PAIR, wide), BF16), pltpu.VMEM(((steps - early) * PAIR, wide), BF16)], 16,
+    )(tau_weight, mix, virt, *owns, *got[1], occ_early, vir_early)
     total = shares[0]
     for distance, share in zip(partners(orb_count)[1:], shares[1:]):
         total = total + xor(share, "orb", distance)

time: 36 us -> 35.1 us (0.975)
  starting transfers between devices: 13.8 us -> 16.5 us
  waiting for transfers between devices: 11.4 us -> 8.78 us
  local copies, waits for them, and re-layouts: 1.24 us -> 0.02 us
    ppermute x11 -> x13, starting transfers between devices: 13.8 us -> 16.5 us  [xor(): lax.ppermute(value, axis, [(i, i ^ distance) for i in range(lax.axis_size...]
    ppermute x11 -> x13, waiting for transfers between devices: 11.4 us -> 8.78 us  [xor(): lax.ppermute(value, axis, [(i, i ^ distance) for i in range(lax.axis_size...]
    unnamed x8, local copies, waits for them, and re-layouts: 1.24 us -> 0.02 us
    pallas_call x6 -> x8, Pallas kernels: 5.37 us -> 5.68 us  [the longest x1 2.48 us: on_device_square(): call(functools.partial(late_kernel, rows_dev, tau_count, early, steps - e...]
  transfers between devices with their start and end apart: 11 -> 13, of which waited for: 10 -> 9; matrix products, arithmetic and copies ran while one was open for 0% -> 0% of each run, Pallas kernels for 7% -> 12%
where the time goes in v5:
time: 35.1 us; the launch traced here: 35 us
  starting transfers between devices  16.5 us (47%)
  Pallas kernels  8.88 us (25%)
  waiting for transfers between devices  8.78 us (25%)
  other arithmetic  0.65 us (2%)
    ppermute x13, starting transfers between devices, xor(): lax.ppermute(value, axis, [(i, i ^ distance) for i in range(lax.axis_size...  16.5 us
    ppermute x13, waiting for transfers between devices, xor(): lax.ppermute(value, axis, [(i, i ^ distance) for i in range(lax.axis_size...  8.78 us
    pallas_call x1, Pallas kernels, on_device_square(): call(functools.partial(late_kernel, rows_dev, tau_count, early, steps - e...  2.48 us
    pallas_call x1, Pallas kernels, on_device_square(): call(functools.partial(message_kernel, message), 'message', [half(message...  1.49 us
    pallas_call x1, Pallas kernels, on_device_square(): call(functools.partial(mix_kernel, sizes, message), 'mix', [half(tau_coun...  1.01 us
    pallas_call x1, Pallas kernels, on_device_square(): call(functools.partial(early_occ_kernel, rows_dev, tau_count, early), 'oc...  0.98 us
    pallas_call x1, Pallas kernels, on_device_square(): call(functools.partial(early_vir_kernel, rows_dev, tau_count, early), 'vi...  0.97 us
  transfers between devices with their start and end apart: 13, of which 9 were waited for; matrix products, arithmetic and copies ran while one was open for 0% of the time, Pallas kernels for 12%

profile of v5, /device:TPU:0, one launch (start us, length us, event | category | flops | bytes accessed | tf_op | source)
XLA Modules:
  0.0 35.0 jit_solution(17008818484890594391)
XLA Ops:
  0.0 0.0 copy-start.3
  0.0 1.5 %message.1 = (bf16[64,128]{1,0:T(8,128)(2,1)}, bf16[64,128]{1,0:T(8,128)(2,1)}, bf16[64,128]{1,0:T(8,128)(2,1)}, bf16[64,128]{1,0:T(8,128)(2,1)}) custom-call(bf16[32,128]{1,0:T(8,128)(2,1)} %bitcast.4, bf16[16,32]{1,0:T(8,128)(2,1)} %bitcast.5, s32[1,2]{1,0:T(1,128)} %col_hbm.1), custom_call_target="tpu_custom_call" | custom-call | flops 10000000000 | tf_op jit(solution)/shard_map/message/pallas_call | solution.py:687
  1.5 4.0 %collective-permute-start = (bf16[64,128]{1,0:T(8,128)(2,1)}, bf16[64,128]{1,0:T(8,128)(2,1)S(1)}, u32[]{:S(2)}, u32[]{:S(2)}) collective-permute-start(bf16[64,128]{1,0:T(8,128)(2,1)} %get-tuple-element.22), channel_id=1, source_target_pairs={{0,24},{8,16},{16,8},{24,0},{1,25},{9,17},{17,9},{25,1},{2,26},{10... | collective-permute-start | bytes 49160 | tf_op jit(solution)/shard_map/ppermute | solution.py:677
  5.5 0.5 %collective-permute-start.1 = (bf16[64,128]{1,0:T(8,128)(2,1)}, bf16[64,128]{1,0:T(8,128)(2,1)S(1)}, u32[]{:S(2)}, u32[]{:S(2)}) collective-permute-start(bf16[64,128]{1,0:T(8,128)(2,1)} %get-tuple-element.23), channel_id=1, source_target_pairs={{0,8},{8,0},{16,24},{24,16},{1,9},{9,1},{17,25},{25,17},{2,10},{10... | collective-permute-start | bytes 49160 | tf_op jit(solution)/shard_map/ppermute | solution.py:677
  6.0 0.1 collective-permute-start.2
  6.1 0.0 copy-done.3
  6.1 0.0 copy-start
  6.1 0.7 %own.1 = (bf16[2048,128]{1,0:T(8,128)(2,1)S(1)}, bf16[2048,128]{1,0:T(8,128)(2,1)S(1)}) custom-call(bf16[4096,128]{1,0:T(8,128)(2,1)S(1)} %bitcast.3), custom_call_target="tpu_custom_call" | custom-call | flops 10000000000 | tf_op jit(solution)/shard_map/own/pallas_call | solution.py:697
  6.8 0.6 %collective-permute-done.refs_3_.refs_1_ = bf16[64,128]{1,0:T(8,128)(2,1)S(1)} collective-permute-done((bf16[64,128]{1,0:T(8,128)(2,1)}, bf16[64,128]{1,0:T(8,128)(2,1)S(1)}, u32[]{:S(2)}, u32[]{:S(2)}) %collective-permute-start) | collective-permute-done | bytes 16416 | tf_op jit(solution)/shard_map/ppermute | solution.py:677
  7.4 2.0 %collective-permute-done.1.refs_4_.refs_2_ = bf16[64,128]{1,0:T(8,128)(2,1)S(1)} collective-permute-done((bf16[64,128]{1,0:T(8,128)(2,1)}, bf16[64,128]{1,0:T(8,128)(2,1)S(1)}, u32[]{:S(2)}, u32[]{:S(2)}) %collective-permute-start.1) | collective-permute-done | bytes 16416 | tf_op jit(solution)/shard_map/ppermute | solution.py:677
  9.4 0.5 %collective-permute-done.2.refs_5_.refs_3_ = bf16[64,128]{1,0:T(8,128)(2,1)S(1)} collective-permute-done((bf16[64,128]{1,0:T(8,128)(2,1)}, bf16[64,128]{1,0:T(8,128)(2,1)S(1)}, u32[]{:S(2)}, u32[]{:S(2)}) %collective-permute-start.2) | collective-permute-done | bytes 16416 | tf_op jit(solution)/shard_map/ppermute | solution.py:677
  9.9 0.0 copy-done
  9.9 0.0 copy-start.1
  9.9 0.7 %send.1 = (bf16[96,128]{1,0:T(8,128)(2,1)S(1)}, f32[8,128]{1,0:T(8,128)S(1)}, bf16[1536,128]{1,0:T(8,128)(2,1)S(1)}, bf16[1536,128]{1,0:T(8,128)(2,1)S(1)}, bf16...) custom-call(bf16[2048,128]{1,0:T(8,128)(2,1)S(1)} %get-tuple-element.25.refs_0_.own0, ...), custom_call_target="tpu_custom_call" | custom-call | flops 10000000000 | tf_op jit(solution)/shard_map/send/pallas_call | solution.py:700
  10.6 1.6 %collective-permute-start.6 = (bf16[1536,128]{1,0:T(8,128)(2,1)S(1)}, bf16[1536,128]{1,0:T(8,128)(2,1)S(1)}, u32[]{:S(2)}, u32[]{:S(2)}) collective-permute-start(bf16[1536,128]{1,0:T(8,128)(2,1)S(1)} %get-tuple-element.29), channel_id=1, source_target_pairs={{0,8},{8,0},{16,24},{24,16},{1,9},{9,1},{17,25},{25,17},{2,10},{10... | collective-permute-start | bytes 1179656 | tf_op jit(solution)/shard_map/ppermute | solution.py:677
  12.2 0.5 %collective-permute-start.7 = (bf16[1536,128]{1,0:T(8,128)(2,1)S(1)}, bf16[1536,128]{1,0:T(8,128)(2,1)S(1)}, u32[]{:S(2)}, u32[]{:S(2)}) collective-permute-start(bf16[1536,128]{1,0:T(8,128)(2,1)S(1)} %get-tuple-element.30), channel_id=1, source_target_pairs={{0,16},{8,24},{16,0},{24,8},{1,17},{9,25},{17,1},{25,9},{2,18},{10... | collective-permute-start | bytes 1179656 | tf_op jit(solution)/shard_map/ppermute | solution.py:677
  12.7 2.6 %collective-permute-start.3 = (bf16[96,128]{1,0:T(8,128)(2,1)S(1)}, bf16[96,128]{1,0:T(8,128)(2,1)S(1)}, u32[]{:S(2)}, u32[]{:S(2)}) collective-permute-start(bf16[96,128]{1,0:T(8,128)(2,1)S(1)} %get-tuple-element.28.one_ref), channel_id=1, source_target_pairs={{0,4},{1,5},{2,6},{3,7},{4,0},{5,1},{6,2},{7,3},{8,12},{9,13},{10,... | collective-permute-start | bytes 73736 | tf_op jit(solution)/shard_map/ppermute | solution.py:677
  15.3 0.0 copy-done.1
  15.3 1.0 %mix.1.anchor.mix_ref = bf16[512,256]{1,0:T(8,128)(2,1)S(1)} custom-call(s32[2,4,4]{2,1,0:T(4,128)S(1)} %copy-done.1, bf16[64,128]{1,0:T(8,128)(2,1)S(1)} %copy-done, bf16[64,128]{1,0:T(8,128)(2,1)S(1)} %collective-permute-done.refs_3_.refs_1_, bf16[64,128]{1,0:T(8,128)(2,1)S(1)} %collective-permute-done.1.refs_4_.refs_2_, ...), custom_call_target="tpu_custom_call" | custom-call | tf_op jit(solution)/shard_map/mix/pallas_call | solution.py:707
  16.3 1.1 %collective-permute-done.3.two_ref = bf16[96,128]{1,0:T(8,128)(2,1)S(1)} collective-permute-done((bf16[96,128]{1,0:T(8,128)(2,1)S(1)}, bf16[96,128]{1,0:T(8,128)(2,1)S(1)}, u32[]{:S(2)}, u32[]{:S(2)}) %collective-permute-start.3) | collective-permute-done | bytes 24608 | tf_op jit(solution)/shard_map/ppermute | solution.py:677
  17.4 1.6 %collective-permute-start.4 = (bf16[192,128]{1,0:T(8,128)(2,1)S(1)}, bf16[192,128]{1,0:T(8,128)(2,1)S(1)}, u32[]{:S(2)}, u32[]{:S(2)}) collective-permute-start(bf16[192,128]{1,0:T(8,128)(2,1)S(1)} %join.3.one_ref), channel_id=1, source_target_pairs={{0,2},{1,3},{2,0},{3,1},{4,6},{5,7},{6,4},{7,5},{8,10},{9,11},{10,... | collective-permute-start | bytes 147464 | tf_op jit(solution)/shard_map/ppermute | solution.py:677
  19.0 0.5 %collective-permute-start.8 = (bf16[512,128]{1,0:T(8,128)(2,1)S(1)}, bf16[512,128]{1,0:T(8,128)(2,1)S(1)}, u32[]{:S(2)}, u32[]{:S(2)}) collective-permute-start(bf16[512,128]{1,0:T(8,128)(2,1)S(1)} %get-tuple-element.31), channel_id=1, source_target_pairs={{0,8},{8,0},{16,24},{24,16},{1,9},{9,1},{17,25},{25,17},{2,10},{10... | collective-permute-start | bytes 393224 | tf_op jit(solution)/shard_map/ppermute | solution.py:677
  19.5 1.5 %collective-permute-start.9 = (bf16[512,128]{1,0:T(8,128)(2,1)S(1)}, bf16[512,128]{1,0:T(8,128)(2,1)S(1)}, u32[]{:S(2)}, u32[]{:S(2)}) collective-permute-start(bf16[512,128]{1,0:T(8,128)(2,1)S(1)} %get-tuple-element.32), channel_id=1, source_target_pairs={{0,16},{8,24},{16,0},{24,8},{1,17},{9,25},{17,1},{25,9},{2,18},{10... | collective-permute-start | bytes 393224 | tf_op jit(solution)/shard_map/ppermute | solution.py:677
  21.1 0.5 %collective-permute-done.4.two_ref = bf16[192,128]{1,0:T(8,128)(2,1)S(1)} collective-permute-done((bf16[192,128]{1,0:T(8,128)(2,1)S(1)}, bf16[192,128]{1,0:T(8,128)(2,1)S(1)}, u32[]{:S(2)}, u32[]{:S(2)}) %collective-permute-start.4) | collective-permute-done | bytes 49184 | tf_op jit(solution)/shard_map/ppermute | solution.py:677
  21.5 0.1 collective-permute-start.5
  21.6 0.0 collective-permute-done.6.from_x
  21.6 0.8 %collective-permute-done.7.from_y = bf16[1536,128]{1,0:T(8,128)(2,1)S(1)} collective-permute-done((bf16[1536,128]{1,0:T(8,128)(2,1)S(1)}, bf16[1536,128]{1,0:T(8,128)(2,1)S(1)}, u32[]{:S(2)}, u32[]{:S(2)}) %collective-permute-start.7) | collective-permute-done | bytes 393248 | tf_op jit(solution)/shard_map/ppermute | solution.py:677
  22.5 1.0 %occ.1.anchor.refs_4_ = bf16[192,8192]{1,0:T(8,128)(2,1)S(1)} custom-call(bf16[512,256]{1,0:T(8,128)(2,1)S(1)} %mix.1.anchor.mix_ref, bf16[2048,128]{1,0:T(8,128)(2,1)S(1)} %get-tuple-element.25.refs_0_.own0, bf16[2048,128]{1,0:T(8,128)(2,1)S(1)} %get-tuple-element.26.refs_1_.own1, bf16[1536,128]{1,0:T(8,128)(2,1)S(1)} %collective-permute-done.6.from_x, ...), custom_call_target="tpu_custom_call" | custom-call | tf_op jit(solution)/shard_map/occ/pallas_call | solution.py:713
  23.5 0.0 collective-permute-done.5.two_ref
  23.5 0.0 copy-start.2
  23.5 0.5 %virt.1.virt_ref = bf16[4,128,256]{2,1,0:T(8,128)(2,1)S(1)} custom-call(f32[8,128]{1,0:T(8,128)S(1)} %get-tuple-element.27.refs_4_.refs_0_, bf16[768,128]{1,0:T(8,128)(2,1)S(1)} %join.5.refs_1_), custom_call_target="tpu_custom_call" | custom-call | tf_op jit(solution)/shard_map/virt/pallas_call | solution.py:724
  24.1 1.0 %vir.1.refs_5_ = bf16[192,8192]{1,0:T(8,128)(2,1)S(1)} custom-call(bf16[4,128,256]{2,1,0:T(8,128)(2,1)S(1)} %virt.1.virt_ref, bf16[2048,128]{1,0:T(8,128)(2,1)S(1)} %get-tuple-element.25.refs_0_.own0, bf16[2048,128]{1,0:T(8,128)(2,1)S(1)} %get-tuple-element.26.refs_1_.own1, bf16[1536,128]{1,0:T(8,128)(2,1)S(1)} %collective-permute-done.6.from_x, ...), custom_call_target="tpu_custom_call" | custom-call | tf_op jit(solution)/shard_map/vir/pallas_call | solution.py:727
  25.0 0.0 collective-permute-done.8.refs_2_
  25.0 0.0 collective-permute-done.9.refs_3_
  25.1 0.0 copy-done.2
  25.1 2.5 %late.1 = (f32[64,256]{1,0:T(8,128)S(1)}, f32[64,256]{1,0:T(8,128)S(1)}, f32[64,256]{1,0:T(8,128)S(1)}, f32[64,256]{1,0:T(8,128)S(1)}) custom-call(f32[2]{0:T(128)S(1)} %copy-done.2, bf16[512,256]{1,0:T(8,128)(2,1)S(1)} %mix.1.anchor.mix_ref, bf16[4,128,256]{2,1,0:T(8,128)(2,1)S(1)} %virt.1.virt_ref, bf16[2048,128]{1,0:T(8,128)(2,1)S(1)} %get-tuple-element.25.refs_0_.own0, ...), custom_call_target="tpu_custom_call" | custom-call | tf_op jit(solution)/shard_map/late/pallas_call | solution.py:730
  27.5 2.0 %collective-permute-start.10 = (f32[64,256]{1,0:T(8,128)S(1)}, f32[64,256]{1,0:T(8,128)S(1)}, u32[]{:S(2)}, u32[]{:S(2)}) collective-permute-start(f32[64,256]{1,0:T(8,128)S(1)} %get-tuple-element.34), channel_id=1, source_target_pairs={{0,24},{8,16},{16,8},{24,0},{1,25},{9,17},{17,9},{25,1},{2,26},{10... | collective-permute-start | bytes 196616 | tf_op jit(solution)/shard_map/ppermute | solution.py:677
  29.5 0.5 %collective-permute-start.11 = (f32[64,256]{1,0:T(8,128)S(1)}, f32[64,256]{1,0:T(8,128)S(1)}, u32[]{:S(2)}, u32[]{:S(2)}) collective-permute-start(f32[64,256]{1,0:T(8,128)S(1)} %get-tuple-element.35), channel_id=1, source_target_pairs={{0,8},{8,0},{16,24},{24,16},{1,9},{9,1},{17,25},{25,17},{2,10},{10... | collective-permute-start | bytes 196616 | tf_op jit(solution)/shard_map/ppermute | solution.py:677
  30.0 1.1 %collective-permute-start.12 = (f32[64,256]{1,0:T(8,128)S(1)}, f32[64,256]{1,0:T(8,128)S(1)}, u32[]{:S(2)}, u32[]{:S(2)}) collective-permute-start(f32[64,256]{1,0:T(8,128)S(1)} %get-tuple-element.36), channel_id=1, source_target_pairs={{0,16},{8,24},{16,0},{24,8},{1,17},{9,25},{17,1},{25,9},{2,18},{10... | collective-permute-start | bytes 196616 | tf_op jit(solution)/shard_map/ppermute | solution.py:677
  31.1 1.9 %collective-permute-done.10 = f32[64,256]{1,0:T(8,128)S(1)} collective-permute-done((f32[64,256]{1,0:T(8,128)S(1)}, f32[64,256]{1,0:T(8,128)S(1)}, u32[]{:S(2)}, u32[]{:S(2)}) %collective-permute-start.10) | collective-permute-done | bytes 65568 | tf_op jit(solution)/shard_map/ppermute | solution.py:677
  33.0 0.8 %collective-permute-done.11 = f32[64,256]{1,0:T(8,128)S(1)} collective-permute-done((f32[64,256]{1,0:T(8,128)S(1)}, f32[64,256]{1,0:T(8,128)S(1)}, u32[]{:S(2)}, u32[]{:S(2)}) %collective-permute-start.11) | collective-permute-done | bytes 65568 | tf_op jit(solution)/shard_map/ppermute | solution.py:677
  33.8 0.5 %collective-permute-done.12 = f32[64,256]{1,0:T(8,128)S(1)} collective-permute-done((f32[64,256]{1,0:T(8,128)S(1)}, f32[64,256]{1,0:T(8,128)S(1)}, u32[]{:S(2)}, u32[]{:S(2)}) %collective-permute-start.12) | collective-permute-done | bytes 65568 | tf_op jit(solution)/shard_map/ppermute | solution.py:677
  34.3 0.6 %add_add_fusion = f32[64,256]{1,0:T(8,128)} fusion(f32[64,256]{1,0:T(8,128)S(1)} %collective-permute-done.12, f32[64,256]{1,0:T(8,128)S(1)} %collective-permute-done.11, f32[64,256]{1,0:T(8,128)S(1)} %get-tuple-element.33, f32[64,256]{1,0:T(8,128)S(1)} %collective-permute-done.10), kind=kLoop, calls=%fused_computation | loop fusion | flops 49152 | bytes 327680 | tf_op jit(solution)/shard_map/add | solution.py:737
  (3 shorter events, 0.0 us)
Async XLA Ops:
  0.0 6.1 %copy-start.3 = (bf16[256,8,2,128]{3,2,1,0:T(2,128)(2,1)S(1)}, bf16[256,8,2,128]{3,2,1,0:T(2,128)(2,1)}, u32[]{:S(2)}) copy-start(bf16[256,8,2,128]{3,2,1,0:T(2,128)(2,1)} %param.6) | copy-start | bytes 3145732
  1.5 5.9 %collective-permute-start = (bf16[64,128]{1,0:T(8,128)(2,1)}, bf16[64,128]{1,0:T(8,128)(2,1)S(1)}, u32[]{:S(2)}, u32[]{:S(2)}) collective-permute-start(bf16[64,128]{1,0:T(8,128)(2,1)} %get-tuple-element.22), channel_id=1, source_target_pairs={{0,24},{8,16},{16,8},{24,0},{1,25},{9,17},{17,9},{25,1},{2,26},{10... | collective-permute-start | bytes 49160 | tf_op jit(solution)/shard_map/ppermute | solution.py:677
  5.5 3.9 %collective-permute-start.1 = (bf16[64,128]{1,0:T(8,128)(2,1)}, bf16[64,128]{1,0:T(8,128)(2,1)S(1)}, u32[]{:S(2)}, u32[]{:S(2)}) collective-permute-start(bf16[64,128]{1,0:T(8,128)(2,1)} %get-tuple-element.23), channel_id=1, source_target_pairs={{0,8},{8,0},{16,24},{24,16},{1,9},{9,1},{17,25},{25,17},{2,10},{10... | collective-permute-start | bytes 49160 | tf_op jit(solution)/shard_map/ppermute | solution.py:677
  6.0 3.9 %collective-permute-start.2 = (bf16[64,128]{1,0:T(8,128)(2,1)}, bf16[64,128]{1,0:T(8,128)(2,1)S(1)}, u32[]{:S(2)}, u32[]{:S(2)}) collective-permute-start(bf16[64,128]{1,0:T(8,128)(2,1)} %get-tuple-element.24), channel_id=1, source_target_pairs={{0,16},{8,24},{16,0},{24,8},{1,17},{9,25},{17,1},{25,9},{2,18},{10... | collective-permute-start | bytes 49160 | tf_op jit(solution)/shard_map/ppermute | solution.py:677
  6.1 3.8 %copy-start = (bf16[64,128]{1,0:T(8,128)(2,1)S(1)}, bf16[64,128]{1,0:T(8,128)(2,1)}, u32[]{:S(2)}) copy-start(bf16[64,128]{1,0:T(8,128)(2,1)} %get-tuple-element.21.refs_2_.refs_0_) | copy-start | bytes 49156
  9.9 5.3 %copy-start.1 = (s32[2,4,4]{2,1,0:T(4,128)S(1)}, s32[2,4,4]{2,1,0:T(4,128)}, u32[]{:S(2)}) copy-start(s32[2,4,4]{2,1,0:T(4,128)} %live_ref.1) | copy-start | bytes 388
  10.6 11.0 %collective-permute-start.6 = (bf16[1536,128]{1,0:T(8,128)(2,1)S(1)}, bf16[1536,128]{1,0:T(8,128)(2,1)S(1)}, u32[]{:S(2)}, u32[]{:S(2)}) collective-permute-start(bf16[1536,128]{1,0:T(8,128)(2,1)S(1)} %get-tuple-element.29), channel_id=1, source_target_pairs={{0,8},{8,0},{16,24},{24,16},{1,9},{9,1},{17,25},{25,17},{2,10},{10... | collective-permute-start | bytes 1179656 | tf_op jit(solution)/shard_map/ppermute | solution.py:677
  12.2 10.3 %collective-permute-start.7 = (bf16[1536,128]{1,0:T(8,128)(2,1)S(1)}, bf16[1536,128]{1,0:T(8,128)(2,1)S(1)}, u32[]{:S(2)}, u32[]{:S(2)}) collective-permute-start(bf16[1536,128]{1,0:T(8,128)(2,1)S(1)} %get-tuple-element.30), channel_id=1, source_target_pairs={{0,16},{8,24},{16,0},{24,8},{1,17},{9,25},{17,1},{25,9},{2,18},{10... | collective-permute-start | bytes 1179656 | tf_op jit(solution)/shard_map/ppermute | solution.py:677
  12.7 4.7 %collective-permute-start.3 = (bf16[96,128]{1,0:T(8,128)(2,1)S(1)}, bf16[96,128]{1,0:T(8,128)(2,1)S(1)}, u32[]{:S(2)}, u32[]{:S(2)}) collective-permute-start(bf16[96,128]{1,0:T(8,128)(2,1)S(1)} %get-tuple-element.28.one_ref), channel_id=1, source_target_pairs={{0,4},{1,5},{2,6},{3,7},{4,0},{5,1},{6,2},{7,3},{8,12},{9,13},{10,... | collective-permute-start | bytes 73736 | tf_op jit(solution)/shard_map/ppermute | solution.py:677
  17.4 4.1 %collective-permute-start.4 = (bf16[192,128]{1,0:T(8,128)(2,1)S(1)}, bf16[192,128]{1,0:T(8,128)(2,1)S(1)}, u32[]{:S(2)}, u32[]{:S(2)}) collective-permute-start(bf16[192,128]{1,0:T(8,128)(2,1)S(1)} %join.3.one_ref), channel_id=1, source_target_pairs={{0,2},{1,3},{2,0},{3,1},{4,6},{5,7},{6,4},{7,5},{8,10},{9,11},{10,... | collective-permute-start | bytes 147464 | tf_op jit(solution)/shard_map/ppermute | solution.py:677
  19.0 6.0 %collective-permute-start.8 = (bf16[512,128]{1,0:T(8,128)(2,1)S(1)}, bf16[512,128]{1,0:T(8,128)(2,1)S(1)}, u32[]{:S(2)}, u32[]{:S(2)}) collective-permute-start(bf16[512,128]{1,0:T(8,128)(2,1)S(1)} %get-tuple-element.31), channel_id=1, source_target_pairs={{0,8},{8,0},{16,24},{24,16},{1,9},{9,1},{17,25},{25,17},{2,10},{10... | collective-permute-start | bytes 393224 | tf_op jit(solution)/shard_map/ppermute | solution.py:677
  19.5 5.5 %collective-permute-start.9 = (bf16[512,128]{1,0:T(8,128)(2,1)S(1)}, bf16[512,128]{1,0:T(8,128)(2,1)S(1)}, u32[]{:S(2)}, u32[]{:S(2)}) collective-permute-start(bf16[512,128]{1,0:T(8,128)(2,1)S(1)} %get-tuple-element.32), channel_id=1, source_target_pairs={{0,16},{8,24},{16,0},{24,8},{1,17},{9,25},{17,1},{25,9},{2,18},{10... | collective-permute-start | bytes 393224 | tf_op jit(solution)/shard_map/ppermute | solution.py:677
  21.5 1.9 %collective-permute-start.5 = (bf16[384,128]{1,0:T(8,128)(2,1)S(1)}, bf16[384,128]{1,0:T(8,128)(2,1)S(1)}, u32[]{:S(2)}, u32[]{:S(2)}) collective-permute-start(bf16[384,128]{1,0:T(8,128)(2,1)S(1)} %join.4.one_ref), channel_id=1, source_target_pairs={{0,1},{1,0},{2,3},{3,2},{4,5},{5,4},{6,7},{7,6},{8,9},{9,8},{10,11... | collective-permute-start | bytes 294920 | tf_op jit(solution)/shard_map/ppermute | solution.py:677
  23.5 1.6 %copy-start.2 = (f32[2]{0:T(128)S(1)}, f32[2]{0:T(128)}, u32[]{:S(2)}) copy-start(f32[2]{0:T(128)} %tau_ref.1) | copy-start | bytes 28
  27.5 5.5 %collective-permute-start.10 = (f32[64,256]{1,0:T(8,128)S(1)}, f32[64,256]{1,0:T(8,128)S(1)}, u32[]{:S(2)}, u32[]{:S(2)}) collective-permute-start(f32[64,256]{1,0:T(8,128)S(1)} %get-tuple-element.34), channel_id=1, source_target_pairs={{0,24},{8,16},{16,8},{24,0},{1,25},{9,17},{17,9},{25,1},{2,26},{10... | collective-permute-start | bytes 196616 | tf_op jit(solution)/shard_map/ppermute | solution.py:677
  29.5 4.3 %collective-permute-start.11 = (f32[64,256]{1,0:T(8,128)S(1)}, f32[64,256]{1,0:T(8,128)S(1)}, u32[]{:S(2)}, u32[]{:S(2)}) collective-permute-start(f32[64,256]{1,0:T(8,128)S(1)} %get-tuple-element.35), channel_id=1, source_target_pairs={{0,8},{8,0},{16,24},{24,16},{1,9},{9,1},{17,25},{25,17},{2,10},{10... | collective-permute-start | bytes 196616 | tf_op jit(solution)/shard_map/ppermute | solution.py:677
  30.0 4.3 %collective-permute-start.12 = (f32[64,256]{1,0:T(8,128)S(1)}, f32[64,256]{1,0:T(8,128)S(1)}, u32[]{:S(2)}, u32[]{:S(2)}) collective-permute-start(f32[64,256]{1,0:T(8,128)S(1)} %get-tuple-element.36), channel_id=1, source_target_pairs={{0,16},{8,24},{16,0},{24,8},{1,17},{9,25},{17,1},{25,9},{2,18},{10... | collective-permute-start | bytes 196616 | tf_op jit(solution)/shard_map/ppermute | solution.py:677

commit v6 on v5

--- a/solution.py
+++ b/solution.py
@@ -586,6 +586,25 @@
             mix_out[at : at + half_rows, :] = jnp.where(keep, spread[at : at + half_rows], 0.0).astype(BF16)
 
 
+def virtual_products(rows_dev, tau_count, first, steps, blocks, virts, vir_ref):
+    half_rows = rows_dev * SUB
+    tile = blocks[0].shape[1]
+
+    def step(index, carry):
+        here = pl.ds(pl.multiple_of(index * PAIR, PAIR), PAIR)
+        for group, (block, virt) in enumerate(zip(blocks, virts)):
+            at = pl.multiple_of((index + first) * 2 * half_rows, half_rows)
+            vir = dot(block[pl.ds(at, 2 * half_rows), :], virt).reshape(2, rows_dev, SUB, tau_count * tile)
+            vir = jnp.concatenate([vir[0], vir[1]], 1).astype(BF16)
+            for moment in range(tau_count):
+                for row in range(rows_dev):
+                    at = ((moment * len(blocks) + group) * rows_dev + row) * tile
+                    vir_ref[here, at : at + tile] = vir[row, :, moment * tile : (moment + 1) * tile]
+        return carry
+
+    lax.fori_loop(0, steps, step, 0, unroll=min(steps, UNROLL))
+
+
 def four_products(rows_dev, tau_count, first, steps, owns, got, mix_ref, virt_ref, occ_ref, vir_ref):
     rows = 4 * rows_dev
     half_rows = rows_dev * SUB
@@ -625,20 +644,26 @@
     four_products(rows_dev, tau_count, 0, steps, [own0, own1], [from_x, from_y], mix_ref, None, occ_out, None)
 
 
-def early_vir_kernel(rows_dev, tau_count, steps, virt_ref, own0, own1, from_x, from_y, vir_out):
+def early_vir_kernel(rows_dev, tau_count, steps, late_steps, virt_ref, own0, own1, from_x, from_y, vir_out, own_out):
+    virts = [virt_ref[0], virt_ref[1]]
     four_products(rows_dev, tau_count, 0, steps, [own0, own1], [from_x, from_y], None, virt_ref, None, vir_out)
+    virtual_products(rows_dev, tau_count, steps, late_steps, [own0, own1], virts, own_out)
 
 
 def late_kernel(rows_dev, tau_count, first, steps, scale, tau_ref, mix_ref, virt_ref, *refs):
-    (own0, own1, from_x, from_y, occ_early, vir_early), outs, (occ_ref, vir_ref) = refs[:6], refs[6:10], refs[10:]
-    four_products(rows_dev, tau_count, first, steps, [own0, own1], [from_x, from_y], mix_ref, virt_ref, occ_ref, vir_ref)
+    (own0, own1, from_x, from_y, occ_early, vir_early, vir_own) = refs[:7]
+    outs, (occ_ref, vir_ref) = refs[7:11], refs[11:]
+    four_products(rows_dev, tau_count, first, steps, [own0, own1], [from_x, from_y], mix_ref, None, occ_ref, None)
+    virtual_products(rows_dev, tau_count, 0, steps, [from_x, from_y], [virt_ref[2], virt_ref[3]], vir_ref)
     depth = 4 * rows_dev * own0.shape[1]
     chi = None
     for moment in range(tau_count):
         here = slice(moment * depth, (moment + 1) * depth)
+        part = slice(moment * depth // 2, (moment + 1) * depth // 2)
+        vir_late = jnp.concatenate([vir_own[:, part], vir_ref[:, part]], 1)
         term = lax.dot_general(
             jnp.concatenate([occ_early[:, here], occ_ref[:, here]], 0),
-            jnp.concatenate([vir_early[:, here], vir_ref[:, here]], 0),
+            jnp.concatenate([vir_early[:, here], vir_late], 0),
             (((1,), (1,)), ((), ())), preferred_element_type=F32,
         ) * tau_ref[moment]
         chi = term if chi is None else chi + term
@@ -724,14 +749,15 @@
     (virt,) = call(
         functools.partial(virt_kernel, sizes), "virt", [half(4, tile, tau_count * tile)], [vmem] * 2, [], 8
     )(chosen, virt)
-    (vir_early,) = call(
-        functools.partial(early_vir_kernel, rows_dev, tau_count, early), "vir", [first], [vmem] * 5, [], 6
+    vir_early, vir_own = call(
+        functools.partial(early_vir_kernel, rows_dev, tau_count, early, steps - early), "vir",
+        [first, half((steps - early) * PAIR, wide // 2)], [vmem] * 5, [], 6
     )(virt, *owns, *got[0])
     shares = call(
         functools.partial(late_kernel, rows_dev, tau_count, early, steps - early, scale), "late",
-        [jax.ShapeDtypeStruct((share_rows, aux_dev), F32)] * orb_count, [smem] + [vmem] * 8,
-        [pltpu.VMEM(((steps - early) * PAIR, wide), BF16), pltpu.VMEM(((steps - early) * PAIR, wide), BF16)], 16,
-    )(tau_weight, mix, virt, *owns, *got[1], occ_early, vir_early)
+        [jax.ShapeDtypeStruct((share_rows, aux_dev), F32)] * orb_count, [smem] + [vmem] * 9,
+        [pltpu.VMEM(((steps - early) * PAIR, wide), BF16), pltpu.VMEM(((steps - early) * PAIR, wide // 2), BF16)], 16,
+    )(tau_weight, mix, virt, *owns, *got[1], occ_early, vir_early, vir_own)
     total = shares[0]
     for distance, share in zip(partners(orb_count)[1:], shares[1:]):
         total = total + xor(share, "orb", distance)

time: 35.1 us -> 35.1 us (level)
  transfers between devices with their start and end apart: 13 -> 13, of which waited for: 9 -> 9; matrix products, arithmetic and copies ran while one was open for 0% -> 0% of each run, Pallas kernels for 12% -> 13%
where the time goes in v6:
time: 35.1 us; the launch traced here: 34.9 us
  starting transfers between devices  16.5 us (47%)
  Pallas kernels  8.89 us (25%)
  waiting for transfers between devices  8.74 us (25%)
  other arithmetic  0.65 us (2%)
    ppermute x13, starting transfers between devices, xor(): lax.ppermute(value, axis, [(i, i ^ distance) for i in range(lax.axis_size...  16.5 us
    ppermute x13, waiting for transfers between devices, xor(): lax.ppermute(value, axis, [(i, i ^ distance) for i in range(lax.axis_size...  8.74 us
    pallas_call x1, Pallas kernels, on_device_square(): call(functools.partial(late_kernel, rows_dev, tau_count, early, steps - e...  2.35 us
    pallas_call x1, Pallas kernels, on_device_square(): call(functools.partial(message_kernel, message), 'message', [half(message...  1.48 us
    pallas_call x1, Pallas kernels, on_device_square(): call(functools.partial(early_vir_kernel, rows_dev, tau_count, early, step...  1.1 us
    pallas_call x1, Pallas kernels, on_device_square(): call(functools.partial(mix_kernel, sizes, message), 'mix', [half(tau_coun...  1.01 us
    pallas_call x1, Pallas kernels, on_device_square(): call(functools.partial(early_occ_kernel, rows_dev, tau_count, early), 'oc...  0.98 us
  transfers between devices with their start and end apart: 13, of which 9 were waited for; matrix products, arithmetic and copies ran while one was open for 0% of the time, Pallas kernels for 13%

profile of v6, /device:TPU:0, one launch (start us, length us, event | category | flops | bytes accessed | tf_op | source)
XLA Modules:
  0.0 34.9 jit_solution(2513213272601646611)
XLA Ops:
  0.0 0.0 copy-start.3
  0.0 1.5 %message.1 = (bf16[64,128]{1,0:T(8,128)(2,1)}, bf16[64,128]{1,0:T(8,128)(2,1)}, bf16[64,128]{1,0:T(8,128)(2,1)}, bf16[64,128]{1,0:T(8,128)(2,1)}) custom-call(bf16[32,128]{1,0:T(8,128)(2,1)} %bitcast.4, bf16[16,32]{1,0:T(8,128)(2,1)} %bitcast.5, s32[1,2]{1,0:T(1,128)} %col_hbm.1), custom_call_target="tpu_custom_call" | custom-call | flops 10000000000 | tf_op jit(solution)/shard_map/message/pallas_call | solution.py:712
  1.5 4.0 %collective-permute-start = (bf16[64,128]{1,0:T(8,128)(2,1)}, bf16[64,128]{1,0:T(8,128)(2,1)S(1)}, u32[]{:S(2)}, u32[]{:S(2)}) collective-permute-start(bf16[64,128]{1,0:T(8,128)(2,1)} %get-tuple-element.24), channel_id=1, source_target_pairs={{0,24},{8,16},{16,8},{24,0},{1,25},{9,17},{17,9},{25,1},{2,26},{10... | collective-permute-start | bytes 49160 | tf_op jit(solution)/shard_map/ppermute | solution.py:702
  5.5 0.5 %collective-permute-start.1 = (bf16[64,128]{1,0:T(8,128)(2,1)}, bf16[64,128]{1,0:T(8,128)(2,1)S(1)}, u32[]{:S(2)}, u32[]{:S(2)}) collective-permute-start(bf16[64,128]{1,0:T(8,128)(2,1)} %get-tuple-element.25), channel_id=1, source_target_pairs={{0,8},{8,0},{16,24},{24,16},{1,9},{9,1},{17,25},{25,17},{2,10},{10... | collective-permute-start | bytes 49160 | tf_op jit(solution)/shard_map/ppermute | solution.py:702
  6.0 0.1 collective-permute-start.2
  6.1 0.0 copy-done.3
  6.1 0.0 copy-start
  6.1 0.7 %own.1 = (bf16[2048,128]{1,0:T(8,128)(2,1)S(1)}, bf16[2048,128]{1,0:T(8,128)(2,1)S(1)}) custom-call(bf16[4096,128]{1,0:T(8,128)(2,1)S(1)} %bitcast.3), custom_call_target="tpu_custom_call" | custom-call | flops 10000000000 | tf_op jit(solution)/shard_map/own/pallas_call | solution.py:722
  6.8 0.6 %collective-permute-done.refs_3_.refs_1_ = bf16[64,128]{1,0:T(8,128)(2,1)S(1)} collective-permute-done((bf16[64,128]{1,0:T(8,128)(2,1)}, bf16[64,128]{1,0:T(8,128)(2,1)S(1)}, u32[]{:S(2)}, u32[]{:S(2)}) %collective-permute-start) | collective-permute-done | bytes 16416 | tf_op jit(solution)/shard_map/ppermute | solution.py:702
  7.4 2.0 %collective-permute-done.1.refs_4_.refs_2_ = bf16[64,128]{1,0:T(8,128)(2,1)S(1)} collective-permute-done((bf16[64,128]{1,0:T(8,128)(2,1)}, bf16[64,128]{1,0:T(8,128)(2,1)S(1)}, u32[]{:S(2)}, u32[]{:S(2)}) %collective-permute-start.1) | collective-permute-done | bytes 16416 | tf_op jit(solution)/shard_map/ppermute | solution.py:702
  9.4 0.5 %collective-permute-done.2.refs_5_.refs_3_ = bf16[64,128]{1,0:T(8,128)(2,1)S(1)} collective-permute-done((bf16[64,128]{1,0:T(8,128)(2,1)}, bf16[64,128]{1,0:T(8,128)(2,1)S(1)}, u32[]{:S(2)}, u32[]{:S(2)}) %collective-permute-start.2) | collective-permute-done | bytes 16416 | tf_op jit(solution)/shard_map/ppermute | solution.py:702
  9.9 0.0 copy-done
  9.9 0.0 copy-start.1
  9.9 0.7 %send.1 = (bf16[96,128]{1,0:T(8,128)(2,1)S(1)}, f32[8,128]{1,0:T(8,128)S(1)}, bf16[1536,128]{1,0:T(8,128)(2,1)S(1)}, bf16[1536,128]{1,0:T(8,128)(2,1)S(1)}, bf16...) custom-call(bf16[2048,128]{1,0:T(8,128)(2,1)S(1)} %get-tuple-element.27.refs_0_.own0, ...), custom_call_target="tpu_custom_call" | custom-call | flops 10000000000 | tf_op jit(solution)/shard_map/send/pallas_call | solution.py:725
  10.6 1.6 %collective-permute-start.6 = (bf16[1536,128]{1,0:T(8,128)(2,1)S(1)}, bf16[1536,128]{1,0:T(8,128)(2,1)S(1)}, u32[]{:S(2)}, u32[]{:S(2)}) collective-permute-start(bf16[1536,128]{1,0:T(8,128)(2,1)S(1)} %get-tuple-element.31), channel_id=1, source_target_pairs={{0,8},{8,0},{16,24},{24,16},{1,9},{9,1},{17,25},{25,17},{2,10},{10... | collective-permute-start | bytes 1179656 | tf_op jit(solution)/shard_map/ppermute | solution.py:702
  12.2 0.5 %collective-permute-start.7 = (bf16[1536,128]{1,0:T(8,128)(2,1)S(1)}, bf16[1536,128]{1,0:T(8,128)(2,1)S(1)}, u32[]{:S(2)}, u32[]{:S(2)}) collective-permute-start(bf16[1536,128]{1,0:T(8,128)(2,1)S(1)} %get-tuple-element.32), channel_id=1, source_target_pairs={{0,16},{8,24},{16,0},{24,8},{1,17},{9,25},{17,1},{25,9},{2,18},{10... | collective-permute-start | bytes 1179656 | tf_op jit(solution)/shard_map/ppermute | solution.py:702
  12.7 2.6 %collective-permute-start.3 = (bf16[96,128]{1,0:T(8,128)(2,1)S(1)}, bf16[96,128]{1,0:T(8,128)(2,1)S(1)}, u32[]{:S(2)}, u32[]{:S(2)}) collective-permute-start(bf16[96,128]{1,0:T(8,128)(2,1)S(1)} %get-tuple-element.30.one_ref), channel_id=1, source_target_pairs={{0,4},{1,5},{2,6},{3,7},{4,0},{5,1},{6,2},{7,3},{8,12},{9,13},{10,... | collective-permute-start | bytes 73736 | tf_op jit(solution)/shard_map/ppermute | solution.py:702
  15.3 0.0 copy-done.1
  15.3 1.0 %mix.1.anchor.mix_ref = bf16[512,256]{1,0:T(8,128)(2,1)S(1)} custom-call(s32[2,4,4]{2,1,0:T(4,128)S(1)} %copy-done.1, bf16[64,128]{1,0:T(8,128)(2,1)S(1)} %copy-done, bf16[64,128]{1,0:T(8,128)(2,1)S(1)} %collective-permute-done.refs_3_.refs_1_, bf16[64,128]{1,0:T(8,128)(2,1)S(1)} %collective-permute-done.1.refs_4_.refs_2_, ...), custom_call_target="tpu_custom_call" | custom-call | tf_op jit(solution)/shard_map/mix/pallas_call | solution.py:732
  16.3 1.1 %collective-permute-done.3.two_ref = bf16[96,128]{1,0:T(8,128)(2,1)S(1)} collective-permute-done((bf16[96,128]{1,0:T(8,128)(2,1)S(1)}, bf16[96,128]{1,0:T(8,128)(2,1)S(1)}, u32[]{:S(2)}, u32[]{:S(2)}) %collective-permute-start.3) | collective-permute-done | bytes 24608 | tf_op jit(solution)/shard_map/ppermute | solution.py:702
  17.4 1.6 %collective-permute-start.4 = (bf16[192,128]{1,0:T(8,128)(2,1)S(1)}, bf16[192,128]{1,0:T(8,128)(2,1)S(1)}, u32[]{:S(2)}, u32[]{:S(2)}) collective-permute-start(bf16[192,128]{1,0:T(8,128)(2,1)S(1)} %join.3.one_ref), channel_id=1, source_target_pairs={{0,2},{1,3},{2,0},{3,1},{4,6},{5,7},{6,4},{7,5},{8,10},{9,11},{10,... | collective-permute-start | bytes 147464 | tf_op jit(solution)/shard_map/ppermute | solution.py:702
  19.0 0.5 %collective-permute-start.8 = (bf16[512,128]{1,0:T(8,128)(2,1)S(1)}, bf16[512,128]{1,0:T(8,128)(2,1)S(1)}, u32[]{:S(2)}, u32[]{:S(2)}) collective-permute-start(bf16[512,128]{1,0:T(8,128)(2,1)S(1)} %get-tuple-element.33), channel_id=1, source_target_pairs={{0,8},{8,0},{16,24},{24,16},{1,9},{9,1},{17,25},{25,17},{2,10},{10... | collective-permute-start | bytes 393224 | tf_op jit(solution)/shard_map/ppermute | solution.py:702
  19.5 1.5 %collective-permute-start.9 = (bf16[512,128]{1,0:T(8,128)(2,1)S(1)}, bf16[512,128]{1,0:T(8,128)(2,1)S(1)}, u32[]{:S(2)}, u32[]{:S(2)}) collective-permute-start(bf16[512,128]{1,0:T(8,128)(2,1)S(1)} %get-tuple-element.34), channel_id=1, source_target_pairs={{0,16},{8,24},{16,0},{24,8},{1,17},{9,25},{17,1},{25,9},{2,18},{10... | collective-permute-start | bytes 393224 | tf_op jit(solution)/shard_map/ppermute | solution.py:702
  21.1 0.5 %collective-permute-done.4.two_ref = bf16[192,128]{1,0:T(8,128)(2,1)S(1)} collective-permute-done((bf16[192,128]{1,0:T(8,128)(2,1)S(1)}, bf16[192,128]{1,0:T(8,128)(2,1)S(1)}, u32[]{:S(2)}, u32[]{:S(2)}) %collective-permute-start.4) | collective-permute-done | bytes 49184 | tf_op jit(solution)/shard_map/ppermute | solution.py:702
  21.5 0.1 collective-permute-start.5
  21.6 0.0 collective-permute-done.6.from_x
  21.6 0.8 %collective-permute-done.7.from_y = bf16[1536,128]{1,0:T(8,128)(2,1)S(1)} collective-permute-done((bf16[1536,128]{1,0:T(8,128)(2,1)S(1)}, bf16[1536,128]{1,0:T(8,128)(2,1)S(1)}, u32[]{:S(2)}, u32[]{:S(2)}) %collective-permute-start.7) | collective-permute-done | bytes 393248 | tf_op jit(solution)/shard_map/ppermute | solution.py:702
  22.5 1.0 %occ.1.anchor.refs_4_ = bf16[192,8192]{1,0:T(8,128)(2,1)S(1)} custom-call(bf16[512,256]{1,0:T(8,128)(2,1)S(1)} %mix.1.anchor.mix_ref, bf16[2048,128]{1,0:T(8,128)(2,1)S(1)} %get-tuple-element.27.refs_0_.own0, bf16[2048,128]{1,0:T(8,128)(2,1)S(1)} %get-tuple-element.28.refs_1_.own1, bf16[1536,128]{1,0:T(8,128)(2,1)S(1)} %collective-permute-done.6.from_x, ...), custom_call_target="tpu_custom_call" | custom-call | tf_op jit(solution)/shard_map/occ/pallas_call | solution.py:738
  23.5 0.0 copy-start.2
  23.5 0.0 collective-permute-done.5.two_ref
  23.5 0.5 %virt.1.virt_ref = bf16[4,128,256]{2,1,0:T(8,128)(2,1)S(1)} custom-call(f32[8,128]{1,0:T(8,128)S(1)} %get-tuple-element.29.refs_4_.refs_0_, bf16[768,128]{1,0:T(8,128)(2,1)S(1)} %join.5.refs_1_), custom_call_target="tpu_custom_call" | custom-call | tf_op jit(solution)/shard_map/virt/pallas_call | solution.py:749
  24.1 1.1 %vir.1 = (bf16[192,8192]{1,0:T(8,128)(2,1)S(1)}, bf16[64,4096]{1,0:T(8,128)(2,1)S(1)}) custom-call(bf16[4,128,256]{2,1,0:T(8,128)(2,1)S(1)} %virt.1.virt_ref, bf16[2048,128]{1,0:T(8,128)(2,1)S(1)} %get-tuple-element.27.refs_0_.own0, bf16[2048,128]{1,0:T(8,128)(2,1)S(1)} %get-tuple-element.28.refs_1_.own1, ...), custom_call_target="tpu_custom_call" | custom-call | tf_op jit(solution)/shard_map/vir/pallas_call | solution.py:752
  25.2 0.0 collective-permute-done.8.refs_2_
  25.2 0.0 collective-permute-done.9.refs_3_
  25.2 0.0 copy-done.2
  25.2 2.4 %late.1 = (f32[64,256]{1,0:T(8,128)S(1)}, f32[64,256]{1,0:T(8,128)S(1)}, f32[64,256]{1,0:T(8,128)S(1)}, f32[64,256]{1,0:T(8,128)S(1)}) custom-call(f32[2]{0:T(128)S(1)} %copy-done.2, bf16[512,256]{1,0:T(8,128)(2,1)S(1)} %mix.1.anchor.mix_ref, bf16[4,128,256]{2,1,0:T(8,128)(2,1)S(1)} %virt.1.virt_ref, bf16[2048,128]{1,0:T(8,128)(2,1)S(1)} %get-tuple-element.27.refs_0_.own0, ...), custom_call_target="tpu_custom_call" | custom-call | tf_op jit(solution)/shard_map/late/pallas_call | solution.py:756
  27.6 1.8 %collective-permute-start.10 = (f32[64,256]{1,0:T(8,128)S(1)}, f32[64,256]{1,0:T(8,128)S(1)}, u32[]{:S(2)}, u32[]{:S(2)}) collective-permute-start(f32[64,256]{1,0:T(8,128)S(1)} %get-tuple-element.38), channel_id=1, source_target_pairs={{0,24},{8,16},{16,8},{24,0},{1,25},{9,17},{17,9},{25,1},{2,26},{10... | collective-permute-start | bytes 196616 | tf_op jit(solution)/shard_map/ppermute | solution.py:702
  29.4 0.6 %collective-permute-start.11 = (f32[64,256]{1,0:T(8,128)S(1)}, f32[64,256]{1,0:T(8,128)S(1)}, u32[]{:S(2)}, u32[]{:S(2)}) collective-permute-start(f32[64,256]{1,0:T(8,128)S(1)} %get-tuple-element.39), channel_id=1, source_target_pairs={{0,8},{8,0},{16,24},{24,16},{1,9},{9,1},{17,25},{25,17},{2,10},{10... | collective-permute-start | bytes 196616 | tf_op jit(solution)/shard_map/ppermute | solution.py:702
  30.0 1.1 %collective-permute-start.12 = (f32[64,256]{1,0:T(8,128)S(1)}, f32[64,256]{1,0:T(8,128)S(1)}, u32[]{:S(2)}, u32[]{:S(2)}) collective-permute-start(f32[64,256]{1,0:T(8,128)S(1)} %get-tuple-element.40), channel_id=1, source_target_pairs={{0,16},{8,24},{16,0},{24,8},{1,17},{9,25},{17,1},{25,9},{2,18},{10... | collective-permute-start | bytes 196616 | tf_op jit(solution)/shard_map/ppermute | solution.py:702
  31.1 1.9 %collective-permute-done.10 = f32[64,256]{1,0:T(8,128)S(1)} collective-permute-done((f32[64,256]{1,0:T(8,128)S(1)}, f32[64,256]{1,0:T(8,128)S(1)}, u32[]{:S(2)}, u32[]{:S(2)}) %collective-permute-start.10) | collective-permute-done | bytes 65568 | tf_op jit(solution)/shard_map/ppermute | solution.py:702
  33.0 0.6 %collective-permute-done.11 = f32[64,256]{1,0:T(8,128)S(1)} collective-permute-done((f32[64,256]{1,0:T(8,128)S(1)}, f32[64,256]{1,0:T(8,128)S(1)}, u32[]{:S(2)}, u32[]{:S(2)}) %collective-permute-start.11) | collective-permute-done | bytes 65568 | tf_op jit(solution)/shard_map/ppermute | solution.py:702
  33.7 0.6 %collective-permute-done.12 = f32[64,256]{1,0:T(8,128)S(1)} collective-permute-done((f32[64,256]{1,0:T(8,128)S(1)}, f32[64,256]{1,0:T(8,128)S(1)}, u32[]{:S(2)}, u32[]{:S(2)}) %collective-permute-start.12) | collective-permute-done | bytes 65568 | tf_op jit(solution)/shard_map/ppermute | solution.py:702
  34.3 0.6 %add_add_fusion = f32[64,256]{1,0:T(8,128)} fusion(f32[64,256]{1,0:T(8,128)S(1)} %collective-permute-done.12, f32[64,256]{1,0:T(8,128)S(1)} %collective-permute-done.11, f32[64,256]{1,0:T(8,128)S(1)} %get-tuple-element.37, f32[64,256]{1,0:T(8,128)S(1)} %collective-permute-done.10), kind=kLoop, calls=%fused_computation | loop fusion | flops 49152 | bytes 327680 | tf_op jit(solution)/shard_map/add | solution.py:763
  (3 shorter events, 0.0 us)
Async XLA Ops:
  0.0 6.1 %copy-start.3 = (bf16[256,8,2,128]{3,2,1,0:T(2,128)(2,1)S(1)}, bf16[256,8,2,128]{3,2,1,0:T(2,128)(2,1)}, u32[]{:S(2)}) copy-start(bf16[256,8,2,128]{3,2,1,0:T(2,128)(2,1)} %param.6) | copy-start | bytes 3145732
  1.5 5.9 %collective-permute-start = (bf16[64,128]{1,0:T(8,128)(2,1)}, bf16[64,128]{1,0:T(8,128)(2,1)S(1)}, u32[]{:S(2)}, u32[]{:S(2)}) collective-permute-start(bf16[64,128]{1,0:T(8,128)(2,1)} %get-tuple-element.24), channel_id=1, source_target_pairs={{0,24},{8,16},{16,8},{24,0},{1,25},{9,17},{17,9},{25,1},{2,26},{10... | collective-permute-start | bytes 49160 | tf_op jit(solution)/shard_map/ppermute | solution.py:702
  5.5 3.9 %collective-permute-start.1 = (bf16[64,128]{1,0:T(8,128)(2,1)}, bf16[64,128]{1,0:T(8,128)(2,1)S(1)}, u32[]{:S(2)}, u32[]{:S(2)}) collective-permute-start(bf16[64,128]{1,0:T(8,128)(2,1)} %get-tuple-element.25), channel_id=1, source_target_pairs={{0,8},{8,0},{16,24},{24,16},{1,9},{9,1},{17,25},{25,17},{2,10},{10... | collective-permute-start | bytes 49160 | tf_op jit(solution)/shard_map/ppermute | solution.py:702
  6.0 3.9 %collective-permute-start.2 = (bf16[64,128]{1,0:T(8,128)(2,1)}, bf16[64,128]{1,0:T(8,128)(2,1)S(1)}, u32[]{:S(2)}, u32[]{:S(2)}) collective-permute-start(bf16[64,128]{1,0:T(8,128)(2,1)} %get-tuple-element.26), channel_id=1, source_target_pairs={{0,16},{8,24},{16,0},{24,8},{1,17},{9,25},{17,1},{25,9},{2,18},{10... | collective-permute-start | bytes 49160 | tf_op jit(solution)/shard_map/ppermute | solution.py:702
  6.1 3.8 %copy-start = (bf16[64,128]{1,0:T(8,128)(2,1)S(1)}, bf16[64,128]{1,0:T(8,128)(2,1)}, u32[]{:S(2)}) copy-start(bf16[64,128]{1,0:T(8,128)(2,1)} %get-tuple-element.23.refs_2_.refs_0_) | copy-start | bytes 49156
  9.9 5.3 %copy-start.1 = (s32[2,4,4]{2,1,0:T(4,128)S(1)}, s32[2,4,4]{2,1,0:T(4,128)}, u32[]{:S(2)}) copy-start(s32[2,4,4]{2,1,0:T(4,128)} %live_ref.1) | copy-start | bytes 388
  10.6 11.0 %collective-permute-start.6 = (bf16[1536,128]{1,0:T(8,128)(2,1)S(1)}, bf16[1536,128]{1,0:T(8,128)(2,1)S(1)}, u32[]{:S(2)}, u32[]{:S(2)}) collective-permute-start(bf16[1536,128]{1,0:T(8,128)(2,1)S(1)} %get-tuple-element.31), channel_id=1, source_target_pairs={{0,8},{8,0},{16,24},{24,16},{1,9},{9,1},{17,25},{25,17},{2,10},{10... | collective-permute-start | bytes 1179656 | tf_op jit(solution)/shard_map/ppermute | solution.py:702
  12.2 10.3 %collective-permute-start.7 = (bf16[1536,128]{1,0:T(8,128)(2,1)S(1)}, bf16[1536,128]{1,0:T(8,128)(2,1)S(1)}, u32[]{:S(2)}, u32[]{:S(2)}) collective-permute-start(bf16[1536,128]{1,0:T(8,128)(2,1)S(1)} %get-tuple-element.32), channel_id=1, source_target_pairs={{0,16},{8,24},{16,0},{24,8},{1,17},{9,25},{17,1},{25,9},{2,18},{10... | collective-permute-start | bytes 1179656 | tf_op jit(solution)/shard_map/ppermute | solution.py:702
  12.7 4.7 %collective-permute-start.3 = (bf16[96,128]{1,0:T(8,128)(2,1)S(1)}, bf16[96,128]{1,0:T(8,128)(2,1)S(1)}, u32[]{:S(2)}, u32[]{:S(2)}) collective-permute-start(bf16[96,128]{1,0:T(8,128)(2,1)S(1)} %get-tuple-element.30.one_ref), channel_id=1, source_target_pairs={{0,4},{1,5},{2,6},{3,7},{4,0},{5,1},{6,2},{7,3},{8,12},{9,13},{10,... | collective-permute-start | bytes 73736 | tf_op jit(solution)/shard_map/ppermute | solution.py:702
  17.4 4.1 %collective-permute-start.4 = (bf16[192,128]{1,0:T(8,128)(2,1)S(1)}, bf16[192,128]{1,0:T(8,128)(2,1)S(1)}, u32[]{:S(2)}, u32[]{:S(2)}) collective-permute-start(bf16[192,128]{1,0:T(8,128)(2,1)S(1)} %join.3.one_ref), channel_id=1, source_target_pairs={{0,2},{1,3},{2,0},{3,1},{4,6},{5,7},{6,4},{7,5},{8,10},{9,11},{10,... | collective-permute-start | bytes 147464 | tf_op jit(solution)/shard_map/ppermute | solution.py:702
  19.0 6.2 %collective-permute-start.8 = (bf16[512,128]{1,0:T(8,128)(2,1)S(1)}, bf16[512,128]{1,0:T(8,128)(2,1)S(1)}, u32[]{:S(2)}, u32[]{:S(2)}) collective-permute-start(bf16[512,128]{1,0:T(8,128)(2,1)S(1)} %get-tuple-element.33), channel_id=1, source_target_pairs={{0,8},{8,0},{16,24},{24,16},{1,9},{9,1},{17,25},{25,17},{2,10},{10... | collective-permute-start | bytes 393224 | tf_op jit(solution)/shard_map/ppermute | solution.py:702
  19.5 5.6 %collective-permute-start.9 = (bf16[512,128]{1,0:T(8,128)(2,1)S(1)}, bf16[512,128]{1,0:T(8,128)(2,1)S(1)}, u32[]{:S(2)}, u32[]{:S(2)}) collective-permute-start(bf16[512,128]{1,0:T(8,128)(2,1)S(1)} %get-tuple-element.34), channel_id=1, source_target_pairs={{0,16},{8,24},{16,0},{24,8},{1,17},{9,25},{17,1},{25,9},{2,18},{10... | collective-permute-start | bytes 393224 | tf_op jit(solution)/shard_map/ppermute | solution.py:702
  21.5 1.9 %collective-permute-start.5 = (bf16[384,128]{1,0:T(8,128)(2,1)S(1)}, bf16[384,128]{1,0:T(8,128)(2,1)S(1)}, u32[]{:S(2)}, u32[]{:S(2)}) collective-permute-start(bf16[384,128]{1,0:T(8,128)(2,1)S(1)} %join.4.one_ref), channel_id=1, source_target_pairs={{0,1},{1,0},{2,3},{3,2},{4,5},{5,4},{6,7},{7,6},{8,9},{9,8},{10,11... | collective-permute-start | bytes 294920 | tf_op jit(solution)/shard_map/ppermute | solution.py:702
  23.5 1.7 %copy-start.2 = (f32[2]{0:T(128)S(1)}, f32[2]{0:T(128)}, u32[]{:S(2)}) copy-start(f32[2]{0:T(128)} %tau_ref.1) | copy-start | bytes 28
  27.6 5.5 %collective-permute-start.10 = (f32[64,256]{1,0:T(8,128)S(1)}, f32[64,256]{1,0:T(8,128)S(1)}, u32[]{:S(2)}, u32[]{:S(2)}) collective-permute-start(f32[64,256]{1,0:T(8,128)S(1)} %get-tuple-element.38), channel_id=1, source_target_pairs={{0,24},{8,16},{16,8},{24,0},{1,25},{9,17},{17,9},{25,1},{2,26},{10... | collective-permute-start | bytes 196616 | tf_op jit(solution)/shard_map/ppermute | solution.py:702
  29.4 4.3 %collective-permute-start.11 = (f32[64,256]{1,0:T(8,128)S(1)}, f32[64,256]{1,0:T(8,128)S(1)}, u32[]{:S(2)}, u32[]{:S(2)}) collective-permute-start(f32[64,256]{1,0:T(8,128)S(1)} %get-tuple-element.39), channel_id=1, source_target_pairs={{0,8},{8,0},{16,24},{24,16},{1,9},{9,1},{17,25},{25,17},{2,10},{10... | collective-permute-start | bytes 196616 | tf_op jit(solution)/shard_map/ppermute | solution.py:702
  30.0 4.3 %collective-permute-start.12 = (f32[64,256]{1,0:T(8,128)S(1)}, f32[64,256]{1,0:T(8,128)S(1)}, u32[]{:S(2)}, u32[]{:S(2)}) collective-permute-start(f32[64,256]{1,0:T(8,128)S(1)} %get-tuple-element.40), channel_id=1, source_target_pairs={{0,16},{8,24},{16,0},{24,8},{1,17},{9,25},{17,1},{25,9},{2,18},{10... | collective-permute-start | bytes 196616 | tf_op jit(solution)/shard_map/ppermute | solution.py:702

commit v7 on v6

--- a/solution.py
+++ b/solution.py
@@ -674,7 +674,7 @@
         picked = chi[0:share_rows]
         for owner in range(1, 4):
             picked = jnp.where(me ^ distance == owner, chi[owner * share_rows : (owner + 1) * share_rows], picked)
-        out[...] = picked
+        out[...] = picked.astype(out.dtype)
 
 
 def on_device_square(b_rows, col_blocks, g_occ, occ_live, g_virt, tau_weight):
@@ -755,12 +755,12 @@
     )(virt, *owns, *got[0])
     shares = call(
         functools.partial(late_kernel, rows_dev, tau_count, early, steps - early, scale), "late",
-        [jax.ShapeDtypeStruct((share_rows, aux_dev), F32)] * orb_count, [smem] + [vmem] * 9,
+        [jax.ShapeDtypeStruct((share_rows, aux_dev), F32)] + [half(share_rows, aux_dev)] * (orb_count - 1), [smem] + [vmem] * 9,
         [pltpu.VMEM(((steps - early) * PAIR, wide), BF16), pltpu.VMEM(((steps - early) * PAIR, wide // 2), BF16)], 16,
     )(tau_weight, mix, virt, *owns, *got[1], occ_early, vir_early, vir_own)
     total = shares[0]
     for distance, share in zip(partners(orb_count)[1:], shares[1:]):
-        total = total + xor(share, "orb", distance)
+        total = total + xor(share, "orb", distance).astype(F32)
     return total
 
 

time: 35.1 us -> 34.7 us (0.989)
    ppermute x13, waiting for transfers between devices: 8.74 us -> 8.39 us  [xor(): lax.ppermute(value, axis, [(i, i ^ distance) for i in range(lax.axis_size...]
where the time goes in v7:
time: 34.7 us; the launch traced here: 34.6 us
  starting transfers between devices  16.5 us (48%)
  Pallas kernels  8.89 us (26%)
  waiting for transfers between devices  8.39 us (24%)
  other arithmetic  0.65 us (2%)
    ppermute x13, starting transfers between devices, xor(): lax.ppermute(value, axis, [(i, i ^ distance) for i in range(lax.axis_size...  16.5 us
    ppermute x13, waiting for transfers between devices, xor(): lax.ppermute(value, axis, [(i, i ^ distance) for i in range(lax.axis_size...  8.39 us
    pallas_call x1, Pallas kernels, on_device_square(): call(functools.partial(late_kernel, rows_dev, tau_count, early, steps - e...  2.36 us
    pallas_call x1, Pallas kernels, on_device_square(): call(functools.partial(message_kernel, message), 'message', [half(message...  1.48 us
    pallas_call x1, Pallas kernels, on_device_square(): call(functools.partial(early_vir_kernel, rows_dev, tau_count, early, step...  1.1 us
    pallas_call x1, Pallas kernels, on_device_square(): call(functools.partial(mix_kernel, sizes, message), 'mix', [half(tau_coun...  1.01 us
    pallas_call x1, Pallas kernels, on_device_square(): call(functools.partial(early_occ_kernel, rows_dev, tau_count, early), 'oc...  0.98 us
    pallas_call x1, Pallas kernels, on_device_square(): call(functools.partial(own_kernel, rows_dev, steps), 'own', [block] * 2,...  0.7 us
  transfers between devices with their start and end apart: 13, of which 9 were waited for; matrix products, arithmetic and copies ran while one was open for 0% of the time, Pallas kernels for 13%

profile of v7, /device:TPU:0, one launch (start us, length us, event | category | flops | bytes accessed | tf_op | source)
XLA Modules:
  0.0 34.6 jit_solution(11692845515315035814)
XLA Ops:
  0.0 0.0 copy-start.3
  0.0 1.5 %message.1 = (bf16[64,128]{1,0:T(8,128)(2,1)}, bf16[64,128]{1,0:T(8,128)(2,1)}, bf16[64,128]{1,0:T(8,128)(2,1)}, bf16[64,128]{1,0:T(8,128)(2,1)}) custom-call(bf16[32,128]{1,0:T(8,128)(2,1)} %bitcast.4, bf16[16,32]{1,0:T(8,128)(2,1)} %bitcast.5, s32[1,2]{1,0:T(1,128)} %col_hbm.1), custom_call_target="tpu_custom_call" | custom-call | flops 10000000000 | tf_op jit(solution)/shard_map/message/pallas_call | solution.py:712
  1.5 4.0 %collective-permute-start = (bf16[64,128]{1,0:T(8,128)(2,1)}, bf16[64,128]{1,0:T(8,128)(2,1)S(1)}, u32[]{:S(2)}, u32[]{:S(2)}) collective-permute-start(bf16[64,128]{1,0:T(8,128)(2,1)} %get-tuple-element.24), channel_id=1, source_target_pairs={{0,24},{8,16},{16,8},{24,0},{1,25},{9,17},{17,9},{25,1},{2,26},{10... | collective-permute-start | bytes 49160 | tf_op jit(solution)/shard_map/ppermute | solution.py:702
  5.5 0.5 %collective-permute-start.1 = (bf16[64,128]{1,0:T(8,128)(2,1)}, bf16[64,128]{1,0:T(8,128)(2,1)S(1)}, u32[]{:S(2)}, u32[]{:S(2)}) collective-permute-start(bf16[64,128]{1,0:T(8,128)(2,1)} %get-tuple-element.25), channel_id=1, source_target_pairs={{0,8},{8,0},{16,24},{24,16},{1,9},{9,1},{17,25},{25,17},{2,10},{10... | collective-permute-start | bytes 49160 | tf_op jit(solution)/shard_map/ppermute | solution.py:702
  6.0 0.1 collective-permute-start.2
  6.1 0.0 copy-done.3
  6.1 0.0 copy-start
  6.1 0.7 %own.1 = (bf16[2048,128]{1,0:T(8,128)(2,1)S(1)}, bf16[2048,128]{1,0:T(8,128)(2,1)S(1)}) custom-call(bf16[4096,128]{1,0:T(8,128)(2,1)S(1)} %bitcast.3), custom_call_target="tpu_custom_call" | custom-call | flops 10000000000 | tf_op jit(solution)/shard_map/own/pallas_call | solution.py:722
  6.8 0.6 %collective-permute-done.refs_3_.refs_1_ = bf16[64,128]{1,0:T(8,128)(2,1)S(1)} collective-permute-done((bf16[64,128]{1,0:T(8,128)(2,1)}, bf16[64,128]{1,0:T(8,128)(2,1)S(1)}, u32[]{:S(2)}, u32[]{:S(2)}) %collective-permute-start) | collective-permute-done | bytes 16416 | tf_op jit(solution)/shard_map/ppermute | solution.py:702
  7.4 2.0 %collective-permute-done.1.refs_4_.refs_2_ = bf16[64,128]{1,0:T(8,128)(2,1)S(1)} collective-permute-done((bf16[64,128]{1,0:T(8,128)(2,1)}, bf16[64,128]{1,0:T(8,128)(2,1)S(1)}, u32[]{:S(2)}, u32[]{:S(2)}) %collective-permute-start.1) | collective-permute-done | bytes 16416 | tf_op jit(solution)/shard_map/ppermute | solution.py:702
  9.4 0.5 %collective-permute-done.2.refs_5_.refs_3_ = bf16[64,128]{1,0:T(8,128)(2,1)S(1)} collective-permute-done((bf16[64,128]{1,0:T(8,128)(2,1)}, bf16[64,128]{1,0:T(8,128)(2,1)S(1)}, u32[]{:S(2)}, u32[]{:S(2)}) %collective-permute-start.2) | collective-permute-done | bytes 16416 | tf_op jit(solution)/shard_map/ppermute | solution.py:702
  9.9 0.0 copy-done
  9.9 0.0 copy-start.1
  9.9 0.7 %send.1 = (bf16[96,128]{1,0:T(8,128)(2,1)S(1)}, f32[8,128]{1,0:T(8,128)S(1)}, bf16[1536,128]{1,0:T(8,128)(2,1)S(1)}, bf16[1536,128]{1,0:T(8,128)(2,1)S(1)}, bf16...) custom-call(bf16[2048,128]{1,0:T(8,128)(2,1)S(1)} %get-tuple-element.27.refs_0_.own0, ...), custom_call_target="tpu_custom_call" | custom-call | flops 10000000000 | tf_op jit(solution)/shard_map/send/pallas_call | solution.py:725
  10.6 1.6 %collective-permute-start.6 = (bf16[1536,128]{1,0:T(8,128)(2,1)S(1)}, bf16[1536,128]{1,0:T(8,128)(2,1)S(1)}, u32[]{:S(2)}, u32[]{:S(2)}) collective-permute-start(bf16[1536,128]{1,0:T(8,128)(2,1)S(1)} %get-tuple-element.31), channel_id=1, source_target_pairs={{0,8},{8,0},{16,24},{24,16},{1,9},{9,1},{17,25},{25,17},{2,10},{10... | collective-permute-start | bytes 1179656 | tf_op jit(solution)/shard_map/ppermute | solution.py:702
  12.2 0.5 %collective-permute-start.7 = (bf16[1536,128]{1,0:T(8,128)(2,1)S(1)}, bf16[1536,128]{1,0:T(8,128)(2,1)S(1)}, u32[]{:S(2)}, u32[]{:S(2)}) collective-permute-start(bf16[1536,128]{1,0:T(8,128)(2,1)S(1)} %get-tuple-element.32), channel_id=1, source_target_pairs={{0,16},{8,24},{16,0},{24,8},{1,17},{9,25},{17,1},{25,9},{2,18},{10... | collective-permute-start | bytes 1179656 | tf_op jit(solution)/shard_map/ppermute | solution.py:702
  12.7 2.6 %collective-permute-start.3 = (bf16[96,128]{1,0:T(8,128)(2,1)S(1)}, bf16[96,128]{1,0:T(8,128)(2,1)S(1)}, u32[]{:S(2)}, u32[]{:S(2)}) collective-permute-start(bf16[96,128]{1,0:T(8,128)(2,1)S(1)} %get-tuple-element.30.one_ref), channel_id=1, source_target_pairs={{0,4},{1,5},{2,6},{3,7},{4,0},{5,1},{6,2},{7,3},{8,12},{9,13},{10,... | collective-permute-start | bytes 73736 | tf_op jit(solution)/shard_map/ppermute | solution.py:702
  15.3 0.0 copy-done.1
  15.3 1.0 %mix.1.anchor.mix_ref = bf16[512,256]{1,0:T(8,128)(2,1)S(1)} custom-call(s32[2,4,4]{2,1,0:T(4,128)S(1)} %copy-done.1, bf16[64,128]{1,0:T(8,128)(2,1)S(1)} %copy-done, bf16[64,128]{1,0:T(8,128)(2,1)S(1)} %collective-permute-done.refs_3_.refs_1_, bf16[64,128]{1,0:T(8,128)(2,1)S(1)} %collective-permute-done.1.refs_4_.refs_2_, ...), custom_call_target="tpu_custom_call" | custom-call | tf_op jit(solution)/shard_map/mix/pallas_call | solution.py:732
  16.3 1.1 %collective-permute-done.3.two_ref = bf16[96,128]{1,0:T(8,128)(2,1)S(1)} collective-permute-done((bf16[96,128]{1,0:T(8,128)(2,1)S(1)}, bf16[96,128]{1,0:T(8,128)(2,1)S(1)}, u32[]{:S(2)}, u32[]{:S(2)}) %collective-permute-start.3) | collective-permute-done | bytes 24608 | tf_op jit(solution)/shard_map/ppermute | solution.py:702
  17.4 1.6 %collective-permute-start.4 = (bf16[192,128]{1,0:T(8,128)(2,1)S(1)}, bf16[192,128]{1,0:T(8,128)(2,1)S(1)}, u32[]{:S(2)}, u32[]{:S(2)}) collective-permute-start(bf16[192,128]{1,0:T(8,128)(2,1)S(1)} %join.3.one_ref), channel_id=1, source_target_pairs={{0,2},{1,3},{2,0},{3,1},{4,6},{5,7},{6,4},{7,5},{8,10},{9,11},{10,... | collective-permute-start | bytes 147464 | tf_op jit(solution)/shard_map/ppermute | solution.py:702
  19.0 0.5 %collective-permute-start.8 = (bf16[512,128]{1,0:T(8,128)(2,1)S(1)}, bf16[512,128]{1,0:T(8,128)(2,1)S(1)}, u32[]{:S(2)}, u32[]{:S(2)}) collective-permute-start(bf16[512,128]{1,0:T(8,128)(2,1)S(1)} %get-tuple-element.33), channel_id=1, source_target_pairs={{0,8},{8,0},{16,24},{24,16},{1,9},{9,1},{17,25},{25,17},{2,10},{10... | collective-permute-start | bytes 393224 | tf_op jit(solution)/shard_map/ppermute | solution.py:702
  19.5 1.5 %collective-permute-start.9 = (bf16[512,128]{1,0:T(8,128)(2,1)S(1)}, bf16[512,128]{1,0:T(8,128)(2,1)S(1)}, u32[]{:S(2)}, u32[]{:S(2)}) collective-permute-start(bf16[512,128]{1,0:T(8,128)(2,1)S(1)} %get-tuple-element.34), channel_id=1, source_target_pairs={{0,16},{8,24},{16,0},{24,8},{1,17},{9,25},{17,1},{25,9},{2,18},{10... | collective-permute-start | bytes 393224 | tf_op jit(solution)/shard_map/ppermute | solution.py:702
  21.1 0.5 %collective-permute-done.4.two_ref = bf16[192,128]{1,0:T(8,128)(2,1)S(1)} collective-permute-done((bf16[192,128]{1,0:T(8,128)(2,1)S(1)}, bf16[192,128]{1,0:T(8,128)(2,1)S(1)}, u32[]{:S(2)}, u32[]{:S(2)}) %collective-permute-start.4) | collective-permute-done | bytes 49184 | tf_op jit(solution)/shard_map/ppermute | solution.py:702
  21.5 0.1 collective-permute-start.5
  21.6 0.0 collective-permute-done.6.from_x
  21.6 0.8 %collective-permute-done.7.from_y = bf16[1536,128]{1,0:T(8,128)(2,1)S(1)} collective-permute-done((bf16[1536,128]{1,0:T(8,128)(2,1)S(1)}, bf16[1536,128]{1,0:T(8,128)(2,1)S(1)}, u32[]{:S(2)}, u32[]{:S(2)}) %collective-permute-start.7) | collective-permute-done | bytes 393248 | tf_op jit(solution)/shard_map/ppermute | solution.py:702
  22.5 1.0 %occ.1.anchor.refs_4_ = bf16[192,8192]{1,0:T(8,128)(2,1)S(1)} custom-call(bf16[512,256]{1,0:T(8,128)(2,1)S(1)} %mix.1.anchor.mix_ref, bf16[2048,128]{1,0:T(8,128)(2,1)S(1)} %get-tuple-element.27.refs_0_.own0, bf16[2048,128]{1,0:T(8,128)(2,1)S(1)} %get-tuple-element.28.refs_1_.own1, bf16[1536,128]{1,0:T(8,128)(2,1)S(1)} %collective-permute-done.6.from_x, ...), custom_call_target="tpu_custom_call" | custom-call | tf_op jit(solution)/shard_map/occ/pallas_call | solution.py:738
  23.5 0.0 copy-start.2
  23.5 0.0 collective-permute-done.5.two_ref
  23.5 0.5 %virt.1.virt_ref = bf16[4,128,256]{2,1,0:T(8,128)(2,1)S(1)} custom-call(f32[8,128]{1,0:T(8,128)S(1)} %get-tuple-element.29.refs_4_.refs_0_, bf16[768,128]{1,0:T(8,128)(2,1)S(1)} %join.5.refs_1_), custom_call_target="tpu_custom_call" | custom-call | tf_op jit(solution)/shard_map/virt/pallas_call | solution.py:749
  24.1 1.1 %vir.1 = (bf16[192,8192]{1,0:T(8,128)(2,1)S(1)}, bf16[64,4096]{1,0:T(8,128)(2,1)S(1)}) custom-call(bf16[4,128,256]{2,1,0:T(8,128)(2,1)S(1)} %virt.1.virt_ref, bf16[2048,128]{1,0:T(8,128)(2,1)S(1)} %get-tuple-element.27.refs_0_.own0, bf16[2048,128]{1,0:T(8,128)(2,1)S(1)} %get-tuple-element.28.refs_1_.own1, ...), custom_call_target="tpu_custom_call" | custom-call | tf_op jit(solution)/shard_map/vir/pallas_call | solution.py:752
  25.2 0.0 collective-permute-done.8.refs_2_
  25.2 0.0 collective-permute-done.9.refs_3_
  25.2 0.0 copy-done.2
  25.2 2.4 %late.1 = (f32[64,256]{1,0:T(8,128)S(1)}, bf16[64,256]{1,0:T(8,128)(2,1)S(1)}, bf16[64,256]{1,0:T(8,128)(2,1)S(1)}, bf16[64,256]{1,0:T(8,128)(2,1)S(1)}) custom-call(f32[2]{0:T(128)S(1)} %copy-done.2, bf16[512,256]{1,0:T(8,128)(2,1)S(1)} %mix.1.anchor.mix_ref, bf16[4,128,256]{2,1,0:T(8,128)(2,1)S(1)} %virt.1.virt_ref, ...), custom_call_target="tpu_custom_call" | custom-call | tf_op jit(solution)/shard_map/late/pallas_call | solution.py:756
  27.6 1.8 %collective-permute-start.10 = (bf16[64,256]{1,0:T(8,128)(2,1)S(1)}, bf16[64,256]{1,0:T(8,128)(2,1)S(1)}, u32[]{:S(2)}, u32[]{:S(2)}) collective-permute-start(bf16[64,256]{1,0:T(8,128)(2,1)S(1)} %get-tuple-element.38), channel_id=1, source_target_pairs={{0,24},{8,16},{16,8},{24,0},{1,25},{9,17},{17,9},{25,1},{2,26},{10... | collective-permute-start | bytes 98312 | tf_op jit(solution)/shard_map/ppermute | solution.py:702
  29.4 0.6 %collective-permute-start.11 = (bf16[64,256]{1,0:T(8,128)(2,1)S(1)}, bf16[64,256]{1,0:T(8,128)(2,1)S(1)}, u32[]{:S(2)}, u32[]{:S(2)}) collective-permute-start(bf16[64,256]{1,0:T(8,128)(2,1)S(1)} %get-tuple-element.39), channel_id=1, source_target_pairs={{0,8},{8,0},{16,24},{24,16},{1,9},{9,1},{17,25},{25,17},{2,10},{10... | collective-permute-start | bytes 98312 | tf_op jit(solution)/shard_map/ppermute | solution.py:702
  30.0 1.1 %collective-permute-start.12 = (bf16[64,256]{1,0:T(8,128)(2,1)S(1)}, bf16[64,256]{1,0:T(8,128)(2,1)S(1)}, u32[]{:S(2)}, u32[]{:S(2)}) collective-permute-start(bf16[64,256]{1,0:T(8,128)(2,1)S(1)} %get-tuple-element.40), channel_id=1, source_target_pairs={{0,16},{8,24},{16,0},{24,8},{1,17},{9,25},{17,1},{25,9},{2,18},{10... | collective-permute-start | bytes 98312 | tf_op jit(solution)/shard_map/ppermute | solution.py:702
  31.1 1.3 %collective-permute-done.10 = bf16[64,256]{1,0:T(8,128)(2,1)S(1)} collective-permute-done((bf16[64,256]{1,0:T(8,128)(2,1)S(1)}, bf16[64,256]{1,0:T(8,128)(2,1)S(1)}, u32[]{:S(2)}, u32[]{:S(2)}) %collective-permute-start.10) | collective-permute-done | bytes 32800 | tf_op jit(solution)/shard_map/ppermute | solution.py:702
  32.5 0.9 %collective-permute-done.11 = bf16[64,256]{1,0:T(8,128)(2,1)S(1)} collective-permute-done((bf16[64,256]{1,0:T(8,128)(2,1)S(1)}, bf16[64,256]{1,0:T(8,128)(2,1)S(1)}, u32[]{:S(2)}, u32[]{:S(2)}) %collective-permute-start.11) | collective-permute-done | bytes 32800 | tf_op jit(solution)/shard_map/ppermute | solution.py:702
  33.3 0.6 %collective-permute-done.12 = bf16[64,256]{1,0:T(8,128)(2,1)S(1)} collective-permute-done((bf16[64,256]{1,0:T(8,128)(2,1)S(1)}, bf16[64,256]{1,0:T(8,128)(2,1)S(1)}, u32[]{:S(2)}, u32[]{:S(2)}) %collective-permute-start.12) | collective-permute-done | bytes 32800 | tf_op jit(solution)/shard_map/ppermute | solution.py:702
  33.9 0.6 %convert_add_fusion = f32[64,256]{1,0:T(8,128)} fusion(bf16[64,256]{1,0:T(8,128)(2,1)S(1)} %collective-permute-done.12, bf16[64,256]{1,0:T(8,128)(2,1)S(1)} %collective-permute-done.11, f32[64,256]{1,0:T(8,128)S(1)} %get-tuple-element.37, bf16[64,256]{1,0:T(8,128)(2,1)S(1)} %collective-permute-done.10), kind=kLoop, calls=%fused_computation | loop fusion | flops 98304 | bytes 229376 | tf_op jit(solution)/shard_map/add | solution.py:763
  (3 shorter events, 0.0 us)
Async XLA Ops:
  0.0 6.1 %copy-start.3 = (bf16[256,8,2,128]{3,2,1,0:T(2,128)(2,1)S(1)}, bf16[256,8,2,128]{3,2,1,0:T(2,128)(2,1)}, u32[]{:S(2)}) copy-start(bf16[256,8,2,128]{3,2,1,0:T(2,128)(2,1)} %param.6) | copy-start | bytes 3145732
  1.5 5.9 %collective-permute-start = (bf16[64,128]{1,0:T(8,128)(2,1)}, bf16[64,128]{1,0:T(8,128)(2,1)S(1)}, u32[]{:S(2)}, u32[]{:S(2)}) collective-permute-start(bf16[64,128]{1,0:T(8,128)(2,1)} %get-tuple-element.24), channel_id=1, source_target_pairs={{0,24},{8,16},{16,8},{24,0},{1,25},{9,17},{17,9},{25,1},{2,26},{10... | collective-permute-start | bytes 49160 | tf_op jit(solution)/shard_map/ppermute | solution.py:702
  5.5 3.9 %collective-permute-start.1 = (bf16[64,128]{1,0:T(8,128)(2,1)}, bf16[64,128]{1,0:T(8,128)(2,1)S(1)}, u32[]{:S(2)}, u32[]{:S(2)}) collective-permute-start(bf16[64,128]{1,0:T(8,128)(2,1)} %get-tuple-element.25), channel_id=1, source_target_pairs={{0,8},{8,0},{16,24},{24,16},{1,9},{9,1},{17,25},{25,17},{2,10},{10... | collective-permute-start | bytes 49160 | tf_op jit(solution)/shard_map/ppermute | solution.py:702
  6.0 3.9 %collective-permute-start.2 = (bf16[64,128]{1,0:T(8,128)(2,1)}, bf16[64,128]{1,0:T(8,128)(2,1)S(1)}, u32[]{:S(2)}, u32[]{:S(2)}) collective-permute-start(bf16[64,128]{1,0:T(8,128)(2,1)} %get-tuple-element.26), channel_id=1, source_target_pairs={{0,16},{8,24},{16,0},{24,8},{1,17},{9,25},{17,1},{25,9},{2,18},{10... | collective-permute-start | bytes 49160 | tf_op jit(solution)/shard_map/ppermute | solution.py:702
  6.1 3.8 %copy-start = (bf16[64,128]{1,0:T(8,128)(2,1)S(1)}, bf16[64,128]{1,0:T(8,128)(2,1)}, u32[]{:S(2)}) copy-start(bf16[64,128]{1,0:T(8,128)(2,1)} %get-tuple-element.23.refs_2_.refs_0_) | copy-start | bytes 49156
  9.9 5.3 %copy-start.1 = (s32[2,4,4]{2,1,0:T(4,128)S(1)}, s32[2,4,4]{2,1,0:T(4,128)}, u32[]{:S(2)}) copy-start(s32[2,4,4]{2,1,0:T(4,128)} %live_ref.1) | copy-start | bytes 388
  10.6 11.0 %collective-permute-start.6 = (bf16[1536,128]{1,0:T(8,128)(2,1)S(1)}, bf16[1536,128]{1,0:T(8,128)(2,1)S(1)}, u32[]{:S(2)}, u32[]{:S(2)}) collective-permute-start(bf16[1536,128]{1,0:T(8,128)(2,1)S(1)} %get-tuple-element.31), channel_id=1, source_target_pairs={{0,8},{8,0},{16,24},{24,16},{1,9},{9,1},{17,25},{25,17},{2,10},{10... | collective-permute-start | bytes 1179656 | tf_op jit(solution)/shard_map/ppermute | solution.py:702
  12.2 10.3 %collective-permute-start.7 = (bf16[1536,128]{1,0:T(8,128)(2,1)S(1)}, bf16[1536,128]{1,0:T(8,128)(2,1)S(1)}, u32[]{:S(2)}, u32[]{:S(2)}) collective-permute-start(bf16[1536,128]{1,0:T(8,128)(2,1)S(1)} %get-tuple-element.32), channel_id=1, source_target_pairs={{0,16},{8,24},{16,0},{24,8},{1,17},{9,25},{17,1},{25,9},{2,18},{10... | collective-permute-start | bytes 1179656 | tf_op jit(solution)/shard_map/ppermute | solution.py:702
  12.7 4.7 %collective-permute-start.3 = (bf16[96,128]{1,0:T(8,128)(2,1)S(1)}, bf16[96,128]{1,0:T(8,128)(2,1)S(1)}, u32[]{:S(2)}, u32[]{:S(2)}) collective-permute-start(bf16[96,128]{1,0:T(8,128)(2,1)S(1)} %get-tuple-element.30.one_ref), channel_id=1, source_target_pairs={{0,4},{1,5},{2,6},{3,7},{4,0},{5,1},{6,2},{7,3},{8,12},{9,13},{10,... | collective-permute-start | bytes 73736 | tf_op jit(solution)/shard_map/ppermute | solution.py:702
  17.4 4.1 %collective-permute-start.4 = (bf16[192,128]{1,0:T(8,128)(2,1)S(1)}, bf16[192,128]{1,0:T(8,128)(2,1)S(1)}, u32[]{:S(2)}, u32[]{:S(2)}) collective-permute-start(bf16[192,128]{1,0:T(8,128)(2,1)S(1)} %join.3.one_ref), channel_id=1, source_target_pairs={{0,2},{1,3},{2,0},{3,1},{4,6},{5,7},{6,4},{7,5},{8,10},{9,11},{10,... | collective-permute-start | bytes 147464 | tf_op jit(solution)/shard_map/ppermute | solution.py:702
  19.0 6.2 %collective-permute-start.8 = (bf16[512,128]{1,0:T(8,128)(2,1)S(1)}, bf16[512,128]{1,0:T(8,128)(2,1)S(1)}, u32[]{:S(2)}, u32[]{:S(2)}) collective-permute-start(bf16[512,128]{1,0:T(8,128)(2,1)S(1)} %get-tuple-element.33), channel_id=1, source_target_pairs={{0,8},{8,0},{16,24},{24,16},{1,9},{9,1},{17,25},{25,17},{2,10},{10... | collective-permute-start | bytes 393224 | tf_op jit(solution)/shard_map/ppermute | solution.py:702
  19.5 5.6 %collective-permute-start.9 = (bf16[512,128]{1,0:T(8,128)(2,1)S(1)}, bf16[512,128]{1,0:T(8,128)(2,1)S(1)}, u32[]{:S(2)}, u32[]{:S(2)}) collective-permute-start(bf16[512,128]{1,0:T(8,128)(2,1)S(1)} %get-tuple-element.34), channel_id=1, source_target_pairs={{0,16},{8,24},{16,0},{24,8},{1,17},{9,25},{17,1},{25,9},{2,18},{10... | collective-permute-start | bytes 393224 | tf_op jit(solution)/shard_map/ppermute | solution.py:702
  21.5 1.9 %collective-permute-start.5 = (bf16[384,128]{1,0:T(8,128)(2,1)S(1)}, bf16[384,128]{1,0:T(8,128)(2,1)S(1)}, u32[]{:S(2)}, u32[]{:S(2)}) collective-permute-start(bf16[384,128]{1,0:T(8,128)(2,1)S(1)} %join.4.one_ref), channel_id=1, source_target_pairs={{0,1},{1,0},{2,3},{3,2},{4,5},{5,4},{6,7},{7,6},{8,9},{9,8},{10,11... | collective-permute-start | bytes 294920 | tf_op jit(solution)/shard_map/ppermute | solution.py:702
  23.5 1.7 %copy-start.2 = (f32[2]{0:T(128)S(1)}, f32[2]{0:T(128)}, u32[]{:S(2)}) copy-start(f32[2]{0:T(128)} %tau_ref.1) | copy-start | bytes 28
  27.6 4.9 %collective-permute-start.10 = (bf16[64,256]{1,0:T(8,128)(2,1)S(1)}, bf16[64,256]{1,0:T(8,128)(2,1)S(1)}, u32[]{:S(2)}, u32[]{:S(2)}) collective-permute-start(bf16[64,256]{1,0:T(8,128)(2,1)S(1)} %get-tuple-element.38), channel_id=1, source_target_pairs={{0,24},{8,16},{16,8},{24,0},{1,25},{9,17},{17,9},{25,1},{2,26},{10... | collective-permute-start | bytes 98312 | tf_op jit(solution)/shard_map/ppermute | solution.py:702
  29.4 3.9 %collective-permute-start.11 = (bf16[64,256]{1,0:T(8,128)(2,1)S(1)}, bf16[64,256]{1,0:T(8,128)(2,1)S(1)}, u32[]{:S(2)}, u32[]{:S(2)}) collective-permute-start(bf16[64,256]{1,0:T(8,128)(2,1)S(1)} %get-tuple-element.39), channel_id=1, source_target_pairs={{0,8},{8,0},{16,24},{24,16},{1,9},{9,1},{17,25},{25,17},{2,10},{10... | collective-permute-start | bytes 98312 | tf_op jit(solution)/shard_map/ppermute | solution.py:702
  30.0 3.9 %collective-permute-start.12 = (bf16[64,256]{1,0:T(8,128)(2,1)S(1)}, bf16[64,256]{1,0:T(8,128)(2,1)S(1)}, u32[]{:S(2)}, u32[]{:S(2)}) collective-permute-start(bf16[64,256]{1,0:T(8,128)(2,1)S(1)} %get-tuple-element.40), channel_id=1, source_target_pairs={{0,16},{8,24},{16,0},{24,8},{1,17},{9,25},{17,1},{25,9},{2,18},{10... | collective-permute-start | bytes 98312 | tf_op jit(solution)/shard_map/ppermute | solution.py:702

commit v8 on v5

--- a/solution.py
+++ b/solution.py
@@ -364,7 +364,7 @@
 
 
 def by_distance(refs):
-    return [refs[partners(4).index(distance)] for distance in range(4)]
+    return [refs[[0, 3, 1, 2].index(distance)] for distance in range(4)]
 
 
 def at_group(group, values):
@@ -645,7 +645,7 @@
     chi = chi * scale
     me = lax.axis_index("orb")
     share_rows = outs[0].shape[0]
-    for distance, out in zip(partners(4), outs):
+    for distance, out in zip([0, 3, 2, 1], outs):
         picked = chi[0:share_rows]
         for owner in range(1, 4):
             picked = jnp.where(me ^ distance == owner, chi[owner * share_rows : (owner + 1) * share_rows], picked)
@@ -691,8 +691,8 @@
             pltpu.SMEM(col_blocks.shape, jnp.int32), dma((3 + orb_count,)),
         ], 60, hbm, 10**10,
     )(virt, occ, col_blocks)
-    came = {distance: xor(part, "orb", distance) for distance, part in zip(partners(orb_count)[1:], sent[1:])}
-    messages = [sent[0]] + [came[distance] for distance in partners(orb_count)[1:]]
+    came = {distance: xor(part, "orb", distance) for distance, part in zip([3, 1, 2], sent[1:])}
+    messages = [sent[0]] + [came[distance] for distance in [3, 1, 2]]
     block = half(aux_dev * rows_dev, tile)
     owns = call(functools.partial(own_kernel, rows_dev, steps), "own", [block] * 2, [vmem], [], 6, vmem, 10**10)(flat)
     early = steps * 12 // 16
@@ -733,7 +733,7 @@
         [pltpu.VMEM(((steps - early) * PAIR, wide), BF16), pltpu.VMEM(((steps - early) * PAIR, wide), BF16)], 16,
     )(tau_weight, mix, virt, *owns, *got[1], occ_early, vir_early)
     total = shares[0]
-    for distance, share in zip(partners(orb_count)[1:], shares[1:]):
+    for distance, share in zip([3, 2, 1], shares[1:]):
         total = total + xor(share, "orb", distance)
     return total
 

time: 35.1 us -> 35.1 us (level)
  no operation moved by 1% of the time
where the time goes in v8:
time: 35.1 us; the launch traced here: 34.9 us
  starting transfers between devices  16.5 us (47%)
  Pallas kernels  8.88 us (25%)
  waiting for transfers between devices  8.75 us (25%)
  other arithmetic  0.65 us (2%)
    ppermute x13, starting transfers between devices, xor(): lax.ppermute(value, axis, [(i, i ^ distance) for i in range(lax.axis_size...  16.5 us
    ppermute x13, waiting for transfers between devices, xor(): lax.ppermute(value, axis, [(i, i ^ distance) for i in range(lax.axis_size...  8.75 us
    pallas_call x1, Pallas kernels, on_device_square(): call(functools.partial(late_kernel, rows_dev, tau_count, early, steps - e...  2.48 us
    pallas_call x1, Pallas kernels, on_device_square(): call(functools.partial(message_kernel, message), 'message', [half(message...  1.49 us
    pallas_call x1, Pallas kernels, on_device_square(): call(functools.partial(mix_kernel, sizes, message), 'mix', [half(tau_coun...  1.01 us
    pallas_call x1, Pallas kernels, on_device_square(): call(functools.partial(early_occ_kernel, rows_dev, tau_count, early), 'oc...  0.98 us
    pallas_call x1, Pallas kernels, on_device_square(): call(functools.partial(early_vir_kernel, rows_dev, tau_count, early), 'vi...  0.97 us
  transfers between devices with their start and end apart: 13, of which 9 were waited for; matrix products, arithmetic and copies ran while one was open for 0% of the time, Pallas kernels for 12%

profile of v8, /device:TPU:0, one launch (start us, length us, event | category | flops | bytes accessed | tf_op | source)
XLA Modules:
  0.0 34.9 jit_solution(8090756682541222745)
XLA Ops:
  0.0 0.0 copy-start.3
  0.0 1.5 %message.1 = (bf16[64,128]{1,0:T(8,128)(2,1)}, bf16[64,128]{1,0:T(8,128)(2,1)}, bf16[64,128]{1,0:T(8,128)(2,1)}, bf16[64,128]{1,0:T(8,128)(2,1)}) custom-call(bf16[32,128]{1,0:T(8,128)(2,1)} %bitcast.4, bf16[16,32]{1,0:T(8,128)(2,1)} %bitcast.5, s32[1,2]{1,0:T(1,128)} %col_hbm.1), custom_call_target="tpu_custom_call" | custom-call | flops 10000000000 | tf_op jit(solution)/shard_map/message/pallas_call | solution.py:687
  1.5 4.0 %collective-permute-start = (bf16[64,128]{1,0:T(8,128)(2,1)}, bf16[64,128]{1,0:T(8,128)(2,1)S(1)}, u32[]{:S(2)}, u32[]{:S(2)}) collective-permute-start(bf16[64,128]{1,0:T(8,128)(2,1)} %get-tuple-element.22), channel_id=1, source_target_pairs={{0,24},{8,16},{16,8},{24,0},{1,25},{9,17},{17,9},{25,1},{2,26},{10... | collective-permute-start | bytes 49160 | tf_op jit(solution)/shard_map/ppermute | solution.py:677
  5.5 0.5 %collective-permute-start.1 = (bf16[64,128]{1,0:T(8,128)(2,1)}, bf16[64,128]{1,0:T(8,128)(2,1)S(1)}, u32[]{:S(2)}, u32[]{:S(2)}) collective-permute-start(bf16[64,128]{1,0:T(8,128)(2,1)} %get-tuple-element.23), channel_id=1, source_target_pairs={{0,8},{8,0},{16,24},{24,16},{1,9},{9,1},{17,25},{25,17},{2,10},{10... | collective-permute-start | bytes 49160 | tf_op jit(solution)/shard_map/ppermute | solution.py:677
  6.0 0.1 collective-permute-start.2
  6.1 0.0 copy-done.3
  6.1 0.0 copy-start
  6.1 0.7 %own.1 = (bf16[2048,128]{1,0:T(8,128)(2,1)S(1)}, bf16[2048,128]{1,0:T(8,128)(2,1)S(1)}) custom-call(bf16[4096,128]{1,0:T(8,128)(2,1)S(1)} %bitcast.3), custom_call_target="tpu_custom_call" | custom-call | flops 10000000000 | tf_op jit(solution)/shard_map/own/pallas_call | solution.py:697
  6.8 0.6 %collective-permute-done.refs_3_.refs_1_ = bf16[64,128]{1,0:T(8,128)(2,1)S(1)} collective-permute-done((bf16[64,128]{1,0:T(8,128)(2,1)}, bf16[64,128]{1,0:T(8,128)(2,1)S(1)}, u32[]{:S(2)}, u32[]{:S(2)}) %collective-permute-start) | collective-permute-done | bytes 16416 | tf_op jit(solution)/shard_map/ppermute | solution.py:677
  7.4 2.0 %collective-permute-done.1.refs_4_.refs_2_ = bf16[64,128]{1,0:T(8,128)(2,1)S(1)} collective-permute-done((bf16[64,128]{1,0:T(8,128)(2,1)}, bf16[64,128]{1,0:T(8,128)(2,1)S(1)}, u32[]{:S(2)}, u32[]{:S(2)}) %collective-permute-start.1) | collective-permute-done | bytes 16416 | tf_op jit(solution)/shard_map/ppermute | solution.py:677
  9.4 0.5 %collective-permute-done.2.refs_5_.refs_3_ = bf16[64,128]{1,0:T(8,128)(2,1)S(1)} collective-permute-done((bf16[64,128]{1,0:T(8,128)(2,1)}, bf16[64,128]{1,0:T(8,128)(2,1)S(1)}, u32[]{:S(2)}, u32[]{:S(2)}) %collective-permute-start.2) | collective-permute-done | bytes 16416 | tf_op jit(solution)/shard_map/ppermute | solution.py:677
  9.9 0.0 copy-done
  9.9 0.0 copy-start.1
  9.9 0.7 %send.1 = (bf16[96,128]{1,0:T(8,128)(2,1)S(1)}, f32[8,128]{1,0:T(8,128)S(1)}, bf16[1536,128]{1,0:T(8,128)(2,1)S(1)}, bf16[1536,128]{1,0:T(8,128)(2,1)S(1)}, bf16...) custom-call(bf16[2048,128]{1,0:T(8,128)(2,1)S(1)} %get-tuple-element.25.refs_0_.own0, ...), custom_call_target="tpu_custom_call" | custom-call | flops 10000000000 | tf_op jit(solution)/shard_map/send/pallas_call | solution.py:700
  10.6 1.6 %collective-permute-start.6 = (bf16[1536,128]{1,0:T(8,128)(2,1)S(1)}, bf16[1536,128]{1,0:T(8,128)(2,1)S(1)}, u32[]{:S(2)}, u32[]{:S(2)}) collective-permute-start(bf16[1536,128]{1,0:T(8,128)(2,1)S(1)} %get-tuple-element.29), channel_id=1, source_target_pairs={{0,8},{8,0},{16,24},{24,16},{1,9},{9,1},{17,25},{25,17},{2,10},{10... | collective-permute-start | bytes 1179656 | tf_op jit(solution)/shard_map/ppermute | solution.py:677
  12.2 0.5 %collective-permute-start.7 = (bf16[1536,128]{1,0:T(8,128)(2,1)S(1)}, bf16[1536,128]{1,0:T(8,128)(2,1)S(1)}, u32[]{:S(2)}, u32[]{:S(2)}) collective-permute-start(bf16[1536,128]{1,0:T(8,128)(2,1)S(1)} %get-tuple-element.30), channel_id=1, source_target_pairs={{0,16},{8,24},{16,0},{24,8},{1,17},{9,25},{17,1},{25,9},{2,18},{10... | collective-permute-start | bytes 1179656 | tf_op jit(solution)/shard_map/ppermute | solution.py:677
  12.7 2.6 %collective-permute-start.3 = (bf16[96,128]{1,0:T(8,128)(2,1)S(1)}, bf16[96,128]{1,0:T(8,128)(2,1)S(1)}, u32[]{:S(2)}, u32[]{:S(2)}) collective-permute-start(bf16[96,128]{1,0:T(8,128)(2,1)S(1)} %get-tuple-element.28.one_ref), channel_id=1, source_target_pairs={{0,4},{1,5},{2,6},{3,7},{4,0},{5,1},{6,2},{7,3},{8,12},{9,13},{10,... | collective-permute-start | bytes 73736 | tf_op jit(solution)/shard_map/ppermute | solution.py:677
  15.3 0.0 copy-done.1
  15.3 1.0 %mix.1.anchor.mix_ref = bf16[512,256]{1,0:T(8,128)(2,1)S(1)} custom-call(s32[2,4,4]{2,1,0:T(4,128)S(1)} %copy-done.1, bf16[64,128]{1,0:T(8,128)(2,1)S(1)} %copy-done, bf16[64,128]{1,0:T(8,128)(2,1)S(1)} %collective-permute-done.refs_3_.refs_1_, bf16[64,128]{1,0:T(8,128)(2,1)S(1)} %collective-permute-done.1.refs_4_.refs_2_, ...), custom_call_target="tpu_custom_call" | custom-call | tf_op jit(solution)/shard_map/mix/pallas_call | solution.py:707
  16.3 1.1 %collective-permute-done.3.two_ref = bf16[96,128]{1,0:T(8,128)(2,1)S(1)} collective-permute-done((bf16[96,128]{1,0:T(8,128)(2,1)S(1)}, bf16[96,128]{1,0:T(8,128)(2,1)S(1)}, u32[]{:S(2)}, u32[]{:S(2)}) %collective-permute-start.3) | collective-permute-done | bytes 24608 | tf_op jit(solution)/shard_map/ppermute | solution.py:677
  17.4 1.6 %collective-permute-start.4 = (bf16[192,128]{1,0:T(8,128)(2,1)S(1)}, bf16[192,128]{1,0:T(8,128)(2,1)S(1)}, u32[]{:S(2)}, u32[]{:S(2)}) collective-permute-start(bf16[192,128]{1,0:T(8,128)(2,1)S(1)} %join.3.one_ref), channel_id=1, source_target_pairs={{0,2},{1,3},{2,0},{3,1},{4,6},{5,7},{6,4},{7,5},{8,10},{9,11},{10,... | collective-permute-start | bytes 147464 | tf_op jit(solution)/shard_map/ppermute | solution.py:677
  19.0 0.5 %collective-permute-start.8 = (bf16[512,128]{1,0:T(8,128)(2,1)S(1)}, bf16[512,128]{1,0:T(8,128)(2,1)S(1)}, u32[]{:S(2)}, u32[]{:S(2)}) collective-permute-start(bf16[512,128]{1,0:T(8,128)(2,1)S(1)} %get-tuple-element.31), channel_id=1, source_target_pairs={{0,8},{8,0},{16,24},{24,16},{1,9},{9,1},{17,25},{25,17},{2,10},{10... | collective-permute-start | bytes 393224 | tf_op jit(solution)/shard_map/ppermute | solution.py:677
  19.5 1.5 %collective-permute-start.9 = (bf16[512,128]{1,0:T(8,128)(2,1)S(1)}, bf16[512,128]{1,0:T(8,128)(2,1)S(1)}, u32[]{:S(2)}, u32[]{:S(2)}) collective-permute-start(bf16[512,128]{1,0:T(8,128)(2,1)S(1)} %get-tuple-element.32), channel_id=1, source_target_pairs={{0,16},{8,24},{16,0},{24,8},{1,17},{9,25},{17,1},{25,9},{2,18},{10... | collective-permute-start | bytes 393224 | tf_op jit(solution)/shard_map/ppermute | solution.py:677
  21.1 0.5 %collective-permute-done.4.two_ref = bf16[192,128]{1,0:T(8,128)(2,1)S(1)} collective-permute-done((bf16[192,128]{1,0:T(8,128)(2,1)S(1)}, bf16[192,128]{1,0:T(8,128)(2,1)S(1)}, u32[]{:S(2)}, u32[]{:S(2)}) %collective-permute-start.4) | collective-permute-done | bytes 49184 | tf_op jit(solution)/shard_map/ppermute | solution.py:677
  21.5 0.1 collective-permute-start.5
  21.6 0.0 collective-permute-done.6.from_x
  21.6 0.8 %collective-permute-done.7.from_y = bf16[1536,128]{1,0:T(8,128)(2,1)S(1)} collective-permute-done((bf16[1536,128]{1,0:T(8,128)(2,1)S(1)}, bf16[1536,128]{1,0:T(8,128)(2,1)S(1)}, u32[]{:S(2)}, u32[]{:S(2)}) %collective-permute-start.7) | collective-permute-done | bytes 393248 | tf_op jit(solution)/shard_map/ppermute | solution.py:677
  22.5 1.0 %occ.1.anchor.refs_4_ = bf16[192,8192]{1,0:T(8,128)(2,1)S(1)} custom-call(bf16[512,256]{1,0:T(8,128)(2,1)S(1)} %mix.1.anchor.mix_ref, bf16[2048,128]{1,0:T(8,128)(2,1)S(1)} %get-tuple-element.25.refs_0_.own0, bf16[2048,128]{1,0:T(8,128)(2,1)S(1)} %get-tuple-element.26.refs_1_.own1, bf16[1536,128]{1,0:T(8,128)(2,1)S(1)} %collective-permute-done.6.from_x, ...), custom_call_target="tpu_custom_call" | custom-call | tf_op jit(solution)/shard_map/occ/pallas_call | solution.py:713
  23.5 0.0 collective-permute-done.5.two_ref
  23.5 0.0 copy-start.2
  23.5 0.5 %virt.1.virt_ref = bf16[4,128,256]{2,1,0:T(8,128)(2,1)S(1)} custom-call(f32[8,128]{1,0:T(8,128)S(1)} %get-tuple-element.27.refs_4_.refs_0_, bf16[768,128]{1,0:T(8,128)(2,1)S(1)} %join.5.refs_1_), custom_call_target="tpu_custom_call" | custom-call | tf_op jit(solution)/shard_map/virt/pallas_call | solution.py:724
  24.1 1.0 %vir.1.refs_5_ = bf16[192,8192]{1,0:T(8,128)(2,1)S(1)} custom-call(bf16[4,128,256]{2,1,0:T(8,128)(2,1)S(1)} %virt.1.virt_ref, bf16[2048,128]{1,0:T(8,128)(2,1)S(1)} %get-tuple-element.25.refs_0_.own0, bf16[2048,128]{1,0:T(8,128)(2,1)S(1)} %get-tuple-element.26.refs_1_.own1, bf16[1536,128]{1,0:T(8,128)(2,1)S(1)} %collective-permute-done.6.from_x, ...), custom_call_target="tpu_custom_call" | custom-call | tf_op jit(solution)/shard_map/vir/pallas_call | solution.py:727
  25.0 0.0 collective-permute-done.8.refs_2_
  25.0 0.0 collective-permute-done.9.refs_3_
  25.1 0.0 copy-done.2
  25.1 2.5 %late.1 = (f32[64,256]{1,0:T(8,128)S(1)}, f32[64,256]{1,0:T(8,128)S(1)}, f32[64,256]{1,0:T(8,128)S(1)}, f32[64,256]{1,0:T(8,128)S(1)}) custom-call(f32[2]{0:T(128)S(1)} %copy-done.2, bf16[512,256]{1,0:T(8,128)(2,1)S(1)} %mix.1.anchor.mix_ref, bf16[4,128,256]{2,1,0:T(8,128)(2,1)S(1)} %virt.1.virt_ref, bf16[2048,128]{1,0:T(8,128)(2,1)S(1)} %get-tuple-element.25.refs_0_.own0, ...), custom_call_target="tpu_custom_call" | custom-call | tf_op jit(solution)/shard_map/late/pallas_call | solution.py:730
  27.5 2.0 %collective-permute-start.10 = (f32[64,256]{1,0:T(8,128)S(1)}, f32[64,256]{1,0:T(8,128)S(1)}, u32[]{:S(2)}, u32[]{:S(2)}) collective-permute-start(f32[64,256]{1,0:T(8,128)S(1)} %get-tuple-element.34), channel_id=1, source_target_pairs={{0,24},{8,16},{16,8},{24,0},{1,25},{9,17},{17,9},{25,1},{2,26},{10... | collective-permute-start | bytes 196616 | tf_op jit(solution)/shard_map/ppermute | solution.py:677
  29.5 0.5 %collective-permute-start.11 = (f32[64,256]{1,0:T(8,128)S(1)}, f32[64,256]{1,0:T(8,128)S(1)}, u32[]{:S(2)}, u32[]{:S(2)}) collective-permute-start(f32[64,256]{1,0:T(8,128)S(1)} %get-tuple-element.35), channel_id=1, source_target_pairs={{0,16},{8,24},{16,0},{24,8},{1,17},{9,25},{17,1},{25,9},{2,18},{10... | collective-permute-start | bytes 196616 | tf_op jit(solution)/shard_map/ppermute | solution.py:677
  30.0 1.1 %collective-permute-start.12 = (f32[64,256]{1,0:T(8,128)S(1)}, f32[64,256]{1,0:T(8,128)S(1)}, u32[]{:S(2)}, u32[]{:S(2)}) collective-permute-start(f32[64,256]{1,0:T(8,128)S(1)} %get-tuple-element.36), channel_id=1, source_target_pairs={{0,8},{8,0},{16,24},{24,16},{1,9},{9,1},{17,25},{25,17},{2,10},{10... | collective-permute-start | bytes 196616 | tf_op jit(solution)/shard_map/ppermute | solution.py:677
  31.1 2.2 %collective-permute-done.10 = f32[64,256]{1,0:T(8,128)S(1)} collective-permute-done((f32[64,256]{1,0:T(8,128)S(1)}, f32[64,256]{1,0:T(8,128)S(1)}, u32[]{:S(2)}, u32[]{:S(2)}) %collective-permute-start.10) | collective-permute-done | bytes 65568 | tf_op jit(solution)/shard_map/ppermute | solution.py:677
  33.3 0.6 %collective-permute-done.11 = f32[64,256]{1,0:T(8,128)S(1)} collective-permute-done((f32[64,256]{1,0:T(8,128)S(1)}, f32[64,256]{1,0:T(8,128)S(1)}, u32[]{:S(2)}, u32[]{:S(2)}) %collective-permute-start.11) | collective-permute-done | bytes 65568 | tf_op jit(solution)/shard_map/ppermute | solution.py:677
  33.9 0.4 %collective-permute-done.12 = f32[64,256]{1,0:T(8,128)S(1)} collective-permute-done((f32[64,256]{1,0:T(8,128)S(1)}, f32[64,256]{1,0:T(8,128)S(1)}, u32[]{:S(2)}, u32[]{:S(2)}) %collective-permute-start.12) | collective-permute-done | bytes 65568 | tf_op jit(solution)/shard_map/ppermute | solution.py:677
  34.3 0.6 %add_add_fusion = f32[64,256]{1,0:T(8,128)} fusion(f32[64,256]{1,0:T(8,128)S(1)} %collective-permute-done.12, f32[64,256]{1,0:T(8,128)S(1)} %collective-permute-done.11, f32[64,256]{1,0:T(8,128)S(1)} %get-tuple-element.33, f32[64,256]{1,0:T(8,128)S(1)} %collective-permute-done.10), kind=kLoop, calls=%fused_computation | loop fusion | flops 49152 | bytes 327680 | tf_op jit(solution)/shard_map/add | solution.py:737
  (3 shorter events, 0.0 us)
Async XLA Ops:
  0.0 6.1 %copy-start.3 = (bf16[256,8,2,128]{3,2,1,0:T(2,128)(2,1)S(1)}, bf16[256,8,2,128]{3,2,1,0:T(2,128)(2,1)}, u32[]{:S(2)}) copy-start(bf16[256,8,2,128]{3,2,1,0:T(2,128)(2,1)} %param.6) | copy-start | bytes 3145732
  1.5 5.9 %collective-permute-start = (bf16[64,128]{1,0:T(8,128)(2,1)}, bf16[64,128]{1,0:T(8,128)(2,1)S(1)}, u32[]{:S(2)}, u32[]{:S(2)}) collective-permute-start(bf16[64,128]{1,0:T(8,128)(2,1)} %get-tuple-element.22), channel_id=1, source_target_pairs={{0,24},{8,16},{16,8},{24,0},{1,25},{9,17},{17,9},{25,1},{2,26},{10... | collective-permute-start | bytes 49160 | tf_op jit(solution)/shard_map/ppermute | solution.py:677
  5.5 3.9 %collective-permute-start.1 = (bf16[64,128]{1,0:T(8,128)(2,1)}, bf16[64,128]{1,0:T(8,128)(2,1)S(1)}, u32[]{:S(2)}, u32[]{:S(2)}) collective-permute-start(bf16[64,128]{1,0:T(8,128)(2,1)} %get-tuple-element.23), channel_id=1, source_target_pairs={{0,8},{8,0},{16,24},{24,16},{1,9},{9,1},{17,25},{25,17},{2,10},{10... | collective-permute-start | bytes 49160 | tf_op jit(solution)/shard_map/ppermute | solution.py:677
  6.0 3.9 %collective-permute-start.2 = (bf16[64,128]{1,0:T(8,128)(2,1)}, bf16[64,128]{1,0:T(8,128)(2,1)S(1)}, u32[]{:S(2)}, u32[]{:S(2)}) collective-permute-start(bf16[64,128]{1,0:T(8,128)(2,1)} %get-tuple-element.24), channel_id=1, source_target_pairs={{0,16},{8,24},{16,0},{24,8},{1,17},{9,25},{17,1},{25,9},{2,18},{10... | collective-permute-start | bytes 49160 | tf_op jit(solution)/shard_map/ppermute | solution.py:677
  6.1 3.8 %copy-start = (bf16[64,128]{1,0:T(8,128)(2,1)S(1)}, bf16[64,128]{1,0:T(8,128)(2,1)}, u32[]{:S(2)}) copy-start(bf16[64,128]{1,0:T(8,128)(2,1)} %get-tuple-element.21.refs_2_.refs_0_) | copy-start | bytes 49156
  9.9 5.3 %copy-start.1 = (s32[2,4,4]{2,1,0:T(4,128)S(1)}, s32[2,4,4]{2,1,0:T(4,128)}, u32[]{:S(2)}) copy-start(s32[2,4,4]{2,1,0:T(4,128)} %live_ref.1) | copy-start | bytes 388
  10.6 11.0 %collective-permute-start.6 = (bf16[1536,128]{1,0:T(8,128)(2,1)S(1)}, bf16[1536,128]{1,0:T(8,128)(2,1)S(1)}, u32[]{:S(2)}, u32[]{:S(2)}) collective-permute-start(bf16[1536,128]{1,0:T(8,128)(2,1)S(1)} %get-tuple-element.29), channel_id=1, source_target_pairs={{0,8},{8,0},{16,24},{24,16},{1,9},{9,1},{17,25},{25,17},{2,10},{10... | collective-permute-start | bytes 1179656 | tf_op jit(solution)/shard_map/ppermute | solution.py:677
  12.2 10.3 %collective-permute-start.7 = (bf16[1536,128]{1,0:T(8,128)(2,1)S(1)}, bf16[1536,128]{1,0:T(8,128)(2,1)S(1)}, u32[]{:S(2)}, u32[]{:S(2)}) collective-permute-start(bf16[1536,128]{1,0:T(8,128)(2,1)S(1)} %get-tuple-element.30), channel_id=1, source_target_pairs={{0,16},{8,24},{16,0},{24,8},{1,17},{9,25},{17,1},{25,9},{2,18},{10... | collective-permute-start | bytes 1179656 | tf_op jit(solution)/shard_map/ppermute | solution.py:677
  12.7 4.7 %collective-permute-start.3 = (bf16[96,128]{1,0:T(8,128)(2,1)S(1)}, bf16[96,128]{1,0:T(8,128)(2,1)S(1)}, u32[]{:S(2)}, u32[]{:S(2)}) collective-permute-start(bf16[96,128]{1,0:T(8,128)(2,1)S(1)} %get-tuple-element.28.one_ref), channel_id=1, source_target_pairs={{0,4},{1,5},{2,6},{3,7},{4,0},{5,1},{6,2},{7,3},{8,12},{9,13},{10,... | collective-permute-start | bytes 73736 | tf_op jit(solution)/shard_map/ppermute | solution.py:677
  17.4 4.1 %collective-permute-start.4 = (bf16[192,128]{1,0:T(8,128)(2,1)S(1)}, bf16[192,128]{1,0:T(8,128)(2,1)S(1)}, u32[]{:S(2)}, u32[]{:S(2)}) collective-permute-start(bf16[192,128]{1,0:T(8,128)(2,1)S(1)} %join.3.one_ref), channel_id=1, source_target_pairs={{0,2},{1,3},{2,0},{3,1},{4,6},{5,7},{6,4},{7,5},{8,10},{9,11},{10,... | collective-permute-start | bytes 147464 | tf_op jit(solution)/shard_map/ppermute | solution.py:677
  19.0 6.0 %collective-permute-start.8 = (bf16[512,128]{1,0:T(8,128)(2,1)S(1)}, bf16[512,128]{1,0:T(8,128)(2,1)S(1)}, u32[]{:S(2)}, u32[]{:S(2)}) collective-permute-start(bf16[512,128]{1,0:T(8,128)(2,1)S(1)} %get-tuple-element.31), channel_id=1, source_target_pairs={{0,8},{8,0},{16,24},{24,16},{1,9},{9,1},{17,25},{25,17},{2,10},{10... | collective-permute-start | bytes 393224 | tf_op jit(solution)/shard_map/ppermute | solution.py:677
  19.5 5.5 %collective-permute-start.9 = (bf16[512,128]{1,0:T(8,128)(2,1)S(1)}, bf16[512,128]{1,0:T(8,128)(2,1)S(1)}, u32[]{:S(2)}, u32[]{:S(2)}) collective-permute-start(bf16[512,128]{1,0:T(8,128)(2,1)S(1)} %get-tuple-element.32), channel_id=1, source_target_pairs={{0,16},{8,24},{16,0},{24,8},{1,17},{9,25},{17,1},{25,9},{2,18},{10... | collective-permute-start | bytes 393224 | tf_op jit(solution)/shard_map/ppermute | solution.py:677
  21.5 1.9 %collective-permute-start.5 = (bf16[384,128]{1,0:T(8,128)(2,1)S(1)}, bf16[384,128]{1,0:T(8,128)(2,1)S(1)}, u32[]{:S(2)}, u32[]{:S(2)}) collective-permute-start(bf16[384,128]{1,0:T(8,128)(2,1)S(1)} %join.4.one_ref), channel_id=1, source_target_pairs={{0,1},{1,0},{2,3},{3,2},{4,5},{5,4},{6,7},{7,6},{8,9},{9,8},{10,11... | collective-permute-start | bytes 294920 | tf_op jit(solution)/shard_map/ppermute | solution.py:677
  23.5 1.6 %copy-start.2 = (f32[2]{0:T(128)S(1)}, f32[2]{0:T(128)}, u32[]{:S(2)}) copy-start(f32[2]{0:T(128)} %tau_ref.1) | copy-start | bytes 28
  27.5 5.8 %collective-permute-start.10 = (f32[64,256]{1,0:T(8,128)S(1)}, f32[64,256]{1,0:T(8,128)S(1)}, u32[]{:S(2)}, u32[]{:S(2)}) collective-permute-start(f32[64,256]{1,0:T(8,128)S(1)} %get-tuple-element.34), channel_id=1, source_target_pairs={{0,24},{8,16},{16,8},{24,0},{1,25},{9,17},{17,9},{25,1},{2,26},{10... | collective-permute-start | bytes 196616 | tf_op jit(solution)/shard_map/ppermute | solution.py:677
  29.5 4.4 %collective-permute-start.11 = (f32[64,256]{1,0:T(8,128)S(1)}, f32[64,256]{1,0:T(8,128)S(1)}, u32[]{:S(2)}, u32[]{:S(2)}) collective-permute-start(f32[64,256]{1,0:T(8,128)S(1)} %get-tuple-element.35), channel_id=1, source_target_pairs={{0,16},{8,24},{16,0},{24,8},{1,17},{9,25},{17,1},{25,9},{2,18},{10... | collective-permute-start | bytes 196616 | tf_op jit(solution)/shard_map/ppermute | solution.py:677
  30.0 4.3 %collective-permute-start.12 = (f32[64,256]{1,0:T(8,128)S(1)}, f32[64,256]{1,0:T(8,128)S(1)}, u32[]{:S(2)}, u32[]{:S(2)}) collective-permute-start(f32[64,256]{1,0:T(8,128)S(1)} %get-tuple-element.36), channel_id=1, source_target_pairs={{0,8},{8,0},{16,24},{24,16},{1,9},{9,1},{17,25},{25,17},{2,10},{10... | collective-permute-start | bytes 196616 | tf_op jit(solution)/shard_map/ppermute | solution.py:677
